TPU v7x, 256 devices: a whole 4x4x8 slice. The times are simulated.
256 devices in a mesh: frames: 64 (over x, z, core), mp: 4 (over y).
Axes of the slice: x: 4, y: 4, z: 8, core: 2. Of those that a mesh axis runs over, the one named last changes fastest.
Arguments:
- frames_in: bfloat16 [256, 16, 32, 768], P('frames'), may hold values from -6 to 6
- fine_gain: float32 [768], replicated, may hold values from 0.1 to 1.9
- fine_query_key_value: bfloat16 [768, 3, 768], P(None, None, 'mp'), may hold values from -64 to 64
- fine_out: bfloat16 [768, 768], P('mp'), may hold values from -1.25 to 1.25
- merge_weight: bfloat16 [768, 1536], replicated, may hold values from -0.875 to 0.875
- coarse_gain: float32 [1536], replicated, may hold values from 0.1 to 1.9
- coarse_query_key_value: bfloat16 [1536, 3, 1536], P(None, None, 'mp'), may hold values from -64 to 64
- coarse_out: bfloat16 [1536, 1536], P('mp'), may hold values from -12 to 12
- split_weight: bfloat16 [1536, 768], P(None, 'mp'), may hold values from -0.15625 to 0.15625
Outputs:
- frames_out: bfloat16 [256, 16, 32, 768], P('frames', None, None, 'mp')
All inputs are finite; a program needn't handle non-finite values.
Results may differ from a plain program's by a relative error of at most 0.04.
Values may be sent and summed in bfloat16 or wider, within the bound.
No kernel may reach another device: no remote copies, remote signals or barrier semaphores. Data moves between devices by JAX's collectives and lax.ppermute only.
A program may use at most 128 MiB of HBM per device.

v0:
```python
import jax
import jax.numpy as jnp
from jax import lax
from jax.sharding import PartitionSpec as P

HEADS = 12


epsilon = 1e-06
reach_space = 3


def padded(value, sides, width):
    for axis, dim in sides:
        peers, length = (lax.axis_size(axis), value.shape[dim])
        up = [(i, (i + 1) % peers) for i in range(peers - 1)]
        down = [(j, i) for i, j in up]
        last = lax.slice_in_dim(value, length - width, length, axis=dim)
        initial = lax.slice_in_dim(value, 0, width, axis=dim)
        before = lax.ppermute(last, axis, up)
        after = lax.ppermute(initial, axis, down)
        value = jnp.concatenate([before, value, after], axis=dim)
    return value


def rms_scale(value_rows, gain):
    value_rows = value_rows.astype(jnp.float32)
    square_mean = jnp.mean(value_rows * value_rows, axis=-1, keepdims=True)
    return value_rows * lax.rsqrt(square_mean + epsilon) * gain


def body(
    frames_in,
    fine_gain,
    fine_query_key_value,
    fine_out,
    merge_weight,
    coarse_gain,
    coarse_query_key_value,
    coarse_out,
    split_weight,
):
    frame_number, row_count, col_count, feature_count = frames_in.shape
    local_width = fine_query_key_value.shape[2]
    heads_here = HEADS // lax.axis_size("mp")
    head_width = local_width // heads_here
    normalized_input = rms_scale(frames_in, fine_gain).astype(jnp.bfloat16)
    projected = jnp.einsum(
        "igzq,qbj->igzbj",
        normalized_input,
        fine_query_key_value,
        preferred_element_type=jnp.float32,
    ).astype(jnp.bfloat16)
    rimmed = padded(projected[:, :, :, 1:], (("frames", 0),), 1)
    token_count = row_count * col_count
    query_index = jnp.arange(token_count, dtype=jnp.int32)
    query_row = query_index // col_count
    query_col = query_index % col_count
    key_index = jnp.arange(3 * token_count, dtype=jnp.int32)
    key_frame = key_index // token_count
    key_row = key_index // col_count % row_count
    key_col = key_index % col_count
    nearby = (jnp.abs(key_row[None, :] - query_row[:, None]) <= reach_space) & (
        jnp.abs(key_col[None, :] - query_col[:, None]) <= reach_space
    )
    first_frame = lax.axis_index("frames") * frame_number - 1
    total_frames = frame_number * lax.axis_size("frames")
    outputs = []
    for frame_at in range(frame_number):
        key_block = rimmed[frame_at : frame_at + 3].reshape(
            3 * token_count, 2, heads_here, head_width
        )
        source_frame = first_frame + frame_at + key_frame
        frame_inside = (source_frame >= 0) & (source_frame < total_frames)
        allowed = nearby & frame_inside[None, :]
        queries = projected[frame_at, :, :, 0].reshape(token_count, heads_here, head_width)
        scores = jnp.einsum(
            "qhe,khe->hqk", queries, key_block[:, 0], preferred_element_type=jnp.float32
        ) * head_width ** (-0.5)
        masked = jnp.where(allowed[None], scores, -jnp.inf)
        row_max = jnp.max(masked, axis=-1, keepdims=True)
        weights = jnp.where(allowed[None], jnp.exp(masked - row_max), 0.0)
        row_total = jnp.sum(weights, axis=-1)
        summed = jnp.einsum(
            "hqk,khe->qhe",
            weights.astype(jnp.bfloat16),
            key_block[:, 1],
            preferred_element_type=jnp.float32,
        )
        frame_result = summed / jnp.transpose(row_total)[..., None]
        outputs.append(frame_result.astype(jnp.bfloat16).reshape(row_count, col_count, local_width))
    attended = jnp.stack(outputs)
    partial_heads = jnp.einsum(
        "frce,ed->frcd", attended, fine_out, preferred_element_type=jnp.float32
    )
    mixed_heads = lax.psum(partial_heads.astype(jnp.bfloat16), "mp").astype(jnp.float32)
    hidden = (frames_in.astype(jnp.float32) + mixed_heads).astype(jnp.bfloat16)
    blocked = hidden.reshape(
        frame_number // 4, 4, row_count // 4, 4, col_count // 4, 4, feature_count
    )
    pooled = jnp.mean(blocked, axis=(1, 3, 5), dtype=jnp.float32).astype(jnp.bfloat16)
    coarse = jnp.dot(
        pooled.reshape(-1, feature_count), merge_weight, preferred_element_type=jnp.float32
    ).astype(jnp.bfloat16)
    merged_token_count = coarse.shape[0]
    coarse_local = coarse_query_key_value.shape[2]
    coarse_head = coarse_local // heads_here
    coarse_rms_output = rms_scale(coarse, coarse_gain).astype(jnp.bfloat16)
    coarse_proj = jnp.einsum(
        "vr,rbh->vbh", coarse_rms_output, coarse_query_key_value, preferred_element_type=jnp.float32
    ).astype(jnp.bfloat16)
    coarse_queries = coarse_proj[:, 0].reshape(merged_token_count, heads_here, coarse_head)
    coarse_pairs = coarse_proj[:, 1:].reshape(merged_token_count, 2, heads_here, coarse_head)
    shard_piece = lax.all_gather(coarse_pairs, "frames", axis=0, tiled=True)
    best = jnp.full((heads_here, merged_token_count), -1e30, jnp.float32)
    scores = jnp.einsum(
        "qhe,khe->hqk", coarse_queries, shard_piece[:, 0], preferred_element_type=jnp.float32
    ) * coarse_head ** (-0.5)
    new_best = jnp.maximum(best, jnp.max(scores, axis=-1))
    weights = jnp.exp(scores - new_best[..., None])
    denominator = jnp.sum(weights, axis=-1)
    update = jnp.einsum(
        "hqk,khe->hqe",
        weights.astype(jnp.bfloat16),
        shard_piece[:, 1],
        preferred_element_type=jnp.float32,
    )
    numerator = update
    best, denominator, numerator = (new_best, denominator, numerator)
    coarse_attended = (
        jnp.transpose(numerator / denominator[..., None], (1, 0, 2))
        .reshape(merged_token_count, coarse_local)
        .astype(jnp.bfloat16)
    )
    coarse_partial = jnp.dot(coarse_attended, coarse_out, preferred_element_type=jnp.float32)
    coarse_mixed = lax.psum(coarse_partial.astype(jnp.bfloat16), "mp").astype(jnp.float32)
    coarse_after = (coarse.astype(jnp.float32) + coarse_mixed).astype(jnp.bfloat16)
    split_rows = jnp.dot(coarse_after, split_weight, preferred_element_type=jnp.float32)
    split_grid = split_rows.reshape(
        frame_number // 4, 1, row_count // 4, 1, col_count // 4, 1, local_width
    )
    own_features = lax.dynamic_slice_in_dim(
        hidden, lax.axis_index("mp") * local_width, local_width, 3
    )
    result = (
        own_features.astype(jnp.float32).reshape(
            frame_number // 4, 4, row_count // 4, 4, col_count // 4, 4, local_width
        )
        + split_grid
    )
    return result.reshape(frame_number, row_count, col_count, local_width).astype(jnp.bfloat16)


def solution(mesh):
    in_specs = (
        P("frames", None, None, None),
        P(),
        P(None, None, "mp"),
        P("mp", None),
        P(),
        P(),
        P(None, None, "mp"),
        P("mp", None),
        P(None, "mp"),
    )
    out_specs = P("frames", None, None, "mp")
    return jax.shard_map(body, mesh=mesh, in_specs=in_specs, out_specs=out_specs, check_vma=False)
```

profile of v0, /device:TPU:6, one launch (start us, length us, event | category | flops | bytes accessed | tf_op | source)
XLA Modules:
  0.0 407.5 jit_solution(2713223858135619573)
XLA Ops:
  9.5 4.1 %fusion.38 = bf16[4,16,32,3,192]{4,2,3,1,0:T(8,128)(2,1)S(1)} fusion(bf16[4,16,32,768]{3,2,1,0:T(8,128)(2,1)S(1)} %copy-done.3, f32[768]{0:T(1024)S(1)} %copy-done.8, f32[4,16,32]{2,1,0:T(8,128)S(1)} %add_rsqrt_fusion, bf16[768,3,192]{0,2,1:T(8,128)(2,1)} %param.11), kind=kOutput, calls=%fused_computation.52 | convolution fusion | flops 1819410432 | bytes 6401024 | tf_op jit(solution)/shard_map/igzq,qbj->igzbj/dot_general | solution.py:48
  16.8 7.5 %collective-permute-start.1 = (bf16[1,16,32,2,192]{4,2,3,1,0:T(8,128)(2,1)}, bf16[1,16,32,2,192]{4,2,3,1,0:T(8,128)(2,1)}, u32[]{:S(2)}, u32[]{:S(2)}) collective-permute-start(bf16[1,16,32,2,192]{4,2,3,1,0:T(8,128)(2,1)} %get-tuple-element.12), channel_id=1, source_target_pairs={{4,0},{8,4},{12,8},{16,12},{20,16},{24,20},{28,24},{32,28},{36,32}... | collective-permute-start | bytes 1179656 | tf_op jit(solution)/shard_map/ppermute | solution.py:21
  30.6 5.2 %copy.95 = bf16[3,16,32,2,192]{2,1,0,4,3:T(8,128)(2,1)} copy(bf16[3,16,32,2,192]{4,2,3,1,0:T(8,128)(2,1)} %get-tuple-element.13) | data formatting | bytes 2359296 | tf_op jit(solution)/shard_map/reshape | solution.py:70
  35.8 7.3 %reshape.448 = bf16[1536,2,3,64]{0,3,2,1:T(8,128)(2,1)} reshape(bf16[3,16,32,2,192]{2,1,0,4,3:T(8,128)(2,1)} %copy.95) | data formatting | bytes 2359296 | tf_op jit(solution)/shard_map/reshape | solution.py:70
  45.1 5.2 %copy.97 = bf16[3,16,32,2,192]{2,1,0,4,3:T(8,128)(2,1)} copy(bf16[3,16,32,2,192]{4,2,3,1,0:T(8,128)(2,1)} %get-tuple-element.14) | data formatting | bytes 2359296 | tf_op jit(solution)/shard_map/reshape | solution.py:70
  50.3 7.3 %reshape.449 = bf16[1536,2,3,64]{0,3,2,1:T(8,128)(2,1)} reshape(bf16[3,16,32,2,192]{2,1,0,4,3:T(8,128)(2,1)} %copy.97) | data formatting | bytes 2359296 | tf_op jit(solution)/shard_map/reshape | solution.py:70
  57.6 5.0 %broadcast_and_fusion.3 = (pred[512,1536]{1,0:T(8,128)(4,1)}, pred[512,1536]{1,0:T(8,128)(4,1)}, pred[512,1536]{1,0:T(8,128)(4,1)}, pred[512,1536]{1,0:T(8,128)(4,1)}) fusion(pred[1536]{0:T(1024)(128)(4,1)} %get-tuple-element.38, s32[512]{0:T(512)} %get-tuple-element.39, s32[1536]{0:T(1024)S(1)} %get-tuple-element.33, s32[512]{0:T(512)} %get-tuple-element.40, ...), kind=kLoop, calls=%fused_computation.66 | loop fusion | flops 8650752 | bytes 3168256 | tf_op jit(solution)/shard_map/and | solution.py:75
  62.6 8.1 %fusion.191 = (f32[3,512]{1,0:T(4,128)S(1)}, bf16[3,512,1536]{2,1,0:T(8,128)(2,1)}) fusion(pred[512,1536]{1,0:T(8,128)(4,1)} %get-tuple-element.18, bf16[1536,2,3,64]{0,3,2,1:T(8,128)(2,1)} %reshape.448, bf16[512,3,64]{2,1,0:T(4,128)(2,1)} %reshape_squeeze.16), kind=kOutput, calls=%fused_computation.201 | convolution fusion | flops 316147200 | bytes 7411712 | tf_op jit(solution)/shard_map/sub | solution.py:82
  70.7 8.0 %fusion.186 = (f32[3,512]{1,0:T(4,128)S(1)}, bf16[3,512,1536]{2,1,0:T(8,128)(2,1)}) fusion(pred[512,1536]{1,0:T(8,128)(4,1)} %get-tuple-element.19, bf16[1536,2,3,64]{0,3,2,1:T(8,128)(2,1)} %reshape.449, bf16[512,3,64]{2,1,0:T(4,128)(2,1)} %reshape_squeeze.17), kind=kOutput, calls=%fused_computation.200 | convolution fusion | flops 316147200 | bytes 7411712 | tf_op jit(solution)/shard_map/sub | solution.py:82
  78.7 4.9 %fusion.70 = bf16[512,3,64]{0,2,1:T(8,128)(2,1)} fusion(bf16[3,512,1536]{2,1,0:T(8,128)(2,1)} %get-tuple-element.26, bf16[1536,2,3,64]{0,3,2,1:T(8,128)(2,1)} %reshape.448, f32[512,3]{0,1:T(4,128)S(1)} %bitcast.193), kind=kOutput, calls=%fused_computation.76 | convolution fusion | flops 302186496 | bytes 5511168 | tf_op jit(solution)/shard_map/hqk,khe->qhe/dot_general | solution.py:84
  93.5 4.7 %fusion.73 = bf16[512,3,64]{0,2,1:T(8,128)(2,1)} fusion(bf16[3,512,1536]{2,1,0:T(8,128)(2,1)} %get-tuple-element.24, bf16[1536,2,3,64]{0,3,2,1:T(8,128)(2,1)} %reshape.449, f32[512,3]{0,1:T(4,128)S(1)} %bitcast.192), kind=kOutput, calls=%fused_computation.77 | convolution fusion | flops 302186496 | bytes 5511168 | tf_op jit(solution)/shard_map/hqk,khe->qhe/dot_general | solution.py:84
  102.5 4.0 pad_maximum_fusion.1
  106.5 5.2 %copy.93 = bf16[3,16,32,2,192]{2,1,0,4,3:T(8,128)(2,1)} copy(bf16[3,16,32,2,192]{4,2,3,1,0:T(8,128)(2,1)} %get-tuple-element.15) | data formatting | bytes 2359296 | tf_op jit(solution)/shard_map/reshape | solution.py:70
  111.7 7.3 %reshape.447 = bf16[1536,2,3,64]{0,3,2,1:T(8,128)(2,1)} reshape(bf16[3,16,32,2,192]{2,1,0,4,3:T(8,128)(2,1)} %copy.93) | data formatting | bytes 2359296 | tf_op jit(solution)/shard_map/reshape | solution.py:70
  118.9 8.1 %fusion.196 = (f32[3,512]{1,0:T(4,128)S(1)}, bf16[3,512,1536]{2,1,0:T(8,128)(2,1)}) fusion(pred[512,1536]{1,0:T(8,128)(4,1)} %get-tuple-element.17, bf16[1536,2,3,64]{0,3,2,1:T(8,128)(2,1)} %reshape.447, bf16[512,3,64]{2,1,0:T(4,128)(2,1)} %reshape_squeeze.15), kind=kOutput, calls=%fused_computation.202 | convolution fusion | flops 316147200 | bytes 7411712 | tf_op jit(solution)/shard_map/sub | solution.py:82
  127.0 4.8 %fusion.67 = bf16[512,3,64]{0,2,1:T(8,128)(2,1)} fusion(bf16[3,512,1536]{2,1,0:T(8,128)(2,1)} %get-tuple-element.28, bf16[1536,2,3,64]{0,3,2,1:T(8,128)(2,1)} %reshape.447, f32[512,3]{0,1:T(4,128)S(1)} %bitcast.194), kind=kOutput, calls=%fused_computation.75 | convolution fusion | flops 302186496 | bytes 5511168 | tf_op jit(solution)/shard_map/hqk,khe->qhe/dot_general | solution.py:84
  135.9 5.2 %copy.99 = bf16[3,16,32,2,192]{2,1,0,4,3:T(8,128)(2,1)} copy(bf16[3,16,32,2,192]{4,2,3,1,0:T(8,128)(2,1)} %get-tuple-element.16) | data formatting | bytes 2359296 | tf_op jit(solution)/shard_map/reshape | solution.py:70
  141.0 7.5 %reshape.450 = bf16[1536,2,3,64]{0,3,2,1:T(8,128)(2,1)} reshape(bf16[3,16,32,2,192]{2,1,0,4,3:T(8,128)(2,1)} %copy.99) | data formatting | bytes 2359296 | tf_op jit(solution)/shard_map/reshape | solution.py:70
  148.5 8.0 %fusion.181 = (f32[3,512]{1,0:T(4,128)S(1)}, bf16[3,512,1536]{2,1,0:T(8,128)(2,1)}) fusion(pred[512,1536]{1,0:T(8,128)(4,1)} %get-tuple-element.20, bf16[1536,2,3,64]{0,3,2,1:T(8,128)(2,1)} %reshape.450, bf16[512,3,64]{2,1,0:T(4,128)(2,1)} %reshape_squeeze.18), kind=kOutput, calls=%fused_computation.199 | convolution fusion | flops 316147200 | bytes 7411712 | tf_op jit(solution)/shard_map/sub | solution.py:82
  156.5 4.7 %fusion.76 = bf16[512,3,64]{0,2,1:T(8,128)(2,1)} fusion(bf16[3,512,1536]{2,1,0:T(8,128)(2,1)} %get-tuple-element.22, bf16[1536,2,3,64]{0,3,2,1:T(8,128)(2,1)} %reshape.450, f32[512,3]{0,1:T(4,128)S(1)} %bitcast.195), kind=kOutput, calls=%fused_computation.78 | convolution fusion | flops 302186496 | bytes 5511168 | tf_op jit(solution)/shard_map/hqk,khe->qhe/dot_general | solution.py:84
  169.4 81.3 %all-reduce.3.cloned.1.call-done = bf16[4,16,32,768]{3,2,1,0:T(8,128)(2,1)} async-done(((bf16[4,16,32,768]{3,2,1,0:T(8,128)(2,1)}), bf16[4,16,32,768]{3,2,1,0:T(8,128)(2,1)}) %all-reduce.3.cloned.1.call-update) | async-done | bytes 3145744 | tf_op jit(solution)/shard_map/psum | solution.py:96
  250.7 6.9 %convert_reduce_fusion = (f32[16,32,768]{2,1,0:T(8,128)}, bf16[4,16,32,768]{3,2,1,0:T(8,128)(2,1)}) fusion(bf16[4,16,32,768]{3,2,1,0:T(8,128)(2,1)} %all-reduce.3.cloned.1.call-done, bf16[4,16,32,768]{3,2,1,0:T(8,128)(2,1)} %param.9), kind=kLoop, calls=%fused_computation.23 | loop fusion | flops 9043968 | bytes 11010048 | tf_op jit(solution)/shard_map/reduce_sum | solution.py:101
  270.6 71.8 %all-gather.2.cloned.1.call-done = bf16[2048,2,3,128]{3,0,2,1:T(8,128)(2,1)} async-done(((bf16[32,2,3,128]{3,0,2,1:T(8,128)(2,1)}), bf16[2048,2,3,128]{3,0,2,1:T(8,128)(2,1)}) %all-gather.2.cloned.1.call-update) | async-done | bytes 3145744 | tf_op jit(solution)/shard_map/all_gather | solution.py:114
  347.7 45.4 %all-reduce.5.cloned.1.call-done = bf16[32,1536]{1,0:T(8,128)(2,1)} async-done(((bf16[32,1536]{1,0:T(8,128)(2,1)}), bf16[32,1536]{1,0:T(8,128)(2,1)}) %all-reduce.5.cloned.1.call-update) | async-done | bytes 98320 | tf_op jit(solution)/shard_map/psum | solution.py:136
  (67 shorter events, 66.7 us)
Async XLA Ops:
  6.5 259.3 %copy-start = (bf16[1536,3,384]{2,0,1:T(8,128)(2,1)S(1)}, bf16[1536,3,384]{2,0,1:T(8,128)(2,1)}, u32[]{:S(2)}) copy-start(bf16[1536,3,384]{2,0,1:T(8,128)(2,1)} %param.15) | copy-start | bytes 10616836
  6.5 2.7 copy-start.8
  6.5 244.1 %all-reduce.3.cloned.1.call-start = ((), (), s32[]{:S(2)}) async-start(), calls=%async_computation | async-start | bytes 6291456 | tf_op jit(solution)/shard_map/psum | solution.py:96
  6.5 3.0 copy-start.3
  13.7 12.2 %copy-start.1 = (bf16[4,16,32,3,192]{4,2,3,1,0:T(8,128)(2,1)}, bf16[4,16,32,3,192]{4,2,3,1,0:T(8,128)(2,1)S(1)}, u32[]{:S(2)}) copy-start(bf16[4,16,32,3,192]{4,2,3,1,0:T(8,128)(2,1)S(1)} %fusion.38) | copy-start | bytes 7077892
  14.8 87.7 %collective-permute-start = (bf16[1,16,32,2,192]{4,2,3,1,0:T(8,128)(2,1)}, bf16[1,16,32,2,192]{4,2,3,1,0:T(8,128)(2,1)}, u32[]{:S(2)}, u32[]{:S(2)}) collective-permute-start(bf16[1,16,32,2,192]{4,2,3,1,0:T(8,128)(2,1)} %get-tuple-element.11), channel_id=1, source_target_pairs={{0,4},{4,8},{8,12},{12,16},{16,20},{20,24},{24,28},{28,32},{32,36}... | collective-permute-start | bytes 1179656 | tf_op jit(solution)/shard_map/ppermute | solution.py:20
  16.8 85.7 %collective-permute-start.1 = (bf16[1,16,32,2,192]{4,2,3,1,0:T(8,128)(2,1)}, bf16[1,16,32,2,192]{4,2,3,1,0:T(8,128)(2,1)}, u32[]{:S(2)}, u32[]{:S(2)}) collective-permute-start(bf16[1,16,32,2,192]{4,2,3,1,0:T(8,128)(2,1)} %get-tuple-element.12), channel_id=1, source_target_pairs={{4,0},{8,4},{12,8},{16,12},{20,16},{24,20},{28,24},{32,28},{36,32}... | collective-permute-start | bytes 1179656 | tf_op jit(solution)/shard_map/ppermute | solution.py:21
  78.7 4.9 %copy-start.2 = (bf16[4,16,32,3,192]{4,2,3,1,0:T(8,128)(2,1)S(1)}, bf16[4,16,32,3,192]{4,2,3,1,0:T(8,128)(2,1)}, u32[]{:S(2)}) copy-start(bf16[4,16,32,3,192]{4,2,3,1,0:T(8,128)(2,1)} %copy-done.1) | copy-start | bytes 7077892
  169.3 173.0 %all-gather.2.cloned.1.call-start = ((), (), s32[]{:S(2)}) async-start(), calls=%async_computation.1 | async-start | bytes 3194880 | tf_op jit(solution)/shard_map/all_gather | solution.py:114
  257.6 8.2 %copy-start.7 = (f32[1536]{0:T(1024)S(1)}, f32[1536]{0:T(1024)}, u32[]{:S(2)}) copy-start(f32[1536]{0:T(1024)} %param.14) | copy-start | bytes 18436
  265.1 0.7 copy-start.4
  266.6 0.6 copy-start.6
  267.8 125.3 %all-reduce.5.cloned.1.call-start = ((), (), s32[]{:S(2)}) async-start(), calls=%async_computation.2 | async-start | bytes 196608 | tf_op jit(solution)/shard_map/psum | solution.py:136
  342.4 4.4 %copy-start.5 = (bf16[384,1536]{1,0:T(8,128)(2,1)S(1)}, bf16[384,1536]{1,0:T(8,128)(2,1)}, u32[]{:S(2)}) copy-start(bf16[384,1536]{1,0:T(8,128)(2,1)} %param.16) | copy-start | bytes 3538948
Sparse Core Ops, SparseCore 0:
  169.4 81.1 all-reduce.2
  268.0 74.3 all-gather.1
  347.8 45.2 all-reduce.4
where the time goes:
time: 415 us; the launch traced here: 407 us
  waiting for transfers between devices  199 us (48%)
  local copies, waits for them, and re-layouts  91.2 us (22%)
  matrix products  69 us (17%)
  other arithmetic  25.8 us (6%)
  between operations  13.5 us (3%)
  starting transfers between devices  9.46 us (2%)
    psum x1, waiting for transfers between devices, body(): lax.psum(partial_heads.astype(jnp.bfloat16), 'mp').astype(jnp.float32)  81.3 us
    all_gather x1, waiting for transfers between devices, body(): shard_piece = lax.all_gather(coarse_pairs, 'frames', axis=0, tiled=True)  71.8 us
    reshape x8, local copies, waits for them, and re-layouts, body(): rimmed[frame_at:frame_at + 3]  50 us
    psum x1, waiting for transfers between devices, body(): lax.psum(coarse_partial.astype(jnp.bfloat16), 'mp').astype(jnp.float32)  45.4 us
    sub x4, matrix products, body(): weights = jnp.where(allowed[None], jnp.exp(masked - row_max), 0.0)  32.2 us
    dot_general x4, matrix products, body(): jnp.einsum('hqk,khe->qhe', weights.astype(jnp.bfloat16), key_block[:, 1],...  19.1 us
    reduce_sum x2, other arithmetic, body(): jnp.mean(blocked, axis=(1, 3, 5), dtype=jnp.float32).astype(jnp.bfloat16)  9.37 us
    another operation x4, local copies, waits for them, and re-layouts, body(): attended = jnp.stack(outputs)  8.6 us
  transfers between devices with their start and end apart: 5, of which 3 were waited for; matrix products, arithmetic and copies ran while one was open for 20% of the time, Pallas kernels for 0%

commit v1 on v0

v1 whole, which is shorter than its diff:
```python
import functools

import jax
import jax.numpy as jnp
import numpy as np
from jax import lax
from jax.experimental import pallas as pl
from jax.experimental.pallas import tpu as pltpu
from jax.sharding import PartitionSpec as P

HEADS = 12
EPSILON = 1e-06
REACH = 3
LOG2E = 1.4426950408889634
ROWS, COLS = 16, 32
TOKENS = ROWS * COLS
FRAMES = ("x", "z", "core")
MIB = 1 << 20
bf16, f32 = jnp.bfloat16, jnp.float32


def nt_dot(a, b):
    return lax.dot_general(a, b, (((1,), (1,)), ((), ())), preferred_element_type=f32)


def nn_dot(a, b):
    return jnp.dot(a, b, preferred_element_type=f32)


def block_mean_matrix():
    token = lax.broadcasted_iota(jnp.int32, (32, TOKENS), 1)
    block = lax.broadcasted_iota(jnp.int32, (32, TOKENS), 0)
    of_token = (token >> 7) * 8 + ((token & 31) >> 2)
    return jnp.where(of_token == block, 1.0 / 64, 0.0).astype(bf16)


def params(mib):
    return pltpu.CompilerParams(vmem_limit_bytes=mib * MIB)


def cost(flops, bytes_accessed, transcendentals=0):
    return pl.CostEstimate(
        flops=int(flops), bytes_accessed=int(bytes_accessed), transcendentals=int(transcendentals)
    )


def key_lanes(head):
    return 128 * head + (0 if head == 1 else 64)


def value_lanes(head):
    return 128 * head + (64 if head == 1 else 0)


def fine_project_kernel(
    x_ref, gain_ref, weight_ref,
    q_ref, key_ref, ones_ref, initial_ref, last_ref, mean_ref, rows_ref,
):
    step = pl.program_id(0)

    @pl.when(step == 0)
    def _():
        for head in range(3):
            k, v, own = key_lanes(head), value_lanes(head), slice(64 * head, 64 * head + 64)
            rows_ref[128 * head : 128 * head + 64, :] = weight_ref[0, own, :]
            rows_ref[128 * head + 64 : 128 * head + 128, :] = jnp.zeros((64, 768), bf16)
            rows_ref[384 + k : 448 + k, :] = weight_ref[1, own, :]
            rows_ref[384 + v : 448 + v, :] = weight_ref[2, own, :]
        mean_ref[...] = jnp.zeros_like(mean_ref)

    x = x_ref[0]
    wide = x.astype(f32)
    scale = lax.rsqrt(jnp.mean(wide * wide, axis=-1, keepdims=True) + EPSILON)
    normed = (wide * scale * gain_ref[...].reshape(1, 768)).astype(bf16)
    projected = nt_dot(normed, rows_ref[...])
    q_ref[0] = (projected[:, :384] * (0.125 * LOG2E)).astype(bf16)
    pairs = projected[:, 384:].astype(bf16)
    keep, fill = value_lane_masks()
    ones_ref[0] = pairs * keep.astype(bf16) + fill.astype(bf16)
    key_ref[0] = nt_dot(weight_ref[1], normed).astype(bf16)
    mean_ref[...] += nn_dot(block_mean_matrix(), x)

    @pl.when(step == 0)
    def _():
        initial_ref[...] = pairs

    @pl.when(step == 3)
    def _():
        last_ref[...] = pairs


def value_lane_masks():
    lane = lax.broadcasted_iota(jnp.int32, (1, 384), 1) >> 6
    is_value = (lane == 0) | (lane == 3) | (lane == 4)
    return jnp.where(is_value, 1.0, 0.0), jnp.where(is_value, 0.0, 1.0)


def in_hbm(*arrays):
    return [pltpu.with_memory_space_constraint(array, pltpu.HBM) for array in arrays]


def fine_project(x, gain, weight):
    x, weight = in_hbm(x, weight)
    return pl.pallas_call(
        fine_project_kernel,
        grid=(4,),
        in_specs=[
            pl.BlockSpec((1, TOKENS, 768), lambda i: (i, 0, 0)),
            pl.BlockSpec((768,), lambda i: (0,)),
            pl.BlockSpec((3, 192, 768), lambda i: (0, 0, 0)),
        ],
        out_specs=[
            pl.BlockSpec((1, TOKENS, 384), lambda i: (i, 0, 0)),
            pl.BlockSpec((1, 192, TOKENS), lambda i: (i, 0, 0)),
            pl.BlockSpec((1, TOKENS, 384), lambda i: (i, 0, 0)),
            whole(TOKENS, 384),
            whole(TOKENS, 384),
            whole(32, 768),
        ],
        out_shape=[
            pltpu.HBM((4, TOKENS, 384), bf16),
            jax.ShapeDtypeStruct((4, 192, TOKENS), bf16),
            jax.ShapeDtypeStruct((4, TOKENS, 384), bf16),
            pltpu.HBM((TOKENS, 384), bf16),
            pltpu.HBM((TOKENS, 384), bf16),
            jax.ShapeDtypeStruct((32, 768), f32),
        ],
        scratch_shapes=[pltpu.VMEM((768, 768), bf16)],
        compiler_params=params(20),
        cost_estimate=cost(2 * 2048 * 768 * 960, 8e6),
        name="fine_project",
    )(x, gain, weight)


BASES = (0, 0, 128, 128)
WINDOWS = ((0, 256), (0, 384), (128, 512), (256, 512))


def near_keys(tile, base):
    query = lax.broadcasted_iota(jnp.int32, (128, 384), 0) + 128 * tile
    key = lax.broadcasted_iota(jnp.int32, (128, 384), 1) + base
    rows = jnp.abs((query >> 5) - (key >> 5))
    cols = jnp.abs((query & 31) - (key & 31))
    return (rows <= REACH) & (cols <= REACH)


def near_masks():
    query = np.arange(512).reshape(4, 128, 1)
    key = np.arange(384).reshape(1, 1, 384) + np.array(BASES).reshape(4, 1, 1)
    rows = np.abs(query // COLS - key // COLS)
    cols = np.abs(query % COLS - key % COLS)
    return jnp.asarray((rows <= REACH) & (cols <= REACH), bf16)


def outside_range(total, least):
    low = lax.broadcasted_iota(jnp.int32, (128, 128), 1) < 64
    bad = jnp.where((total < 2.0**60) & (least > 2.0**-60), 0.0, 1.0)
    return jnp.max(jnp.where(low, bad, 0.0)) > 0.0


def rows_at(part, tile):
    start = part * TOKENS + tile * 128
    return pl.ds(start if isinstance(start, int) else pl.multiple_of(start, 128), 128)


def put_rows(out_ref, tile, pair):
    low = lax.broadcasted_iota(jnp.int32, (128, 128), 1) < 64
    thirds, counts = [], []
    for at, sums in enumerate(pair):
        turned = [pltpu.roll(one, 64, axis=1) for one in sums]
        heads = [one / other for one, other in zip(sums, turned)]
        out_ref[0, rows_at(at, tile), :] = jnp.where(
            low, heads[0], heads[1]
        ).astype(bf16)
        thirds.append(heads[2])
        counts += [turned[0], sums[1], turned[2]]
    packed = jnp.where(low, thirds[0], pltpu.roll(thirds[1], 64, axis=1))
    out_ref[0, rows_at(2, tile), :] = packed.astype(bf16)
    return sum(counts), functools.reduce(jnp.minimum, counts)


def attend_again(q_ref, frames, out_ref):
    def redo(tile, _):
        base = pl.multiple_of((tile >> 1) * 128, 128)
        window, own = pl.ds(base, 384), pl.ds(pl.multiple_of(tile * 128, 128), 128)
        near = near_keys(tile, base)
        pair = []
        for frame, sources in frames:
            sums = []
            for head in range(3):
                query = q_ref[frame, own, 128 * head : 128 * head + 64]
                scores = []
                for keys, _, inside in sources:
                    seen = near if inside is None else near & (inside > 0.0)
                    scored = nn_dot(query, keys[64 * head : 64 * head + 64, window])
                    scores.append(jnp.where(seen, scored, -jnp.inf))
                top = jnp.max(
                    jnp.maximum(jnp.maximum(scores[0], scores[1]), scores[2]),
                    axis=-1,
                    keepdims=True,
                )
                sums.append(
                    sum(
                        nn_dot(
                            jnp.exp2(score - top).astype(bf16),
                            ones[window, 128 * head : 128 * head + 128],
                        )
                        for score, (_, ones, _) in zip(scores, sources)
                    )
                )
            pair.append(sums)
        put_rows(out_ref, tile, pair)
        return 0

    lax.fori_loop(0, 4, redo, 0)


def weigh(query, keys, ones, mask):
    n = query.shape[0]
    weights = jnp.exp2(nn_dot(query.reshape(n * 128, 64), keys)).astype(bf16)
    weights = (weights.reshape(n, *mask.shape) * mask[None]).reshape(n * 128, mask.shape[1])
    return nn_dot(weights, ones).reshape(n, 128, 128)


def tiles():
    for tile in range(4):
        first, last = WINDOWS[tile]
        own = slice(128 * tile, 128 * tile + 128)
        yield tile, own, slice(first, last), slice(first - BASES[tile], last - BASES[tile])


def head_slices(head):
    return (
        slice(128 * head, 128 * head + 64),
        slice(64 * head, 64 * head + 64),
        slice(128 * head, 128 * head + 128),
    )


def block_means(out_ref):
    matrix = block_mean_matrix()
    pairs = nn_dot(matrix, out_ref[0, :TOKENS, :])
    pairs += nn_dot(matrix, out_ref[0, TOKENS : 2 * TOKENS, :])
    return pairs, nn_dot(matrix, out_ref[0, 2 * TOKENS :, :])


def inner_kernel(mask_ref, q_ref, k_ref, v_ref, out_ref, mean_ref, part_ref):
    total, least = jnp.zeros((128, 128), f32), jnp.ones((128, 128), f32)
    for tile, own, window, seen in tiles():
        pair = [[], []]
        for head in range(3):
            q_lanes, k_rows, lanes = head_slices(head)
            sums = [None] * 4
            for g in range(4):
                lo, hi = max(g - 1, 0), min(g + 1, 3)
                parts = weigh(
                    q_ref[lo : hi + 1, own, q_lanes],
                    k_ref[g, k_rows, window],
                    v_ref[g, window, lanes],
                    mask_ref[tile, :, seen],
                )
                for f in range(lo, hi + 1):
                    sums[f] = parts[f - lo] if sums[f] is None else sums[f] + parts[f - lo]
            part_ref[0, own, lanes] = sums[0]
            part_ref[1, own, lanes] = sums[3]
            pair[0].append(sums[1])
            pair[1].append(sums[2])
        tile_total, tile_least = put_rows(out_ref, tile, pair)
        total, least = total + tile_total, jnp.minimum(least, tile_least)

    @pl.when(outside_range(total, least))
    def _():
        own_frames = [(k_ref.at[g], v_ref.at[g], None) for g in range(4)]
        attend_again(q_ref, [(1, own_frames[:3]), (2, own_frames[1:])], out_ref)

    mean_ref[:, :128], mean_ref[:, 128:] = block_means(out_ref)


def outer_kernel(
    edge_ref, mask_ref, q_ref, k_ref, v_ref, part_ref, first_ref, last_ref, inner_mean_ref,
    weight_ref, inner_ref, out_ref, partial_ref, halo_key_ref, halo_ones_ref,
):
    keep, fill = value_lane_masks()
    for at, halo_ref in enumerate((first_ref, last_ref)):
        halo, inside = halo_ref[...].astype(f32), edge_ref[at]
        halo_ones_ref[at] = (halo * (keep * inside) + fill * inside).astype(bf16)
        turned = jnp.transpose(halo).astype(bf16)
        for head in range(3):
            start = key_lanes(head)
            halo_key_ref[at, 64 * head : 64 * head + 64, :] = turned[start : start + 64]

    total, least = jnp.zeros((128, 128), f32), jnp.ones((128, 128), f32)
    for tile, own, window, seen in tiles():
        pair = [[], []]
        for head in range(3):
            q_lanes, k_rows, lanes = head_slices(head)
            for at, frame in enumerate((0, 3)):
                more = weigh(
                    q_ref[frame : frame + 1, own, q_lanes],
                    halo_key_ref[at, k_rows, window],
                    halo_ones_ref[at, window, lanes],
                    mask_ref[tile, :, seen],
                )
                pair[at].append(part_ref[at, own, lanes] + more[0])
        tile_total, tile_least = put_rows(out_ref, tile, pair)
        total, least = total + tile_total, jnp.minimum(least, tile_least)

    @pl.when(outside_range(total, least))
    def _():
        own_frames = [(k_ref.at[g], v_ref.at[g], None) for g in range(4)]
        halos = [(halo_key_ref.at[at], halo_ones_ref.at[at], edge_ref[at]) for at in (0, 1)]
        attend_again(
            q_ref, [(0, own_frames[:2] + halos[:1]), (3, own_frames[2:] + halos[1:])], out_ref
        )

    here = block_means(out_ref)
    pairs = here[0] + inner_mean_ref[:, :128]
    third = here[1] + inner_mean_ref[:, 128:]
    third = third + pltpu.roll(third, 64, axis=1)
    partial = nn_dot(pairs.astype(bf16), weight_ref[:128, :])
    partial += nn_dot(third[:, :64].astype(bf16), weight_ref[128:, :])
    partial_ref[...] = partial.astype(bf16)


def whole(*shape):
    return pl.BlockSpec(shape, lambda *i: (0,) * len(shape))


def attend_inner(mask, q, k, v):
    return pl.pallas_call(
        inner_kernel,
        grid=(1,),
        in_specs=[pl.BlockSpec(memory_space=pltpu.VMEM)] * 4,
        out_specs=[
            pl.BlockSpec((1, 3 * TOKENS, 128), lambda i: (0, 0, 0)),
            whole(32, 256),
            whole(2, TOKENS, 384),
        ],
        out_shape=[
            pltpu.HBM((2, 3 * TOKENS, 128), bf16),
            jax.ShapeDtypeStruct((32, 256), f32),
            jax.ShapeDtypeStruct((2, TOKENS, 384), f32),
        ],
        compiler_params=params(24),
        cost_estimate=cost(10 * 2 * 512 * 320 * 3 * 256, 6e6, 10 * 512 * 320 * 3),
        name="attend_inner",
    )(mask, q, k, v)


def attend_outer(edge, mask, q, k, v, part, first, last, inner_mean, weight, inner):
    vmem = pl.BlockSpec(memory_space=pltpu.VMEM)
    return pl.pallas_call(
        outer_kernel,
        grid=(1,),
        in_specs=[pl.BlockSpec(memory_space=pltpu.SMEM)]
        + [vmem] * 9
        + [pl.BlockSpec(memory_space=pltpu.HBM)],
        out_specs=[pl.BlockSpec((1, 3 * TOKENS, 128), lambda i: (1, 0, 0)), whole(32, 768)],
        out_shape=[
            pltpu.HBM((2, 3 * TOKENS, 128), bf16),
            jax.ShapeDtypeStruct((32, 768), bf16),
        ],
        input_output_aliases={10: 0},
        scratch_shapes=[
            pltpu.VMEM((2, 192, TOKENS), bf16),
            pltpu.VMEM((2, TOKENS, 384), bf16),
        ],
        compiler_params=params(24),
        cost_estimate=cost(2 * 2 * 512 * 320 * 3 * 256, 6e6, 2 * 512 * 320 * 3),
        name="attend_outer",
    )(edge, mask, q, k, v, part, first, last, inner_mean, weight, inner)


def load_kernel(_, merge_ref, weight_ref, merge_out, weight_out, sems):
    copies = [
        pltpu.make_async_copy(merge_ref, merge_out, sems.at[0]),
        pltpu.make_async_copy(weight_ref, weight_out, sems.at[1]),
    ]
    for copy in copies:
        copy.start()
    for copy in copies:
        copy.wait()


def load_weights(after, merge, weight):
    anywhere = pl.BlockSpec(memory_space=pl.ANY)
    return pl.pallas_call(
        load_kernel,
        in_specs=[anywhere] * 3,
        out_specs=[anywhere] * 2,
        out_shape=[pltpu.VMEM(merge.shape, bf16), pltpu.VMEM(weight.shape, bf16)],
        scratch_shapes=[pltpu.SemaphoreType.DMA((2,))],
        compiler_params=params(4),
        cost_estimate=cost(0, 6e6),
        name="load_weights",
    )(after, *in_hbm(merge, weight))


def coarse_project_kernel(
    p0, p1, p2, p3, mean_ref, merge_ref, gain_ref, weight_ref, coarse_ref, q_ref, kv_ref
):
    pooled = mean_ref[...] + (
        (p0[...].astype(f32) + p1[...].astype(f32)) + (p2[...].astype(f32) + p3[...].astype(f32))
    )
    coarse = nn_dot(pooled.astype(bf16), merge_ref[...]).astype(bf16)
    coarse_ref[...] = coarse
    wide = coarse.astype(f32)
    scale = lax.rsqrt(jnp.mean(wide * wide, axis=-1, keepdims=True) + EPSILON)
    normed = (wide * scale * gain_ref[...].reshape(1, 1536)).astype(bf16)
    q_ref[...] = (nn_dot(normed, weight_ref[0]) * (128**-0.5 * LOG2E)).astype(bf16)
    key = nn_dot(normed, weight_ref[1]).astype(bf16)
    value = nn_dot(normed, weight_ref[2]).astype(bf16)
    for copy in range(8):
        kv_ref[copy, :, :384] = key
        kv_ref[copy, :, 384:] = value


def coarse_project(partials, mean, merge, gain, weight):
    return pl.pallas_call(
        coarse_project_kernel,
        in_specs=[pl.BlockSpec(memory_space=pltpu.VMEM)] * 8,
        out_specs=[whole(32, 1536), whole(32, 384), whole(8, 32, 768)],
        out_shape=[
            jax.ShapeDtypeStruct((32, 1536), bf16),
            jax.ShapeDtypeStruct((32, 384), bf16),
            pltpu.HBM((8, 32, 768), bf16),
        ],
        compiler_params=params(20),
        cost_estimate=cost(2 * 32 * 1536 * 1920, 7e6),
        name="coarse_project",
    )(*partials, mean, merge, gain, weight)


def coarse_attend_kernel(q0, q1, q2, q3, kv_ref, other_ref, o0, o1, o2, o3):
    query = jnp.concatenate([ref[...] for ref in (q0, q1, q2, q3)], axis=0)
    outs = (o0, o1, o2, o3)
    lane = lax.broadcasted_iota(jnp.int32, (128, 128), 1)
    stats = jnp.zeros((128, 128), f32)
    for head in range(3):
        lanes = slice(128 * head, 128 * head + 128)
        values = slice(384 + 128 * head, 512 + 128 * head)
        scores = [nt_dot(query[:, lanes], ref[:, lanes]) for ref in (kv_ref, other_ref)]
        top = jnp.max(jnp.maximum(scores[0], scores[1]), axis=-1, keepdims=True)
        weights = [jnp.exp2(score - top) for score in scores]
        total = jnp.sum(weights[0] + weights[1], axis=-1, keepdims=True)
        summed = nn_dot(weights[0].astype(bf16), kv_ref[:, values])
        summed += nn_dot(weights[1].astype(bf16), other_ref[:, values])
        summed = (summed / total).astype(bf16)
        rest = top + jnp.log(total) * LOG2E
        for part in range(3):
            piece = rest.astype(bf16).astype(f32)
            stats = jnp.where(lane == 3 * head + part, piece, stats)
            rest = rest - piece
        for i, out in enumerate(outs):
            out[:, lanes] = summed[32 * i : 32 * i + 32]
    for i, out in enumerate(outs):
        out[:, 384:] = stats[32 * i : 32 * i + 32].astype(bf16)


def coarse_attend(queries, kv, other):
    return pl.pallas_call(
        coarse_attend_kernel,
        out_shape=[jax.ShapeDtypeStruct((32, 512), bf16)] * 4,
        compiler_params=params(16),
        cost_estimate=cost(4 * 128 * 512 * 384, 1e6, 128 * 512 * 3),
        name="coarse_attend",
    )(*queries, kv, other)


def coarse_combine_kernel(p0, p1, p2, p3, weight_ref, out_ref):
    parts = (p0, p1, p2, p3)
    heads = []
    for head in range(3):
        lanes = slice(128 * head, 128 * head + 128)
        logs = [
            jnp.sum(part[:, 384 + 3 * head : 387 + 3 * head].astype(f32), axis=-1, keepdims=True)
            for part in parts
        ]
        top = functools.reduce(jnp.maximum, logs)
        shares = [jnp.exp2(log - top) for log in logs]
        summed = sum(share * part[:, lanes].astype(f32) for share, part in zip(shares, parts))
        heads.append((summed / sum(shares)).astype(bf16))
    attended = jnp.concatenate(heads, axis=-1)
    out_ref[...] = nn_dot(attended, weight_ref[...]).astype(bf16)


def coarse_combine(parts, weight):
    return pl.pallas_call(
        coarse_combine_kernel,
        out_shape=jax.ShapeDtypeStruct((32, 1536), bf16),
        compiler_params=params(16),
        cost_estimate=cost(2 * 32 * 384 * 1536, 2e6),
        name="coarse_combine",
    )(*parts, weight)


def own_features_kernel(place_ref, x_ref, weight_ref, x_out, pair_ref, low_ref, high_ref, pick_ref):
    step = pl.program_id(0)

    @pl.when(step == 0)
    def _():
        place = place_ref[0] * 192
        row = lax.broadcasted_iota(jnp.int32, (768, 192), 0)
        col = lax.broadcasted_iota(jnp.int32, (768, 192), 1)
        pick_ref[...] = jnp.where(row == col + place, 1.0, 0.0).astype(bf16)
        zeros = jnp.zeros((64, 192), bf16)
        for s in range(4):
            weight = nn_dot(weight_ref[s], pick_ref[...]).astype(bf16)
            pair_ref[128 * s : 128 * s + 128, :] = weight[:128]
            low_ref[128 * s : 128 * s + 64, :] = weight[128:]
            low_ref[128 * s + 64 : 128 * s + 128, :] = zeros
            high_ref[128 * s : 128 * s + 64, :] = zeros
            high_ref[128 * s + 64 : 128 * s + 128, :] = weight[128:]

    x_out[0] = nn_dot(x_ref[0], pick_ref[...]).astype(bf16)


def row_place(frame):
    return jnp.where(frame == 3, 3, (frame + 2) % 3)


def own_features(place, x, weight):
    x, weight = in_hbm(x, weight)
    return pl.pallas_call(
        own_features_kernel,
        grid=(4,),
        in_specs=[
            pl.BlockSpec(memory_space=pltpu.SMEM),
            pl.BlockSpec((1, TOKENS, 768), lambda i: (i, 0, 0)),
            whole(4, 192, 768),
        ],
        out_specs=[pl.BlockSpec((1, TOKENS, 192), lambda i: (row_place(i), 0, 0))]
        + [whole(512, 192)] * 3,
        out_shape=[jax.ShapeDtypeStruct((4, TOKENS, 192), bf16)]
        + [jax.ShapeDtypeStruct((512, 192), bf16)] * 3,
        scratch_shapes=[pltpu.VMEM((768, 192), bf16)],
        compiler_params=params(16),
        cost_estimate=cost(2 * 2048 * 192 * 768, 5e6),
        name="own_features",
    )(place, x, weight)


def hidden_kernel(x_ref, rows_ref, pair_ref, low_ref, high_ref, out_ref):
    parts = [
        jnp.concatenate([rows_ref[s, 0, TOKENS * i : TOKENS * (i + 1)] for s in range(4)], axis=1)
        for i in range(3)
    ]
    for at, third_ref in enumerate((low_ref, high_ref)):
        mixed = nn_dot(parts[at], pair_ref[...]) + nn_dot(parts[2], third_ref[...])
        out_ref[at] = (x_ref[at].astype(f32) + mixed).astype(bf16)


def hidden_rows(x, rows, pair, low, high):
    (rows,) = in_hbm(rows)
    return pl.pallas_call(
        hidden_kernel,
        grid=(2,),
        in_specs=[
            pl.BlockSpec((2, TOKENS, 192), lambda i: (i, 0, 0)),
            pl.BlockSpec((4, 1, 3 * TOKENS, 128), lambda i: (0, i, 0, 0)),
        ]
        + [whole(512, 192)] * 3,
        out_specs=pl.BlockSpec((2, TOKENS, 192), lambda i: (i, 0, 0)),
        out_shape=jax.ShapeDtypeStruct((4, TOKENS, 192), bf16),
        compiler_params=params(20),
        cost_estimate=cost(2 * 2048 * 192 * 1024, 5e6),
        name="hidden_rows",
    )(x, rows, pair, low, high)


def split_kernel(hidden_ref, coarse_ref, p0, p1, p2, p3, weight_ref, out_ref):
    mixed = (p0[...].astype(f32) + p1[...].astype(f32)) + (
        p2[...].astype(f32) + p3[...].astype(f32)
    )
    after = (coarse_ref[...].astype(f32) + mixed).astype(bf16)
    split = nt_dot(after, weight_ref[...])
    row = lax.broadcasted_iota(jnp.int32, (128, 32), 0)
    col = lax.broadcasted_iota(jnp.int32, (128, 32), 1)
    spread = jnp.where(col == (row >> 5) * 8 + ((row & 31) >> 2), 1.0, 0.0)
    grid = jnp.dot(spread, split, preferred_element_type=f32, precision=lax.Precision.HIGHEST)
    for at_frame, frame in enumerate((1, 2, 0, 3)):
        for block in range(4):
            rows = grid[32 * block : 32 * block + 32]
            for r in range(4):
                at = 4 * block + r
                here = hidden_ref[at_frame, at * COLS : (at + 1) * COLS, :].astype(f32)
                out_ref[frame, at] = (here + rows).astype(bf16)


def split_rows(hidden, coarse, partials, weight):
    return pl.pallas_call(
        split_kernel,
        out_shape=jax.ShapeDtypeStruct((4, ROWS, COLS, 192), bf16),
        compiler_params=params(20),
        cost_estimate=cost(2 * 32 * 1536 * 192, 4e6),
        name="split_rows",
    )(hidden, coarse, *partials, weight)


def shifted(value, axis, shift):
    return lax.ppermute(value, axis, [(i, (i + shift) % 4) for i in range(4)])


def from_others(value, axis):
    return [shifted(value, axis, shift) for shift in (1, 2, 3)]


def body(x, fine_gain, fine_qkv, fine_out, merge, coarse_gain, coarse_qkv, coarse_out, split):
    x = x.reshape(4, TOKENS, 768)
    groups = lax.axis_size(FRAMES)
    here = lax.axis_index(FRAMES)
    place = lax.axis_index("mp").astype(jnp.int32).reshape(1)
    edge = jnp.stack(
        [jnp.where(here == 0, 0.0, 1.0), jnp.where(here == groups - 1, 0.0, 1.0)]
    ).astype(f32)

    fine_outs = lax.all_gather(fine_out, "mp", axis=0)
    q, k, v, initial, final, frame_mean = fine_project(
        x, fine_gain, jnp.transpose(fine_qkv, (1, 2, 0))
    )
    first = lax.ppermute(final, FRAMES, [(i, i + 1) for i in range(groups - 1)])
    last = lax.ppermute(initial, FRAMES, [(i + 1, i) for i in range(groups - 1)])
    mask = near_masks()
    inner, inner_mean, part = attend_inner(mask, q, k, v)
    rows, partial = attend_outer(
        edge, mask, q, k, v, part, first, last, inner_mean, fine_out, inner
    )
    partials = [partial] + from_others(partial, "mp")
    merge, coarse_qkv = load_weights(partials[1], merge, jnp.transpose(coarse_qkv, (1, 0, 2)))
    rows = lax.all_gather(rows, "mp", axis=0)

    coarse, coarse_q, coarse_kv = coarse_project(
        partials, frame_mean, merge, coarse_gain, coarse_qkv
    )
    coarse_kv = lax.all_to_all(coarse_kv, "z", 0, 0, tiled=True).reshape(256, 768)
    queries = [coarse_q] + from_others(coarse_q, "x")
    own = own_features(place, x, fine_outs)
    coarse_kv, queries, own = lax.optimization_barrier((coarse_kv, queries, own))
    other_kv = lax.ppermute(coarse_kv, "core", [(0, 1), (1, 0)])
    parts = list(coarse_attend(queries, coarse_kv, other_kv))
    parts = parts[:1] + [shifted(parts[s], "x", 4 - s) for s in (1, 2, 3)]
    coarse_partial = coarse_combine(parts, coarse_out)
    coarse_partials = [coarse_partial] + from_others(coarse_partial, "mp")
    hidden = hidden_rows(own[0], rows, *own[1:])
    return split_rows(hidden, coarse, coarse_partials, jnp.transpose(split, (1, 0)))


def solution(mesh):
    parts = jax.sharding.Mesh(mesh.devices.reshape(4, 8, 2, 4), FRAMES + ("mp",))
    in_specs = (
        P(FRAMES, None, None, None),
        P(),
        P(None, None, "mp"),
        P("mp", None),
        P(),
        P(),
        P(None, None, "mp"),
        P("mp", None),
        P(None, "mp"),
    )
    out_specs = P(FRAMES, None, None, "mp")
    return jax.shard_map(body, mesh=parts, in_specs=in_specs, out_specs=out_specs, check_vma=False)
```

time: 415 us -> 120 us (0.29); the launches traced: 407 us -> 120 us
  waiting for transfers between devices: 199 us -> 13.6 us
  local copies, waits for them, and re-layouts: 91.2 us -> 2.76 us
  matrix products: 69 us -> 0 us
  Pallas kernels: 0 us -> 57.9 us
  other arithmetic: 25.8 us -> 0.08 us
  starting transfers between devices: 9.46 us -> 32.1 us
    psum x2 -> x0, waiting for transfers between devices: 127 us -> none  [the longest x1 81.3 us: body(): lax.psum(partial_heads.astype(jnp.bfloat16), 'mp').astype(jnp.float32)]
    all_gather x1 -> x2, waiting for transfers between devices: 71.8 us -> 0.01 us  [the longest x1 0.01 us: body(): fine_outs = lax.all_gather(fine_out, 'mp', axis=0)]
    pallas_call x0 -> x10, Pallas kernels: none -> 57.9 us  [the longest x1 18.8 us: attend_inner(): pl.pallas_call(inner_kernel, grid=(1,), in_specs=[pl.BlockSpec(memory_spa...]
    reshape x9 -> x0, local copies, waits for them, and re-layouts: 50.6 us -> none  [the longest x8 50 us: body(): rimmed[frame_at:frame_at + 3]]
    dot_general x12 -> x0, matrix products: 36.7 us -> none  [the longest x4 19.1 us: body(): jnp.einsum('hqk,khe->qhe', weights.astype(jnp.bfloat16), key_block[:, 1],...]
    sub x4 -> x0, matrix products: 32.2 us -> none  [body(): weights = jnp.where(allowed[None], jnp.exp(masked - row_max), 0.0)]
    another operation x9 -> x0, local copies, waits for them, and re-layouts: 18.3 us -> none  [the longest x4 8.6 us: body(): attended = jnp.stack(outputs)]
    ppermute x2 -> x15, starting transfers between devices: 9.38 us -> 26.1 us  [the longest x12 16.7 us: shifted(): return lax.ppermute(value, axis, [(i, (i + shift) % 4) for i in range(4)])]
  transfers between devices with their start and end apart: 5 -> 18, of which waited for: 3 -> 7; matrix products, arithmetic and copies ran while one was open for 20% -> 0% of each run, Pallas kernels for 0% -> 47%
where the time goes in v1:
time: 120 us
  Pallas kernels  57.9 us (48%)
  starting transfers between devices  32.1 us (27%)
  waiting for transfers between devices  13.6 us (11%)
  between operations  13.6 us (11%)
  local copies, waits for them, and re-layouts  2.76 us (2%)
    pallas_call x1, Pallas kernels, attend_inner(): pl.pallas_call(inner_kernel, grid=(1,), in_specs=[pl.BlockSpec(memory_spa...  18.8 us
    ppermute x12, starting transfers between devices, shifted(): return lax.ppermute(value, axis, [(i, (i + shift) % 4) for i in range(4)])  16.7 us
    pallas_call x1, Pallas kernels, attend_outer(): pl.pallas_call(outer_kernel, grid=(1,), in_specs=[pl.BlockSpec(memory_spa...  15.5 us
    pallas_call x1, Pallas kernels, fine_project(): pl.pallas_call(fine_project_kernel, grid=(4,), in_specs=[pl.BlockSpec((1,...  7.48 us
    ppermute x1, starting transfers between devices, body(): lax.ppermute(initial, FRAMES, [(i + 1, i) for i in range(groups - 1)])  7.47 us
    ppermute x12, waiting for transfers between devices, shifted(): return lax.ppermute(value, axis, [(i, (i + shift) % 4) for i in range(4)])  7.15 us
    all_to_all x1, starting transfers between devices, body(): lax.all_to_all(coarse_kv, 'z', 0, 0, tiled=True).reshape(256, 768)  5.91 us
    pallas_call x1, Pallas kernels, own_features(): pl.pallas_call(own_features_kernel, grid=(4,), in_specs=[pl.BlockSpec(mem...  4.54 us
  transfers between devices with their start and end apart: 18, of which 7 were waited for; matrix products, arithmetic and copies ran while one was open for 0% of the time, Pallas kernels for 47%

profile of v1, /device:TPU:6, one launch (start us, length us, event | category | flops | bytes accessed | tf_op | source)
XLA Modules:
  0.0 119.9 jit_solution(7368421546794895856)
XLA Ops:
  8.0 7.5 %fine_project.1 = (bf16[4,512,384]{2,1,0:T(8,128)(2,1)}, bf16[4,192,512]{2,1,0:T(8,128)(2,1)S(1)}, bf16[4,512,384]{2,1,0:T(8,128)(2,1)S(1)}, bf16[512,384]{1,0:T...) custom-call(bf16[4,512,768]{2,1,0:T(8,128)(2,1)} %bitcast.14, f32[768]{0:T(1024)S(1)} %copy-done.8, ...), custom_call_target="tpu_custom_call" | custom-call | flops 3019898880 | bytes 8000000 | tf_op jit(solution)/shard_map/fine_project/pallas_call | solution.py:104
  16.1 1.9 %collective-permute-start = (bf16[512,384]{1,0:T(8,128)(2,1)}, bf16[512,384]{1,0:T(8,128)(2,1)S(1)}, u32[]{:S(2)}, u32[]{:S(2)}) collective-permute-start(bf16[512,384]{1,0:T(8,128)(2,1)} %get-tuple-element.42), channel_id=1, source_target_pairs={{0,4},{4,8},{8,12},{12,16},{16,20},{20,24},{24,28},{28,32},{32,36}... | collective-permute-start | bytes 1179656 | tf_op jit(solution)/shard_map/ppermute | solution.py:621
  18.0 7.5 %collective-permute-start.1 = (bf16[512,384]{1,0:T(8,128)(2,1)}, bf16[512,384]{1,0:T(8,128)(2,1)}, u32[]{:S(2)}, u32[]{:S(2)}) collective-permute-start(bf16[512,384]{1,0:T(8,128)(2,1)} %get-tuple-element.43), channel_id=1, source_target_pairs={{4,0},{8,4},{12,8},{16,12},{20,16},{24,20},{28,24},{32,28},{36,32}... | collective-permute-start | bytes 1179656 | tf_op jit(solution)/shard_map/ppermute | solution.py:622
  25.6 1.4 %copy-done = bf16[4,512,384]{2,1,0:T(8,128)(2,1)S(1)} copy-done((bf16[4,512,384]{2,1,0:T(8,128)(2,1)S(1)}, bf16[4,512,384]{2,1,0:T(8,128)(2,1)}, u32[]{:S(2)}) %copy-start) | copy-done | bytes 1572888
  27.0 18.8 %attend_inner.1 = (bf16[2,1536,128]{2,1,0:T(8,128)(2,1)}, f32[32,256]{1,0:T(8,128)S(1)}, f32[2,512,384]{2,1,0:T(8,128)S(1)}) custom-call(bf16[4,128,384]{2,1,0:T(8,128)(2,1)S(1)} %copy-done.4, bf16[4,512,384]{2,1,0:T(8,128)(2,1)S(1)} %copy-done, bf16[4,192,512]{2,1,0:T(8,128)(2,1)S(1)} %get-tuple-element.39.k_ref, ...), custom_call_target="tpu_custom_call" | custom-call | flops 2516582400 | bytes 6000000 | tf_op jit(solution)/shard_map/attend_inner/pallas_call | solution.py:330
  45.8 15.5 %attend_outer.1 = (bf16[2,1536,128]{2,1,0:T(8,128)(2,1)}, bf16[32,768]{1,0:T(8,128)(2,1)S(1)}) custom-call(f32[2]{0:T(128)S(1)} %pad_maximum_fusion.edge_ref, bf16[4,128,384]{2,1,0:T(8,128)(2,1)S(1)} %copy-done.4, bf16[4,512,384]{2,1,0:T(8,128)(2,1)S(1)} %copy-done, ...), custom_call_target="tpu_custom_call", output_to_operand_aliasing={{0}: (10, {})} | custom-call | flops 503316480 | bytes 6000000 | tf_op jit(solution)/shard_map/attend_outer/pallas_call | solution.py:352
  61.3 1.7 %collective-permute-start.2 = (bf16[32,768]{1,0:T(8,128)(2,1)S(1)}, bf16[32,768]{1,0:T(8,128)(2,1)S(1)}, u32[]{:S(2)}, u32[]{:S(2)}) collective-permute-start(bf16[32,768]{1,0:T(8,128)(2,1)S(1)} %get-tuple-element.46.p0), channel_id=1, source_target_pairs={{0,1},{1,2},{2,3},{3,0},{4,5},{5,6},{6,7},{7,4},{8,9},{9,10},{10,1... | collective-permute-start | bytes 147464 | tf_op jit(solution)/shard_map/ppermute | solution.py:601
  62.9 2.9 %collective-permute-start.3 = (bf16[32,768]{1,0:T(8,128)(2,1)S(1)}, bf16[32,768]{1,0:T(8,128)(2,1)S(1)}, u32[]{:S(2)}, u32[]{:S(2)}) collective-permute-start(bf16[32,768]{1,0:T(8,128)(2,1)S(1)} %get-tuple-element.46.p0), channel_id=1, source_target_pairs={{0,2},{1,3},{2,0},{3,1},{4,6},{5,7},{6,4},{7,5},{8,10},{9,11},{10,... | collective-permute-start | bytes 147464 | tf_op jit(solution)/shard_map/ppermute | solution.py:601
  65.8 1.3 %collective-permute-start.4 = (bf16[32,768]{1,0:T(8,128)(2,1)S(1)}, bf16[32,768]{1,0:T(8,128)(2,1)S(1)}, u32[]{:S(2)}, u32[]{:S(2)}) collective-permute-start(bf16[32,768]{1,0:T(8,128)(2,1)S(1)} %get-tuple-element.46.p0), channel_id=1, source_target_pairs={{0,3},{1,0},{2,1},{3,2},{4,7},{5,4},{6,5},{7,6},{8,11},{9,8},{10,9... | collective-permute-start | bytes 147464 | tf_op jit(solution)/shard_map/ppermute | solution.py:601
  67.2 2.8 %load_weights.1 = (bf16[768,1536]{1,0:T(8,128)(2,1)S(1)}, bf16[3,1536,384]{2,1,0:T(8,128)(2,1)S(1)}) custom-call(bf16[32,768]{1,0:T(8,128)(2,1)S(1)} %collective-permute-done.2._.p1, bf16[768,1536]{1,0:T(8,128)(2,1)} %merge_ref.1, bf16[3,1536,384]{2,1,0:T(8,128)(2,1)} %bitcast.13), custom_call_target="tpu_custom_call" | custom-call | bytes 6000000 | tf_op jit(solution)/shard_map/load_weights/pallas_call | solution.py:387
  70.0 2.0 %coarse_project.1 = (bf16[32,1536]{1,0:T(8,128)(2,1)S(1)}, bf16[32,384]{1,0:T(8,128)(2,1)}, bf16[8,32,768]{2,1,0:T(8,128)(2,1)}) custom-call(bf16[32,768]{1,0:T(8,128)(2,1)S(1)} %get-tuple-element.46.p0, bf16[32,768]{1,0:T(8,128)(2,1)S(1)} %collective-permute-done.2._.p1, bf16[32,768]{1,0:T(8,128)(2,1)S(1)} %collective-permute-done.3.p2, ...), custom_call_target="tpu_custom_call" | custom-call | flops 188743680 | bytes 7000000 | tf_op jit(solution)/shard_map/coarse_project/pallas_call | solution.py:419
  72.0 5.9 %all-to-all-start = ((bf16[8,32,768]{2,1,0:T(8,128)(2,1)}), bf16[8,32,768]{2,1,0:T(8,128)(2,1)S(1)}, u32[]{:S(2)}, u32[]{:S(2)}) async-start(bf16[8,32,768]{2,1,0:T(8,128)(2,1)} %get-tuple-element.50), calls=%async_computation | async-start | bytes 786432 | tf_op jit(solution)/shard_map/all_to_all | solution.py:635
  78.4 2.4 %collective-permute-start.6 = (bf16[32,384]{1,0:T(8,128)(2,1)}, bf16[32,384]{1,0:T(8,128)(2,1)S(1)}, u32[]{:S(2)}, u32[]{:S(2)}) collective-permute-start(bf16[32,384]{1,0:T(8,128)(2,1)} %get-tuple-element.62.q0), channel_id=1, source_target_pairs={{0,128},{64,192},{128,0},{192,64},{1,129},{65,193},{129,1},{193,65... | collective-permute-start | bytes 73736 | tf_op jit(solution)/shard_map/ppermute | solution.py:601
  80.8 4.5 %own_features.1 = (bf16[4,512,192]{2,1,0:T(8,128)(2,1)S(1)}, bf16[512,192]{1,0:T(8,128)(2,1)S(1)}, bf16[512,192]{1,0:T(8,128)(2,1)S(1)}, bf16[512,192]{1,0:T(8,128)(2,1)S(1)}) custom-call(s32[1]{0:T(128)} %bitcast.6.place_ref, bf16[4,512,768]{2,1,0:T(8,128)(2,1)} %bitcast.15, bf16[4,192,768]{2,1,0:T(8,128)(2,1)} %bitcast.17), custom_call_target="tpu_custom_call" | custom-call | flops 603979776 | bytes 5000000 | tf_op jit(solution)/shard_map/own_features/pallas_call | solution.py:524
  86.1 3.9 %all-to-all-done = bf16[8,32,768]{2,1,0:T(8,128)(2,1)S(1)} async-done(((bf16[8,32,768]{2,1,0:T(8,128)(2,1)}), bf16[8,32,768]{2,1,0:T(8,128)(2,1)S(1)}, u32[]{:S(2)}, u32[]{:S(2)}) %all-to-all-start) | async-done | bytes 393248 | tf_op jit(solution)/shard_map/all_to_all | solution.py:635
  90.1 1.7 %collective-permute-done.8.other_ref = bf16[256,768]{1,0:T(8,128)(2,1)S(1)} collective-permute-done((bf16[256,768]{1,0:T(8,128)(2,1)S(1)}, bf16[256,768]{1,0:T(8,128)(2,1)S(1)}, u32[]{:S(2)}, u32[]{:S(2)}) %collective-permute-start.8) | collective-permute-done | bytes 393248 | tf_op jit(solution)/shard_map/ppermute | solution.py:639
  91.8 1.7 %coarse_attend.1 = (bf16[32,512]{1,0:T(8,128)(2,1)S(1)}, bf16[32,512]{1,0:T(8,128)(2,1)S(1)}, bf16[32,512]{1,0:T(8,128)(2,1)S(1)}, bf16[32,512]{1,0:T(8,128)(2,1)S(1)}) custom-call(bf16[32,384]{1,0:T(8,128)(2,1)} %get-tuple-element.62.q0, bf16[32,384]{1,0:T(8,128)(2,1)S(1)} %collective-permute-done.5.q1, bf16[32,384]{1,0:T(8,128)(2,1)S(1)} %collective-permute-done.6.q2, ...), custom_call_target="tpu_custom_call" | custom-call | flops 100663296 | bytes 1000000 | tf_op jit(solution)/shard_map/coarse_attend/pallas_call | solution.py:461
  93.5 1.7 %collective-permute-start.10 = (bf16[32,512]{1,0:T(8,128)(2,1)S(1)}, bf16[32,512]{1,0:T(8,128)(2,1)S(1)}, u32[]{:S(2)}, u32[]{:S(2)}) collective-permute-start(bf16[32,512]{1,0:T(8,128)(2,1)S(1)} %get-tuple-element.69), channel_id=1, source_target_pairs={{0,128},{64,192},{128,0},{192,64},{1,129},{65,193},{129,1},{193,65... | collective-permute-start | bytes 98312 | tf_op jit(solution)/shard_map/ppermute | solution.py:601
  95.2 2.1 %collective-permute-start.11 = (bf16[32,512]{1,0:T(8,128)(2,1)S(1)}, bf16[32,512]{1,0:T(8,128)(2,1)S(1)}, u32[]{:S(2)}, u32[]{:S(2)}) collective-permute-start(bf16[32,512]{1,0:T(8,128)(2,1)S(1)} %get-tuple-element.70), channel_id=1, source_target_pairs={{0,64},{64,128},{128,192},{192,0},{1,65},{65,129},{129,193},{193,1... | collective-permute-start | bytes 98312 | tf_op jit(solution)/shard_map/ppermute | solution.py:601
  97.3 1.9 %collective-permute-done.10.p2 = bf16[32,512]{1,0:T(8,128)(2,1)S(1)} collective-permute-done((bf16[32,512]{1,0:T(8,128)(2,1)S(1)}, bf16[32,512]{1,0:T(8,128)(2,1)S(1)}, u32[]{:S(2)}, u32[]{:S(2)}) %collective-permute-start.10) | collective-permute-done | bytes 32800 | tf_op jit(solution)/shard_map/ppermute | solution.py:601
  99.2 3.2 %collective-permute-done.9.p1 = bf16[32,512]{1,0:T(8,128)(2,1)S(1)} collective-permute-done((bf16[32,512]{1,0:T(8,128)(2,1)S(1)}, bf16[32,512]{1,0:T(8,128)(2,1)S(1)}, u32[]{:S(2)}, u32[]{:S(2)}) %collective-permute-start.9) | collective-permute-done | bytes 32800 | tf_op jit(solution)/shard_map/ppermute | solution.py:601
  103.7 3.0 %collective-permute-start.13 = (bf16[32,1536]{1,0:T(8,128)(2,1)S(1)}, bf16[32,1536]{1,0:T(8,128)(2,1)S(1)}, u32[]{:S(2)}, u32[]{:S(2)}) collective-permute-start(bf16[32,1536]{1,0:T(8,128)(2,1)S(1)} %coarse_combine.1.p0), channel_id=1, source_target_pairs={{0,2},{1,3},{2,0},{3,1},{4,6},{5,7},{6,4},{7,5},{8,10},{9,11},{10,... | collective-permute-start | bytes 294920 | tf_op jit(solution)/shard_map/ppermute | solution.py:601
  107.1 2.9 %hidden_rows.1.hidden_ref = bf16[4,512,192]{2,1,0:T(8,128)(2,1)S(1)} custom-call(bf16[4,512,192]{2,1,0:T(8,128)(2,1)S(1)} %get-tuple-element.56.x_ref, bf16[4,2,1536,128]{3,2,1,0:T(8,128)(2,1)} %bitcast.16, bf16[512,192]{1,0:T(8,128)(2,1)S(1)} %get-tuple-element.58.pair_ref, bf16[512,192]{1,0:T(8,128)(2,1)S(1)} %get-tuple-element.59.low_ref, ...), custom_call_target="tpu_custom_call" | custom-call | flops 805306368 | bytes 5000000 | tf_op jit(solution)/shard_map/hidden_rows/pallas_call | solution.py:555
  111.2 1.8 %split_rows.1 = bf16[4,16,32,192]{3,2,1,0:T(8,128)(2,1)} custom-call(bf16[4,512,192]{2,1,0:T(8,128)(2,1)S(1)} %hidden_rows.1.hidden_ref, bf16[32,1536]{1,0:T(8,128)(2,1)S(1)} %get-tuple-element.61.coarse_ref, bf16[32,1536]{1,0:T(8,128)(2,1)S(1)} %coarse_combine.1.p0, bf16[32,1536]{1,0:T(8,128)(2,1)S(1)} %collective-permute-done.12.p1, ...), custom_call_target="tpu_custom_call" | custom-call | flops 18874368 | bytes 4000000 | tf_op jit(solution)/shard_map/split_rows/pallas_call | solution.py:591
  (43 shorter events, 6.4 us)
Async XLA Ops:
  6.5 74.3 %all-gather.5.cloned.1.call-start = ((), (), s32[]{:S(2)}) async-start(), calls=%async_computation.1 | async-start | bytes 1474560 | tf_op jit(solution)/shard_map/all_gather | solution.py:617
  7.3 99.8 %all-gather.7.cloned.1.call-start = ((), (), s32[]{:S(2)}) async-start(), calls=%async_computation.2 | async-start | bytes 3932160 | tf_op jit(solution)/shard_map/all_gather | solution.py:630
  8.0 17.6 %copy-start.4 = (bf16[4,128,384]{2,1,0:T(8,128)(2,1)S(1)}, bf16[4,128,384]{2,1,0:T(8,128)(2,1)}, u32[]{:S(2)}) copy-start(bf16[4,128,384]{2,1,0:T(8,128)(2,1)} %constant.31.clone.mask_ref) | copy-start | bytes 1179652
  16.1 29.7 %collective-permute-start = (bf16[512,384]{1,0:T(8,128)(2,1)}, bf16[512,384]{1,0:T(8,128)(2,1)S(1)}, u32[]{:S(2)}, u32[]{:S(2)}) collective-permute-start(bf16[512,384]{1,0:T(8,128)(2,1)} %get-tuple-element.42), channel_id=1, source_target_pairs={{0,4},{4,8},{8,12},{12,16},{16,20},{20,24},{24,28},{28,32},{32,36}... | collective-permute-start | bytes 1179656 | tf_op jit(solution)/shard_map/ppermute | solution.py:621
  18.0 27.7 %collective-permute-start.1 = (bf16[512,384]{1,0:T(8,128)(2,1)}, bf16[512,384]{1,0:T(8,128)(2,1)}, u32[]{:S(2)}, u32[]{:S(2)}) collective-permute-start(bf16[512,384]{1,0:T(8,128)(2,1)} %get-tuple-element.43), channel_id=1, source_target_pairs={{4,0},{8,4},{12,8},{16,12},{20,16},{24,20},{28,24},{32,28},{36,32}... | collective-permute-start | bytes 1179656 | tf_op jit(solution)/shard_map/ppermute | solution.py:622
  27.0 18.8 %copy-start.1 = (bf16[192,768]{1,0:T(8,128)(2,1)S(1)}, bf16[192,768]{1,0:T(8,128)(2,1)}, u32[]{:S(2)}) copy-start(bf16[192,768]{1,0:T(8,128)(2,1)} %weight_ref.2) | copy-start | bytes 884740
  61.3 5.9 %collective-permute-start.2 = (bf16[32,768]{1,0:T(8,128)(2,1)S(1)}, bf16[32,768]{1,0:T(8,128)(2,1)S(1)}, u32[]{:S(2)}, u32[]{:S(2)}) collective-permute-start(bf16[32,768]{1,0:T(8,128)(2,1)S(1)} %get-tuple-element.46.p0), channel_id=1, source_target_pairs={{0,1},{1,2},{2,3},{3,0},{4,5},{5,6},{6,7},{7,4},{8,9},{9,10},{10,1... | collective-permute-start | bytes 147464 | tf_op jit(solution)/shard_map/ppermute | solution.py:601
  62.9 7.0 %collective-permute-start.3 = (bf16[32,768]{1,0:T(8,128)(2,1)S(1)}, bf16[32,768]{1,0:T(8,128)(2,1)S(1)}, u32[]{:S(2)}, u32[]{:S(2)}) collective-permute-start(bf16[32,768]{1,0:T(8,128)(2,1)S(1)} %get-tuple-element.46.p0), channel_id=1, source_target_pairs={{0,2},{1,3},{2,0},{3,1},{4,6},{5,7},{6,4},{7,5},{8,10},{9,11},{10,... | collective-permute-start | bytes 147464 | tf_op jit(solution)/shard_map/ppermute | solution.py:601
  65.8 4.1 %collective-permute-start.4 = (bf16[32,768]{1,0:T(8,128)(2,1)S(1)}, bf16[32,768]{1,0:T(8,128)(2,1)S(1)}, u32[]{:S(2)}, u32[]{:S(2)}) collective-permute-start(bf16[32,768]{1,0:T(8,128)(2,1)S(1)} %get-tuple-element.46.p0), channel_id=1, source_target_pairs={{0,3},{1,0},{2,1},{3,2},{4,7},{5,4},{6,5},{7,6},{8,11},{9,8},{10,9... | collective-permute-start | bytes 147464 | tf_op jit(solution)/shard_map/ppermute | solution.py:601
  67.2 2.8 %copy-start.6 = (f32[32,768]{1,0:T(8,128)S(1)}, f32[32,768]{1,0:T(8,128)}, u32[]{:S(2)}) copy-start(f32[32,768]{1,0:T(8,128)} %copy-done.5) | copy-start | bytes 294916
  67.2 2.8 %copy-start.7 = (f32[1536]{0:T(1024)S(1)}, f32[1536]{0:T(1024)}, u32[]{:S(2)}) copy-start(f32[1536]{0:T(1024)} %gain_ref.3) | copy-start | bytes 18436
  72.0 18.1 %all-to-all-start = ((bf16[8,32,768]{2,1,0:T(8,128)(2,1)}), bf16[8,32,768]{2,1,0:T(8,128)(2,1)S(1)}, u32[]{:S(2)}, u32[]{:S(2)}) async-start(bf16[8,32,768]{2,1,0:T(8,128)(2,1)} %get-tuple-element.50), calls=%async_computation | async-start | bytes 786432 | tf_op jit(solution)/shard_map/all_to_all | solution.py:635
  77.9 7.5 %collective-permute-start.5 = (bf16[32,384]{1,0:T(8,128)(2,1)}, bf16[32,384]{1,0:T(8,128)(2,1)S(1)}, u32[]{:S(2)}, u32[]{:S(2)}) collective-permute-start(bf16[32,384]{1,0:T(8,128)(2,1)} %get-tuple-element.62.q0), channel_id=1, source_target_pairs={{0,64},{64,128},{128,192},{192,0},{1,65},{65,129},{129,193},{193,1... | collective-permute-start | bytes 73736 | tf_op jit(solution)/shard_map/ppermute | solution.py:601
  78.4 7.0 %collective-permute-start.6 = (bf16[32,384]{1,0:T(8,128)(2,1)}, bf16[32,384]{1,0:T(8,128)(2,1)S(1)}, u32[]{:S(2)}, u32[]{:S(2)}) collective-permute-start(bf16[32,384]{1,0:T(8,128)(2,1)} %get-tuple-element.62.q0), channel_id=1, source_target_pairs={{0,128},{64,192},{128,0},{192,64},{1,129},{65,193},{129,1},{193,65... | collective-permute-start | bytes 73736 | tf_op jit(solution)/shard_map/ppermute | solution.py:601
  80.8 5.4 %collective-permute-start.7 = (bf16[32,384]{1,0:T(8,128)(2,1)}, bf16[32,384]{1,0:T(8,128)(2,1)}, u32[]{:S(2)}, u32[]{:S(2)}) collective-permute-start(bf16[32,384]{1,0:T(8,128)(2,1)} %get-tuple-element.62.q0), channel_id=1, source_target_pairs={{0,192},{64,0},{128,64},{192,128},{1,193},{65,1},{129,65},{193,129... | collective-permute-start | bytes 73736 | tf_op jit(solution)/shard_map/ppermute | solution.py:601
  80.8 21.6 %copy-start.2 = (bf16[384,1536]{1,0:T(8,128)(2,1)S(1)}, bf16[384,1536]{1,0:T(8,128)(2,1)}, u32[]{:S(2)}) copy-start(bf16[384,1536]{1,0:T(8,128)(2,1)} %weight_ref.3) | copy-start | bytes 3538948
  90.1 1.7 %collective-permute-start.8 = (bf16[256,768]{1,0:T(8,128)(2,1)S(1)}, bf16[256,768]{1,0:T(8,128)(2,1)S(1)}, u32[]{:S(2)}, u32[]{:S(2)}) collective-permute-start(bf16[256,768]{1,0:T(8,128)(2,1)S(1)} %bitcast.10), channel_id=1, source_target_pairs={{0,4},{4,0},{1,5},{5,1},{2,6},{6,2},{3,7},{7,3},{8,12},{12,8},{9,1... | collective-permute-start | bytes 1179656 | tf_op jit(solution)/shard_map/ppermute | solution.py:639
  93.5 5.7 %collective-permute-start.10 = (bf16[32,512]{1,0:T(8,128)(2,1)S(1)}, bf16[32,512]{1,0:T(8,128)(2,1)S(1)}, u32[]{:S(2)}, u32[]{:S(2)}) collective-permute-start(bf16[32,512]{1,0:T(8,128)(2,1)S(1)} %get-tuple-element.69), channel_id=1, source_target_pairs={{0,128},{64,192},{128,0},{192,64},{1,129},{65,193},{129,1},{193,65... | collective-permute-start | bytes 98312 | tf_op jit(solution)/shard_map/ppermute | solution.py:601
  95.2 4.0 %collective-permute-start.11 = (bf16[32,512]{1,0:T(8,128)(2,1)S(1)}, bf16[32,512]{1,0:T(8,128)(2,1)S(1)}, u32[]{:S(2)}, u32[]{:S(2)}) collective-permute-start(bf16[32,512]{1,0:T(8,128)(2,1)S(1)} %get-tuple-element.70), channel_id=1, source_target_pairs={{0,64},{64,128},{128,192},{192,0},{1,65},{65,129},{129,193},{193,1... | collective-permute-start | bytes 98312 | tf_op jit(solution)/shard_map/ppermute | solution.py:601
  97.3 5.1 %collective-permute-start.9 = (bf16[32,512]{1,0:T(8,128)(2,1)S(1)}, bf16[32,512]{1,0:T(8,128)(2,1)S(1)}, u32[]{:S(2)}, u32[]{:S(2)}) collective-permute-start(bf16[32,512]{1,0:T(8,128)(2,1)S(1)} %get-tuple-element.68), channel_id=1, source_target_pairs={{0,192},{64,0},{128,64},{192,128},{1,193},{65,1},{129,65},{193,129... | collective-permute-start | bytes 98312 | tf_op jit(solution)/shard_map/ppermute | solution.py:601
  102.9 7.1 %collective-permute-start.12 = (bf16[32,1536]{1,0:T(8,128)(2,1)S(1)}, bf16[32,1536]{1,0:T(8,128)(2,1)S(1)}, u32[]{:S(2)}, u32[]{:S(2)}) collective-permute-start(bf16[32,1536]{1,0:T(8,128)(2,1)S(1)} %coarse_combine.1.p0), channel_id=1, source_target_pairs={{0,1},{1,2},{2,3},{3,0},{4,5},{5,6},{6,7},{7,4},{8,9},{9,10},{10,1... | collective-permute-start | bytes 294920 | tf_op jit(solution)/shard_map/ppermute | solution.py:601
  103.7 6.6 %collective-permute-start.13 = (bf16[32,1536]{1,0:T(8,128)(2,1)S(1)}, bf16[32,1536]{1,0:T(8,128)(2,1)S(1)}, u32[]{:S(2)}, u32[]{:S(2)}) collective-permute-start(bf16[32,1536]{1,0:T(8,128)(2,1)S(1)} %coarse_combine.1.p0), channel_id=1, source_target_pairs={{0,2},{1,3},{2,0},{3,1},{4,6},{5,7},{6,4},{7,5},{8,10},{9,11},{10,... | collective-permute-start | bytes 294920 | tf_op jit(solution)/shard_map/ppermute | solution.py:601
  106.6 4.6 %collective-permute-start.14 = (bf16[32,1536]{1,0:T(8,128)(2,1)S(1)}, bf16[32,1536]{1,0:T(8,128)(2,1)S(1)}, u32[]{:S(2)}, u32[]{:S(2)}) collective-permute-start(bf16[32,1536]{1,0:T(8,128)(2,1)S(1)} %coarse_combine.1.p0), channel_id=1, source_target_pairs={{0,3},{1,0},{2,1},{3,2},{4,7},{5,4},{6,5},{7,6},{8,11},{9,8},{10,9... | collective-permute-start | bytes 294920 | tf_op jit(solution)/shard_map/ppermute | solution.py:601
  107.1 4.2 %copy-start.3 = (bf16[1536,192]{0,1:T(8,128)(2,1)S(1)}, bf16[1536,192]{0,1:T(8,128)(2,1)}, u32[]{:S(2)}) copy-start(bf16[1536,192]{0,1:T(8,128)(2,1)} %param.18) | copy-start | bytes 1769476
  (3 other events, 2.7 us)
Sparse Core Ops, SparseCore 0:
  9.2 29.8 all-gather.4
  61.4 42.4 all-gather.6

commit v2 on v1

v2 whole, which is shorter than its diff:
```python
import functools

import jax
import jax.numpy as jnp
from jax import lax
from jax.experimental import pallas as pl
from jax.experimental.pallas import tpu as pltpu
from jax.sharding import PartitionSpec as P

HEADS = 12
EPSILON = 1e-06
REACH = 3
LOG2E = 1.4426950408889634
ROWS, COLS = 16, 32
TOKENS = ROWS * COLS
FRAMES = ("x", "z", "core")
MIB = 1 << 20
bf16, f32 = jnp.bfloat16, jnp.float32


def nt_dot(a, b):
    return lax.dot_general(a, b, (((1,), (1,)), ((), ())), preferred_element_type=f32)


def nn_dot(a, b):
    return jnp.dot(a, b, preferred_element_type=f32)


def block_mean_matrix(rows):
    token = lax.broadcasted_iota(jnp.int32, (32, rows * COLS), 1)
    block = lax.broadcasted_iota(jnp.int32, (32, rows * COLS), 0)
    of_token = token // (rows * COLS // 4) * 8 + ((token & 31) >> 2)
    return jnp.where(of_token == block, 1.0 / 64, 0.0)


def params(mib):
    return pltpu.CompilerParams(vmem_limit_bytes=mib * MIB)


def cost(flops, bytes_accessed, transcendentals=0):
    return pl.CostEstimate(
        flops=int(flops), bytes_accessed=int(bytes_accessed), transcendentals=int(transcendentals)
    )


def whole(*shape):
    return pl.BlockSpec(shape, lambda *i: (0,) * len(shape))


def fine_project_kernel(
    place_ref, x_hbm, gain_hbm, weight_hbm,
    q_ref, key_ref, ones_ref, initial_hbm, last_hbm, mean_hbm, own_hbm,
    x_ref, gain_ref, weight_ref, rows_ref, sum_ref, edge_ref, own_ref, mean_ref,
    in_sems, out_sems,
):
    gain_copy = pltpu.make_async_copy(gain_hbm, gain_ref, in_sems.at[5])
    gain_copy.start()
    weight_copy = pltpu.make_async_copy(weight_hbm, weight_ref, in_sems.at[4])
    weight_copy.start()
    x_copies = [
        pltpu.make_async_copy(x_hbm.at[frame], x_ref.at[frame], in_sems.at[frame])
        for frame in range(4)
    ]
    order = (0, 3, 1, 2)
    for frame in order:
        x_copies[frame].start()
    gain_copy.wait()
    weight_copy.wait()
    gain = gain_ref[...].reshape(1, 768)
    query, key, value = (weight_ref[i].astype(f32) * gain for i in range(3))
    rows_ref[:192, :] = value.astype(bf16)
    rows_ref[192:384, :] = key.astype(bf16)
    rows_ref[384:, :] = (query * (0.125 * LOG2E)).astype(bf16)

    out_copies = [
        pltpu.make_async_copy(edge_ref.at[i], out, out_sems.at[i])
        for i, out in enumerate((initial_hbm, last_hbm))
    ]

    for step, frame in enumerate(order):
        x_copies[frame].wait()
        if step == 3:
            for place in range(4):

                @pl.when(place_ref[0] == place)
                def _():
                    own_ref[...] = x_ref[:, :, 192 * place : 192 * place + 192]

            out_copies.append(pltpu.make_async_copy(own_ref, own_hbm, out_sems.at[2]))
            out_copies[-1].start()
        x = x_ref[frame]
        wide = x.astype(f32)
        projected = nt_dot(x, rows_ref[...])
        scale = lax.rsqrt(jnp.mean(wide * wide, axis=-1, keepdims=True) + EPSILON)
        projected = projected * scale
        q_ref[frame] = projected[:, 384:].astype(bf16)
        pairs = projected[:, :384]
        lane = lax.broadcasted_iota(jnp.int32, (1, 256), 1)
        ones_ref[frame] = jnp.where(lane < 192, projected[:, :256], 1.0).astype(bf16)
        along = jnp.transpose(jnp.broadcast_to(scale, (TOKENS, 128)))[:1]
        key_ref[frame] = (nt_dot(rows_ref[192:384, :], x) * along).astype(bf16)
        added = jnp.sum(wide.reshape(4, 4, COLS, 768), axis=1).reshape(4 * COLS, 768)
        sum_ref[...] = sum_ref[...] + added if step else added
        if step < 2:
            edge_ref[step] = pairs.astype(bf16)
            out_copies[step].start()
    mean_ref[...] = jnp.dot(
        block_mean_matrix(4),
        sum_ref[...],
        preferred_element_type=f32,
        precision=lax.Precision.HIGHEST,
    )
    out_copies.append(pltpu.make_async_copy(mean_ref, mean_hbm, out_sems.at[3]))
    out_copies[-1].start()
    for copy in out_copies:
        copy.wait()


def in_hbm(*arrays):
    return [pltpu.with_memory_space_constraint(array, pltpu.HBM) for array in arrays]


def fine_project(place, x, gain, weight):
    vmem, hbm = pl.BlockSpec(memory_space=pltpu.VMEM), pl.BlockSpec(memory_space=pltpu.HBM)
    return pl.pallas_call(
        fine_project_kernel,
        in_specs=[pl.BlockSpec(memory_space=pltpu.SMEM), hbm, hbm, hbm],
        out_specs=[vmem, vmem, vmem, hbm, hbm, hbm, hbm],
        out_shape=[
            jax.ShapeDtypeStruct((4, TOKENS, 192), bf16),
            jax.ShapeDtypeStruct((4, 192, TOKENS), bf16),
            jax.ShapeDtypeStruct((4, TOKENS, 256), bf16),
            pltpu.HBM((TOKENS, 384), bf16),
            pltpu.HBM((TOKENS, 384), bf16),
            pltpu.HBM((32, 768), f32),
            pltpu.HBM((4, TOKENS, 192), bf16),
        ],
        scratch_shapes=[
            pltpu.VMEM((4, TOKENS, 768), bf16),
            pltpu.VMEM((768,), f32),
            pltpu.VMEM((3, 192, 768), bf16),
            pltpu.VMEM((576, 768), bf16),
            pltpu.VMEM((128, 768), f32),
            pltpu.VMEM((2, TOKENS, 384), bf16),
            pltpu.VMEM((4, TOKENS, 192), bf16),
            pltpu.VMEM((32, 768), f32),
            pltpu.SemaphoreType.DMA((6,)),
            pltpu.SemaphoreType.DMA((4,)),
        ],
        compiler_params=params(24),
        cost_estimate=cost(2 * 2048 * 768 * 768, 8e6),
        name="fine_project",
    )(place, *in_hbm(x, gain, weight))


BASES = (0, 0, 128, 128)
WINDOWS = ((0, 256), (0, 384), (128, 512), (256, 512))


def near_keys(tile, base):
    query = lax.broadcasted_iota(jnp.int32, (128, 384), 0) + 128 * tile
    key = lax.broadcasted_iota(jnp.int32, (128, 384), 1) + base
    rows = jnp.abs((query >> 5) - (key >> 5))
    cols = jnp.abs((query & 31) - (key & 31))
    return (rows <= REACH) & (cols <= REACH)


def outside_range(total, least):
    low = lax.broadcasted_iota(jnp.int32, (128, 128), 1) < 64
    bad = jnp.where((total < 2.0**60) & (least > 2.0**-60), 0.0, 1.0)
    return jnp.max(jnp.where(low, bad, 0.0))


def rows_at(part, tile):
    start = part * TOKENS + tile * 128
    return pl.ds(start if isinstance(start, int) else pl.multiple_of(start, 128), 128)


def window_of(tile):
    base = pl.multiple_of((tile >> 1) * 128, 128)
    return base, pl.ds(base, 384), pl.ds(pl.multiple_of(tile * 128, 128), 128)


def put_rows(out_ref, tile, pair):
    low = lax.broadcasted_iota(jnp.int32, (128, 128), 1) < 64
    thirds, counts = [], []
    for at, sums in enumerate(pair):
        turned = [pltpu.roll(one, 64, axis=1) for one in sums]
        heads = [one / other for one, other in zip(sums, turned)]
        out_ref[0, rows_at(at, tile), :] = jnp.where(
            low, heads[0], heads[1]
        ).astype(bf16)
        thirds.append(heads[2])
        counts += [turned[0], sums[1], turned[2]]
    packed = jnp.where(low, thirds[0], pltpu.roll(thirds[1], 64, axis=1))
    out_ref[0, rows_at(2, tile), :] = packed.astype(bf16)
    return sum(counts), functools.reduce(jnp.minimum, counts)


def stack_heads(query):
    head = lax.broadcasted_iota(jnp.int32, (1, 192), 1) >> 6
    return jnp.concatenate(
        [query * jnp.where(head == i, 1.0, 0.0).astype(bf16) for i in range(3)], axis=0
    )


def own_parts(summed):
    low = lax.broadcasted_iota(jnp.int32, (1, 128, 128), 2) < 64
    first, second = summed[..., :128], summed[..., 128:]
    n = summed.shape[1]
    turned = pltpu.roll(second[1].reshape(n * 128, 128), 64, axis=1).reshape(n, 128, 128)
    return [
        jnp.where(low, first[0], second[0]),
        jnp.where(low, turned, first[1]),
        second[2],
    ]


def attend_again(q_ref, frames, out_ref):
    def redo(tile, _):
        base, window, own = window_of(tile)
        near = jnp.concatenate([near_keys(tile, base)] * 3, axis=0)
        pair = []
        for frame, sources in frames:
            query = stack_heads(q_ref[frame, own, :])
            scores = []
            for keys, _, inside in sources:
                seen = near if inside is None else near & (inside > 0.0)
                scores.append(jnp.where(seen, nn_dot(query, keys[:, window]), -jnp.inf))
            top = jnp.max(
                jnp.maximum(jnp.maximum(scores[0], scores[1]), scores[2]), axis=-1, keepdims=True
            )
            summed = sum(
                nn_dot(jnp.exp2(score - top).astype(bf16), ones[window, :])
                for score, (_, ones, _) in zip(scores, sources)
            )
            pair.append([part[0] for part in own_parts(summed.reshape(3, 1, 128, 256))])
        put_rows(out_ref, tile, pair)
        return 0

    lax.fori_loop(0, 4, redo, 0)


def weigh(query, keys, ones, mask):
    n = query.shape[0]
    weights = jnp.exp2(nn_dot(stack_heads(query.reshape(n * 128, 192)), keys)).astype(bf16)
    weights = (weights.reshape(3 * n, *mask.shape) * mask[None]).reshape(-1, mask.shape[1])
    return own_parts(nn_dot(weights, ones).reshape(3, n, 128, 256))


def tiles():
    for tile in range(4):
        first, last = WINDOWS[tile]
        own = slice(128 * tile, 128 * tile + 128)
        yield tile, own, slice(first, last), slice(first - BASES[tile], last - BASES[tile])


def block_means(out_ref):
    matrix = block_mean_matrix(ROWS).astype(bf16)
    pairs = nn_dot(matrix, out_ref[0, :TOKENS, :])
    pairs += nn_dot(matrix, out_ref[0, TOKENS : 2 * TOKENS, :])
    return pairs, nn_dot(matrix, out_ref[0, 2 * TOKENS :, :])


def set_weights(weight_ref, first_ref, third_ref):
    first_ref[...] = jnp.zeros_like(first_ref)
    third_ref[...] = jnp.zeros_like(third_ref)
    for place in range(4):
        weight = weight_ref[:, 192 * place : 192 * place + 192]
        lanes = slice(128 * place, 128 * place + 128)
        for at in (0, 1):
            first_ref[at, :128, lanes] = weight[:128, :128]
            first_ref[at, 128 + 64 * at : 192 + 64 * at, lanes] = weight[128:, :128]
            half = slice(128 * place + 64 * at, 128 * place + 64 * at + 64)
            third_ref[128 * at : 128 * at + 128, half] = weight[:128, 128:]
            third_ref[256 + 64 * at : 320 + 64 * at, half] = weight[128:, 128:]


def put_products(rows_ref, first_ref, third_ref, out_ref, out_hbm, sems):
    parts = [rows_ref[0, TOKENS * i : TOKENS * (i + 1), :] for i in range(3)]
    copies = []
    for i in range(3):
        if i < 2:
            product = nn_dot(jnp.concatenate([parts[i], parts[2]], axis=1), first_ref[i])
        else:
            product = nn_dot(jnp.concatenate(parts, axis=1), third_ref[...])
        own = pl.ds(TOKENS * i, TOKENS)
        for place in range(4):
            out_ref[place, own, :] = product[:, 128 * place : 128 * place + 128].astype(bf16)
        copies.append(
            pltpu.make_async_copy(out_ref.at[:, own, :], out_hbm.at[:, own, :], sems.at[i])
        )
        copies[-1].start()
    for copy in copies:
        copy.wait()


def inner_kernel(
    q_ref, k_ref, v_ref, weight_hbm,
    out_hbm, mask_ref, mean_ref, part_ref, first_ref, third_ref, rows_ref, out_ref, weight_ref, sems,
):
    weight_copy = pltpu.make_async_copy(weight_hbm, weight_ref, sems.at[3])
    weight_copy.start()

    total, least = jnp.zeros((128, 128), f32), jnp.ones((128, 128), f32)
    for tile, own, window, seen in tiles():
        mask_ref[tile] = jnp.where(near_keys(tile, BASES[tile]), 1.0, 0.0).astype(bf16)
        sums = [None] * 4
        for g in range(4):
            lo, hi = max(g - 1, 0), min(g + 1, 3)
            parts = weigh(
                q_ref[lo : hi + 1, own, :],
                k_ref[g, :, window],
                v_ref[g, window, :],
                mask_ref[tile, :, seen],
            )
            for f in range(lo, hi + 1):
                here = [part[f - lo] for part in parts]
                sums[f] = here if sums[f] is None else [a + b for a, b in zip(sums[f], here)]
        for head in range(3):
            lanes = slice(128 * head, 128 * head + 128)
            part_ref[0, own, lanes] = sums[0][head]
            part_ref[1, own, lanes] = sums[3][head]
        tile_total, tile_least = put_rows(rows_ref, tile, sums[1:3])
        total, least = total + tile_total, jnp.minimum(least, tile_least)
    bad = outside_range(total, least)

    @pl.when(bad > 0.0)
    def _():
        own_frames = [(k_ref.at[g], v_ref.at[g], None) for g in range(4)]
        attend_again(q_ref, [(1, own_frames[:3]), (2, own_frames[1:])], rows_ref)

    mean_ref[:, :128], mean_ref[:, 128:] = block_means(rows_ref)
    weight_copy.wait()
    set_weights(weight_ref, first_ref, third_ref)
    put_products(rows_ref, first_ref, third_ref, out_ref, out_hbm.at[:, 0], sems)


def outer_kernel(
    edge_ref, mask_ref, q_ref, k_ref, v_ref, part_ref, halo_first_ref, halo_last_ref,
    inner_mean_ref, first_ref, third_ref, weight_hbm, inner_ref,
    out_hbm, partial_ref, halo_key_ref, halo_ones_ref,
    rows_ref, out_ref, weight_ref, sems,
):
    weight_copy = pltpu.make_async_copy(weight_hbm, weight_ref, sems.at[3])
    weight_copy.start()
    lane = lax.broadcasted_iota(jnp.int32, (1, 256), 1)
    for at, halo_ref in enumerate((halo_first_ref, halo_last_ref)):
        halo = halo_ref[...].astype(f32)
        halo_ones_ref[at] = (jnp.where(lane < 192, halo[:, :256], 1.0) * edge_ref[at]).astype(bf16)
        halo_key_ref[at] = jnp.transpose(halo)[192:].astype(bf16)

    total, least = jnp.zeros((128, 128), f32), jnp.ones((128, 128), f32)
    for tile, own, window, seen in tiles():
        pair = []
        for at, frame in enumerate((0, 3)):
            more = weigh(
                q_ref[frame : frame + 1, own, :],
                halo_key_ref[at, :, window],
                halo_ones_ref[at, window, :],
                mask_ref[tile, :, seen],
            )
            pair.append(
                [
                    part_ref[at, own, 128 * head : 128 * head + 128] + more[head][0]
                    for head in range(3)
                ]
            )
        tile_total, tile_least = put_rows(rows_ref, tile, pair)
        total, least = total + tile_total, jnp.minimum(least, tile_least)
    bad = outside_range(total, least)

    @pl.when(bad > 0.0)
    def _():
        own_frames = [(k_ref.at[g], v_ref.at[g], None) for g in range(4)]
        halos = [(halo_key_ref.at[at], halo_ones_ref.at[at], edge_ref[at]) for at in (0, 1)]
        attend_again(
            q_ref, [(0, own_frames[:2] + halos[:1]), (3, own_frames[2:] + halos[1:])], rows_ref
        )

    here = block_means(rows_ref)
    pairs = here[0] + inner_mean_ref[:, :128]
    third = here[1] + inner_mean_ref[:, 128:]
    third = third + pltpu.roll(third, 64, axis=1)
    weight_copy.wait()
    partial = nn_dot(pairs.astype(bf16), weight_ref[:128, :])
    partial += nn_dot(third[:, :64].astype(bf16), weight_ref[128:, :])
    partial_ref[...] = partial.astype(bf16)
    put_products(rows_ref, first_ref, third_ref, out_ref, out_hbm.at[:, 1], sems)


OUT_SCRATCH = [
    pltpu.VMEM((1, 3 * TOKENS, 128), bf16),
    pltpu.VMEM((4, 3 * TOKENS, 128), bf16),
    pltpu.VMEM((192, 768), bf16),
    pltpu.SemaphoreType.DMA((4,)),
]


def attend_inner(q, k, v, weight):
    vmem, hbm = pl.BlockSpec(memory_space=pltpu.VMEM), pl.BlockSpec(memory_space=pltpu.HBM)
    return pl.pallas_call(
        inner_kernel,
        in_specs=[vmem] * 3 + [hbm],
        out_specs=[hbm] + [vmem] * 5,
        out_shape=[
            pltpu.HBM((4, 2, 3 * TOKENS, 128), bf16),
            jax.ShapeDtypeStruct((4, 128, 384), bf16),
            jax.ShapeDtypeStruct((32, 256), f32),
            jax.ShapeDtypeStruct((2, TOKENS, 384), f32),
            jax.ShapeDtypeStruct((2, 256, 512), bf16),
            jax.ShapeDtypeStruct((384, 512), bf16),
        ],
        scratch_shapes=OUT_SCRATCH,
        compiler_params=params(24),
        cost_estimate=cost(10 * 2 * 512 * 320 * 3 * 256, 6e6, 10 * 512 * 320 * 3),
        name="attend_inner",
    )(q, k, v, *in_hbm(weight))


def attend_outer(
    edge, mask, q, k, v, part, first, last, inner_mean, weight, first_weight, third_weight, inner
):
    vmem, hbm = pl.BlockSpec(memory_space=pltpu.VMEM), pl.BlockSpec(memory_space=pltpu.HBM)
    return pl.pallas_call(
        outer_kernel,
        in_specs=[pl.BlockSpec(memory_space=pltpu.SMEM)] + [vmem] * 10 + [hbm] * 2,
        out_specs=[hbm, vmem],
        out_shape=[
            pltpu.HBM((4, 2, 3 * TOKENS, 128), bf16),
            jax.ShapeDtypeStruct((32, 768), bf16),
        ],
        input_output_aliases={12: 0},
        scratch_shapes=[
            pltpu.VMEM((2, 192, TOKENS), bf16),
            pltpu.VMEM((2, TOKENS, 256), bf16),
        ]
        + OUT_SCRATCH,
        compiler_params=params(24),
        cost_estimate=cost(2 * 2 * 512 * 320 * 3 * 256, 6e6, 2 * 512 * 320 * 3),
        name="attend_outer",
    )(
        edge, mask, q, k, v, part, first, last, inner_mean, first_weight, third_weight,
        *in_hbm(weight), inner,
    )


def load_kernel(_, *refs):
    sources, targets, sems = refs[:4], refs[4:8], refs[8]
    copies = [
        pltpu.make_async_copy(source, target, sems.at[i])
        for i, (source, target) in enumerate(zip(sources, targets))
    ]
    for copy in copies:
        copy.start()
    for copy in copies:
        copy.wait()


def load(after, *arrays):
    anywhere = pl.BlockSpec(memory_space=pl.ANY)
    return pl.pallas_call(
        load_kernel,
        in_specs=[anywhere] * 5,
        out_specs=[anywhere] * 4,
        out_shape=[pltpu.VMEM(array.shape, array.dtype) for array in arrays],
        scratch_shapes=[pltpu.SemaphoreType.DMA((4,))],
        compiler_params=params(4),
        cost_estimate=cost(0, 6e6),
        name="load",
    )(after, *in_hbm(*arrays))


def coarse_project_kernel(
    p0, p1, p2, p3, mean_ref, merge_ref, gain_ref, weight_ref, coarse_ref, q_ref, kv_ref
):
    pooled = mean_ref[...] + (
        (p0[...].astype(f32) + p1[...].astype(f32)) + (p2[...].astype(f32) + p3[...].astype(f32))
    )
    coarse = nn_dot(pooled.astype(bf16), merge_ref[...]).astype(bf16)
    coarse_ref[...] = coarse
    wide = coarse.astype(f32)
    scale = lax.rsqrt(jnp.mean(wide * wide, axis=-1, keepdims=True) + EPSILON)
    normed = (wide * scale * gain_ref[...].reshape(1, 1536)).astype(bf16)
    q_ref[...] = (nn_dot(normed, weight_ref[0]) * (128**-0.5 * LOG2E)).astype(bf16)
    key = nn_dot(normed, weight_ref[1]).astype(bf16)
    value = nn_dot(normed, weight_ref[2]).astype(bf16)
    for copy in range(8):
        kv_ref[copy, :, :384] = key
        kv_ref[copy, :, 384:] = value


def coarse_project(partials, mean, merge, gain, weight):
    return pl.pallas_call(
        coarse_project_kernel,
        in_specs=[pl.BlockSpec(memory_space=pltpu.VMEM)] * 8,
        out_specs=[whole(32, 1536), whole(32, 384), whole(8, 32, 768)],
        out_shape=[
            jax.ShapeDtypeStruct((32, 1536), bf16),
            jax.ShapeDtypeStruct((32, 384), bf16),
            pltpu.HBM((8, 32, 768), bf16),
        ],
        compiler_params=params(20),
        cost_estimate=cost(2 * 32 * 1536 * 1920, 7e6),
        name="coarse_project",
    )(*partials, mean, merge, gain, weight)


def coarse_attend_kernel(
    q0, q1, q2, q3, kv_ref, other_ref, split_hbm, o0, o1, o2, o3, split_out, sems
):
    split_copy = pltpu.make_async_copy(split_hbm, split_out, sems.at[0])
    split_copy.start()
    query = jnp.concatenate([ref[...] for ref in (q0, q1, q2, q3)], axis=0)
    outs = (o0, o1, o2, o3)
    lane = lax.broadcasted_iota(jnp.int32, (128, 128), 1)
    stats = jnp.zeros((128, 128), f32)
    for head in range(3):
        lanes = slice(128 * head, 128 * head + 128)
        values = slice(384 + 128 * head, 512 + 128 * head)
        scores = [nt_dot(query[:, lanes], ref[:, lanes]) for ref in (kv_ref, other_ref)]
        top = jnp.max(jnp.maximum(scores[0], scores[1]), axis=-1, keepdims=True)
        weights = [jnp.exp2(score - top) for score in scores]
        total = jnp.sum(weights[0] + weights[1], axis=-1, keepdims=True)
        summed = nn_dot(weights[0].astype(bf16), kv_ref[:, values])
        summed += nn_dot(weights[1].astype(bf16), other_ref[:, values])
        summed = (summed / total).astype(bf16)
        rest = top + jnp.log(total) * LOG2E
        for part in range(3):
            piece = rest.astype(bf16).astype(f32)
            stats = jnp.where(lane == 3 * head + part, piece, stats)
            rest = rest - piece
        for i, out in enumerate(outs):
            out[:, lanes] = summed[32 * i : 32 * i + 32]
    for i, out in enumerate(outs):
        out[:, 384:] = stats[32 * i : 32 * i + 32].astype(bf16)
    split_copy.wait()


def coarse_attend(queries, kv, other, split):
    vmem, anywhere = pl.BlockSpec(memory_space=pltpu.VMEM), pl.BlockSpec(memory_space=pl.ANY)
    return pl.pallas_call(
        coarse_attend_kernel,
        in_specs=[vmem] * 6 + [anywhere],
        out_specs=[vmem] * 4 + [anywhere],
        out_shape=[jax.ShapeDtypeStruct((32, 512), bf16)] * 4 + [pltpu.VMEM(split.shape, bf16)],
        scratch_shapes=[pltpu.SemaphoreType.DMA((1,))],
        compiler_params=params(16),
        cost_estimate=cost(4 * 128 * 512 * 384, 1e6, 128 * 512 * 3),
        name="coarse_attend",
    )(*queries, kv, other, *in_hbm(split))


def coarse_combine_kernel(p0, p1, p2, p3, weight_ref, out_ref):
    parts = (p0, p1, p2, p3)
    heads = []
    for head in range(3):
        lanes = slice(128 * head, 128 * head + 128)
        logs = [
            jnp.sum(part[:, 384 + 3 * head : 387 + 3 * head].astype(f32), axis=-1, keepdims=True)
            for part in parts
        ]
        top = functools.reduce(jnp.maximum, logs)
        shares = [jnp.exp2(log - top) for log in logs]
        summed = sum(share * part[:, lanes].astype(f32) for share, part in zip(shares, parts))
        heads.append((summed / sum(shares)).astype(bf16))
    attended = jnp.concatenate(heads, axis=-1)
    out_ref[...] = nn_dot(attended, weight_ref[...]).astype(bf16)


def coarse_combine(parts, weight):
    return pl.pallas_call(
        coarse_combine_kernel,
        out_shape=jax.ShapeDtypeStruct((32, 1536), bf16),
        compiler_params=params(16),
        cost_estimate=cost(2 * 32 * 384 * 1536, 2e6),
        name="coarse_combine",
    )(*parts, weight)


def split_kernel(
    x_hbm, rows_hbm, coarse_ref, p0, p1, p2, p3, weight_ref, out_hbm,
    x_ref, rows_ref, out_ref, in_sems, out_sems,
):
    x_copy = pltpu.make_async_copy(x_hbm, x_ref, in_sems.at[2])
    x_copy.start()
    in_copies = [
        pltpu.make_async_copy(rows_hbm.at[pair], rows_ref.at[pair], in_sems.at[pair])
        for pair in (0, 1)
    ]
    for copy in in_copies:
        copy.start()
    mixed = (p0[...].astype(f32) + p1[...].astype(f32)) + (
        p2[...].astype(f32) + p3[...].astype(f32)
    )
    after = (coarse_ref[...].astype(f32) + mixed).astype(bf16)
    split = nt_dot(after, weight_ref[...])
    row = lax.broadcasted_iota(jnp.int32, (128, 32), 0)
    col = lax.broadcasted_iota(jnp.int32, (128, 32), 1)
    spread = jnp.where(col == (row >> 5) * 8 + ((row & 31) >> 2), 1.0, 0.0)
    grid = jnp.dot(spread, split, preferred_element_type=f32, precision=lax.Precision.HIGHEST)
    out_copies = []
    x_copy.wait()
    for pair, frames in enumerate(((1, 2), (0, 3))):
        in_copies[pair].wait()
        third = rows_ref[pair, 2 * TOKENS :, :].astype(f32)
        for at, frame in enumerate(frames):
            x = x_ref[frame].astype(f32)
            one = rows_ref[pair, TOKENS * at : TOKENS * (at + 1), :].astype(f32)
            two = pltpu.roll(third, 64, axis=1) if at else third
            for lanes, added in ((slice(0, 128), one), (slice(128, 192), two[:, :64])):
                hidden = (x[:, lanes] + added).astype(bf16).astype(f32)
                hidden = hidden.reshape(4, 4, COLS, -1) + grid[:, lanes].reshape(4, 1, COLS, -1)
                out_ref[frame, :, :, lanes] = hidden.reshape(ROWS, COLS, -1).astype(bf16)
            out_copies.append(
                pltpu.make_async_copy(out_ref.at[frame], out_hbm.at[frame], out_sems.at[frame])
            )
            out_copies[-1].start()
    for copy in out_copies:
        copy.wait()


def split_rows(x, rows, coarse, partials, weight):
    vmem, hbm = pl.BlockSpec(memory_space=pltpu.VMEM), pl.BlockSpec(memory_space=pltpu.HBM)
    return pl.pallas_call(
        split_kernel,
        in_specs=[hbm, hbm] + [vmem] * 6,
        out_specs=hbm,
        out_shape=jax.ShapeDtypeStruct((4, ROWS, COLS, 192), bf16),
        scratch_shapes=[
            pltpu.VMEM((4, TOKENS, 192), bf16),
            pltpu.VMEM((2, 3 * TOKENS, 128), bf16),
            pltpu.VMEM((4, ROWS, COLS, 192), bf16),
            pltpu.SemaphoreType.DMA((3,)),
            pltpu.SemaphoreType.DMA((4,)),
        ],
        compiler_params=params(24),
        cost_estimate=cost(2 * 32 * 1536 * 192, 4e6),
        name="split_rows",
    )(*in_hbm(x, rows), coarse, *partials, weight)


def shifted(value, axis, shift):
    return lax.ppermute(value, axis, [(i, (i + shift) % 4) for i in range(4)])


def from_others(value, axis):
    return [shifted(value, axis, shift) for shift in (1, 2, 3)]


def body(x, fine_gain, fine_qkv, fine_out, merge, coarse_gain, coarse_qkv, coarse_out, split):
    x = x.reshape(4, TOKENS, 768)
    groups = lax.axis_size(FRAMES)
    here = lax.axis_index(FRAMES)
    place = lax.axis_index("mp").astype(jnp.int32).reshape(1)
    edge = jnp.stack(
        [jnp.where(here == 0, 0.0, 1.0), jnp.where(here == groups - 1, 0.0, 1.0)]
    ).astype(f32)

    q, k, v, initial, final, frame_mean, own = fine_project(
        place, x, fine_gain, jnp.transpose(fine_qkv, (1, 2, 0))
    )
    first = lax.ppermute(final, FRAMES, [(i, i + 1) for i in range(groups - 1)])
    last = lax.ppermute(initial, FRAMES, [(i + 1, i) for i in range(groups - 1)])
    inner, mask, inner_mean, part, *weights = attend_inner(q, k, v, fine_out)
    products, partial = attend_outer(
        edge, mask, q, k, v, part, first, last, inner_mean, fine_out, *weights, inner
    )
    partials = from_others(partial, "mp")
    rows = lax.psum_scatter(products, "mp", scatter_dimension=0, tiled=True)
    frame_mean, merge, coarse_qkv, coarse_gain = load(
        partials[0], frame_mean, merge, jnp.transpose(coarse_qkv, (1, 0, 2)), coarse_gain
    )

    coarse, coarse_q, coarse_kv = coarse_project(
        [partial] + partials, frame_mean, merge, coarse_gain, coarse_qkv
    )
    coarse_kv = lax.all_to_all(coarse_kv, "z", 0, 0, tiled=True).reshape(256, 768)
    queries = [coarse_q] + from_others(coarse_q, "x")
    coarse_kv, queries = lax.optimization_barrier((coarse_kv, queries))
    other_kv = lax.ppermute(coarse_kv, "core", [(0, 1), (1, 0)])
    *parts, split = coarse_attend(queries, coarse_kv, other_kv, jnp.transpose(split, (1, 0)))
    parts = parts[:1] + [shifted(parts[s], "x", 4 - s) for s in (1, 2, 3)]
    coarse_partial = coarse_combine(parts, coarse_out)
    coarse_partials = [coarse_partial] + from_others(coarse_partial, "mp")
    return split_rows(
        own, rows.reshape(2, 3 * TOKENS, 128), coarse, coarse_partials, split
    )


def solution(mesh):
    parts = jax.sharding.Mesh(mesh.devices.reshape(4, 8, 2, 4), FRAMES + ("mp",))
    in_specs = (
        P(FRAMES, None, None, None),
        P(),
        P(None, None, "mp"),
        P("mp", None),
        P(),
        P(),
        P(None, None, "mp"),
        P("mp", None),
        P(None, "mp"),
    )
    out_specs = P(FRAMES, None, None, "mp")
    return jax.shard_map(body, mesh=parts, in_specs=in_specs, out_specs=out_specs, check_vma=False)
```

time: 120 us -> 115 us (0.958)
  Pallas kernels: 57.9 us -> 49.6 us
  waiting for transfers between devices: 13.6 us -> 18.7 us
  local copies, waits for them, and re-layouts: 2.76 us -> 0.01 us
    pallas_call x8 -> x6, Pallas kernels: 55.4 us -> 47.2 us  [the longest x1 18.8 us: attend_inner(): pl.pallas_call(inner_kernel, in_specs=[vmem] * 3 + [hbm], out_specs=[hbm]...]
    ppermute x12, waiting for transfers between devices: 7.15 us -> 11.2 us  [shifted(): return lax.ppermute(value, axis, [(i, (i + shift) % 4) for i in range(4)])]
    unnamed x18 -> x2, local copies, waits for them, and re-layouts: 2.76 us -> 0.01 us
    all_to_all x1, waiting for transfers between devices: 3.94 us -> 5.73 us  [body(): lax.all_to_all(coarse_kv, 'z', 0, 0, tiled=True).reshape(256, 768)]
  transfers between devices with their start and end apart: 18 -> 17, of which waited for: 7 -> 12; matrix products, arithmetic and copies ran while one was open for 0% -> 0% of each run, Pallas kernels for 47% -> 22%
where the time goes in v2:
time: 115 us; the launch traced here: 114 us
  Pallas kernels  49.6 us (43%)
  starting transfers between devices  32 us (28%)
  waiting for transfers between devices  18.7 us (16%)
  between operations  13.5 us (12%)
    pallas_call x1, Pallas kernels, attend_inner(): pl.pallas_call(inner_kernel, in_specs=[vmem] * 3 + [hbm], out_specs=[hbm]...  18.8 us
    ppermute x12, starting transfers between devices, shifted(): return lax.ppermute(value, axis, [(i, (i + shift) % 4) for i in range(4)])  16.7 us
    pallas_call x1, Pallas kernels, attend_outer(): pl.pallas_call(outer_kernel, in_specs=[pl.BlockSpec(memory_space=pltpu.SM...  15 us
    ppermute x12, waiting for transfers between devices, shifted(): return lax.ppermute(value, axis, [(i, (i + shift) % 4) for i in range(4)])  11.2 us
    ppermute x1, starting transfers between devices, body(): lax.ppermute(initial, FRAMES, [(i + 1, i) for i in range(groups - 1)])  7.47 us
    pallas_call x1, Pallas kernels, fine_project(): pl.pallas_call(fine_project_kernel, in_specs=[pl.BlockSpec(memory_space=p...  6.8 us
    all_to_all x1, starting transfers between devices, body(): lax.all_to_all(coarse_kv, 'z', 0, 0, tiled=True).reshape(256, 768)  5.87 us
    all_to_all x1, waiting for transfers between devices, body(): lax.all_to_all(coarse_kv, 'z', 0, 0, tiled=True).reshape(256, 768)  5.73 us
  transfers between devices with their start and end apart: 17, of which 12 were waited for; matrix products, arithmetic and copies ran while one was open for 0% of the time, Pallas kernels for 22%

profile of v2, /device:TPU:6, one launch (start us, length us, event | category | flops | bytes accessed | tf_op | source)
XLA Modules:
  0.0 113.9 jit_solution(16557090866559069043)
XLA Ops:
  6.5 6.8 %fine_project.1 = (bf16[4,512,192]{2,1,0:T(8,128)(2,1)S(1)}, bf16[4,192,512]{2,1,0:T(8,128)(2,1)S(1)}, bf16[4,512,256]{2,1,0:T(8,128)(2,1)S(1)}, bf16[512,384]{1...) custom-call(s32[1]{0:T(128)} %bitcast.place_ref, ...), custom_call_target="tpu_custom_call" | custom-call | flops 2415919104 | bytes 8000000 | tf_op jit(solution)/shard_map/fine_project/pallas_call | solution.py:125
  13.3 1.9 %collective-permute-start = (bf16[512,384]{1,0:T(8,128)(2,1)}, bf16[512,384]{1,0:T(8,128)(2,1)S(1)}, u32[]{:S(2)}, u32[]{:S(2)}) collective-permute-start(bf16[512,384]{1,0:T(8,128)(2,1)} %get-tuple-element.43), channel_id=1, source_target_pairs={{0,4},{4,8},{8,12},{12,16},{16,20},{20,24},{24,28},{28,32},{32,36}... | collective-permute-start | bytes 1179656 | tf_op jit(solution)/shard_map/ppermute | solution.py:663
  15.3 7.5 %collective-permute-start.1 = (bf16[512,384]{1,0:T(8,128)(2,1)}, bf16[512,384]{1,0:T(8,128)(2,1)}, u32[]{:S(2)}, u32[]{:S(2)}) collective-permute-start(bf16[512,384]{1,0:T(8,128)(2,1)} %get-tuple-element.44), channel_id=1, source_target_pairs={{4,0},{8,4},{12,8},{16,12},{20,16},{24,20},{28,24},{32,28},{36,32}... | collective-permute-start | bytes 1179656 | tf_op jit(solution)/shard_map/ppermute | solution.py:664
  22.8 18.8 %attend_inner.1 = (bf16[4,2,1536,128]{3,2,1,0:T(8,128)(2,1)}, bf16[4,128,384]{2,1,0:T(8,128)(2,1)S(1)}, f32[32,256]{1,0:T(8,128)S(1)}, f32[2,512,384]{2,1,0:T(8,...) custom-call(bf16[4,512,192]{2,1,0:T(8,128)(2,1)S(1)} %get-tuple-element.38.q_ref, ...), custom_call_target="tpu_custom_call" | custom-call | flops 2516582400 | bytes 6000000 | tf_op jit(solution)/shard_map/attend_inner/pallas_call | solution.py:402
  41.7 15.0 %attend_outer.1 = (bf16[4,2,1536,128]{3,2,1,0:T(8,128)(2,1)}, bf16[32,768]{1,0:T(8,128)(2,1)S(1)}) custom-call(f32[2]{0:T(128)S(1)} %pad_maximum_fusion.edge_ref, bf16[4,128,384]{2,1,0:T(8,128)(2,1)S(1)} %get-tuple-element.41.mask_ref, bf16[4,512,192]{2,1,0:T(8,128)(2,1)S(1)} %get-tuple-element.38.q_ref, ...), custom_call_target="tpu_custom_call", output_to_operand_aliasing={{0}: (12, {})} | custom-call | flops 503316480 | bytes 6000000 | tf_op jit(solution)/shard_map/attend_outer/pallas_call | solution.py:425
  56.7 1.9 %collective-permute-start.2 = (bf16[32,768]{1,0:T(8,128)(2,1)S(1)}, bf16[32,768]{1,0:T(8,128)(2,1)S(1)}, u32[]{:S(2)}, u32[]{:S(2)}) collective-permute-start(bf16[32,768]{1,0:T(8,128)(2,1)S(1)} %get-tuple-element.50.p0), channel_id=1, source_target_pairs={{0,1},{1,2},{2,3},{3,0},{4,5},{5,6},{6,7},{7,4},{8,9},{9,10},{10,1... | collective-permute-start | bytes 147464 | tf_op jit(solution)/shard_map/ppermute | solution.py:644
  58.6 1.5 %collective-permute-start.4 = (bf16[32,768]{1,0:T(8,128)(2,1)S(1)}, bf16[32,768]{1,0:T(8,128)(2,1)S(1)}, u32[]{:S(2)}, u32[]{:S(2)}) collective-permute-start(bf16[32,768]{1,0:T(8,128)(2,1)S(1)} %get-tuple-element.50.p0), channel_id=1, source_target_pairs={{0,3},{1,0},{2,1},{3,2},{4,7},{5,4},{6,5},{7,6},{8,11},{9,8},{10,9... | collective-permute-start | bytes 147464 | tf_op jit(solution)/shard_map/ppermute | solution.py:644
  60.1 1.8 %collective-permute-start.3 = (bf16[32,768]{1,0:T(8,128)(2,1)S(1)}, bf16[32,768]{1,0:T(8,128)(2,1)S(1)}, u32[]{:S(2)}, u32[]{:S(2)}) collective-permute-start(bf16[32,768]{1,0:T(8,128)(2,1)S(1)} %get-tuple-element.50.p0), channel_id=1, source_target_pairs={{0,2},{1,3},{2,0},{3,1},{4,6},{5,7},{6,4},{7,5},{8,10},{9,11},{10,... | collective-permute-start | bytes 147464 | tf_op jit(solution)/shard_map/ppermute | solution.py:644
  62.1 2.8 %load.1 = (f32[32,768]{1,0:T(8,128)S(1)}, bf16[768,1536]{1,0:T(8,128)(2,1)S(1)}, bf16[3,1536,384]{2,1,0:T(8,128)(2,1)S(1)}, f32[1536]{0:T(1024)S(1)}) custom-call(bf16[32,768]{1,0:T(8,128)(2,1)S(1)} %collective-permute-done.2._.p1, f32[32,768]{1,0:T(8,128)} %get-tuple-element.51.refs_0_, bf16[768,1536]{1,0:T(8,128)(2,1)} %refs_1_.1, ...), custom_call_target="tpu_custom_call" | custom-call | bytes 6000000 | tf_op jit(solution)/shard_map/load/pallas_call | solution.py:462
  65.7 2.0 %coarse_project.1 = (bf16[32,1536]{1,0:T(8,128)(2,1)S(1)}, bf16[32,384]{1,0:T(8,128)(2,1)S(1)}, bf16[8,32,768]{2,1,0:T(8,128)(2,1)}) custom-call(bf16[32,768]{1,0:T(8,128)(2,1)S(1)} %get-tuple-element.50.p0, bf16[32,768]{1,0:T(8,128)(2,1)S(1)} %collective-permute-done.2._.p1, bf16[32,768]{1,0:T(8,128)(2,1)S(1)} %collective-permute-done.3.p2, ...), custom_call_target="tpu_custom_call" | custom-call | flops 188743680 | bytes 7000000 | tf_op jit(solution)/shard_map/coarse_project/pallas_call | solution.py:494
  67.7 5.9 %all-to-all-start = ((bf16[8,32,768]{2,1,0:T(8,128)(2,1)}), bf16[8,32,768]{2,1,0:T(8,128)(2,1)S(1)}, u32[]{:S(2)}, u32[]{:S(2)}) async-start(bf16[8,32,768]{2,1,0:T(8,128)(2,1)} %get-tuple-element.57), calls=%async_computation.1 | async-start | bytes 786432 | tf_op jit(solution)/shard_map/all_to_all | solution.py:678
  74.4 1.1 collective-permute-start.6
  75.4 2.1 %collective-permute-start.5 = (bf16[32,384]{1,0:T(8,128)(2,1)S(1)}, bf16[32,384]{1,0:T(8,128)(2,1)S(1)}, u32[]{:S(2)}, u32[]{:S(2)}) collective-permute-start(bf16[32,384]{1,0:T(8,128)(2,1)S(1)} %get-tuple-element.59.q0), channel_id=1, source_target_pairs={{0,64},{64,128},{128,192},{192,0},{1,65},{65,129},{129,193},{193,1... | collective-permute-start | bytes 73736 | tf_op jit(solution)/shard_map/ppermute | solution.py:644
  77.5 1.1 collective-permute-done.7.q3
  78.6 1.1 collective-permute-done.6.q2
  79.7 5.7 %all-to-all-done = bf16[8,32,768]{2,1,0:T(8,128)(2,1)S(1)} async-done(((bf16[8,32,768]{2,1,0:T(8,128)(2,1)}), bf16[8,32,768]{2,1,0:T(8,128)(2,1)S(1)}, u32[]{:S(2)}, u32[]{:S(2)}) %all-to-all-start) | async-done | bytes 393248 | tf_op jit(solution)/shard_map/all_to_all | solution.py:678
  85.5 1.7 %collective-permute-done.8.other_ref = bf16[256,768]{1,0:T(8,128)(2,1)S(1)} collective-permute-done((bf16[256,768]{1,0:T(8,128)(2,1)S(1)}, bf16[256,768]{1,0:T(8,128)(2,1)S(1)}, u32[]{:S(2)}, u32[]{:S(2)}) %collective-permute-start.8) | collective-permute-done | bytes 393248 | tf_op jit(solution)/shard_map/ppermute | solution.py:681
  87.2 1.1 coarse_attend.1
  90.2 2.1 %collective-permute-start.11 = (bf16[32,512]{1,0:T(8,128)(2,1)S(1)}, bf16[32,512]{1,0:T(8,128)(2,1)S(1)}, u32[]{:S(2)}, u32[]{:S(2)}) collective-permute-start(bf16[32,512]{1,0:T(8,128)(2,1)S(1)} %get-tuple-element.67), channel_id=1, source_target_pairs={{0,64},{64,128},{128,192},{192,0},{1,65},{65,129},{129,193},{193,1... | collective-permute-start | bytes 98312 | tf_op jit(solution)/shard_map/ppermute | solution.py:644
  92.3 1.5 %collective-permute-done.9.p1 = bf16[32,512]{1,0:T(8,128)(2,1)S(1)} collective-permute-done((bf16[32,512]{1,0:T(8,128)(2,1)S(1)}, bf16[32,512]{1,0:T(8,128)(2,1)S(1)}, u32[]{:S(2)}, u32[]{:S(2)}) %collective-permute-start.9) | collective-permute-done | bytes 32800 | tf_op jit(solution)/shard_map/ppermute | solution.py:644
  95.2 2.0 %collective-permute-start.14 = (bf16[32,1536]{1,0:T(8,128)(2,1)S(1)}, bf16[32,1536]{1,0:T(8,128)(2,1)S(1)}, u32[]{:S(2)}, u32[]{:S(2)}) collective-permute-start(bf16[32,1536]{1,0:T(8,128)(2,1)S(1)} %coarse_combine.1.p0), channel_id=1, source_target_pairs={{0,3},{1,0},{2,1},{3,2},{4,7},{5,4},{6,5},{7,6},{8,11},{9,8},{10,9... | collective-permute-start | bytes 294920 | tf_op jit(solution)/shard_map/ppermute | solution.py:644
  98.6 2.0 %collective-permute-done.14.p3 = bf16[32,1536]{1,0:T(8,128)(2,1)S(1)} collective-permute-done((bf16[32,1536]{1,0:T(8,128)(2,1)S(1)}, bf16[32,1536]{1,0:T(8,128)(2,1)S(1)}, u32[]{:S(2)}, u32[]{:S(2)}) %collective-permute-start.14) | collective-permute-done | bytes 98336 | tf_op jit(solution)/shard_map/ppermute | solution.py:644
  100.6 2.7 %collective-permute-done.13.p2 = bf16[32,1536]{1,0:T(8,128)(2,1)S(1)} collective-permute-done((bf16[32,1536]{1,0:T(8,128)(2,1)S(1)}, bf16[32,1536]{1,0:T(8,128)(2,1)S(1)}, u32[]{:S(2)}, u32[]{:S(2)}) %collective-permute-start.13) | collective-permute-done | bytes 98336 | tf_op jit(solution)/shard_map/ppermute | solution.py:644
  104.3 2.7 %split_rows.1 = bf16[4,16,32,192]{3,2,1,0:T(8,128)(2,1)} custom-call(bf16[4,512,192]{2,1,0:T(8,128)(2,1)} %get-tuple-element.37.x_hbm, bf16[2,1536,128]{2,1,0:T(8,128)(2,1)} %bitcast.12, bf16[32,1536]{1,0:T(8,128)(2,1)S(1)} %get-tuple-element.56.coarse_ref, bf16[32,1536]{1,0:T(8,128)(2,1)S(1)} %coarse_combine.1.p0, ...), custom_call_target="tpu_custom_call" | custom-call | flops 18874368 | bytes 4000000 | tf_op jit(solution)/shard_map/split_rows/pallas_call | solution.py:625
  (22 shorter events, 7.6 us)
Async XLA Ops:
  6.5 97.8 %reduce-scatter.2.cloned.1.call-start = ((), (), s32[]{:S(2)}) async-start(), calls=%async_computation.2 | async-start | bytes 3932160 | tf_op jit(solution)/shard_map/reduce_scatter | solution.py:670
  13.3 28.3 %collective-permute-start = (bf16[512,384]{1,0:T(8,128)(2,1)}, bf16[512,384]{1,0:T(8,128)(2,1)S(1)}, u32[]{:S(2)}, u32[]{:S(2)}) collective-permute-start(bf16[512,384]{1,0:T(8,128)(2,1)} %get-tuple-element.43), channel_id=1, source_target_pairs={{0,4},{4,8},{8,12},{12,16},{16,20},{20,24},{24,28},{28,32},{32,36}... | collective-permute-start | bytes 1179656 | tf_op jit(solution)/shard_map/ppermute | solution.py:663
  15.3 26.4 %collective-permute-start.1 = (bf16[512,384]{1,0:T(8,128)(2,1)}, bf16[512,384]{1,0:T(8,128)(2,1)}, u32[]{:S(2)}, u32[]{:S(2)}) collective-permute-start(bf16[512,384]{1,0:T(8,128)(2,1)} %get-tuple-element.44), channel_id=1, source_target_pairs={{4,0},{8,4},{12,8},{16,12},{20,16},{24,20},{28,24},{32,28},{36,32}... | collective-permute-start | bytes 1179656 | tf_op jit(solution)/shard_map/ppermute | solution.py:664
  56.7 5.4 %collective-permute-start.2 = (bf16[32,768]{1,0:T(8,128)(2,1)S(1)}, bf16[32,768]{1,0:T(8,128)(2,1)S(1)}, u32[]{:S(2)}, u32[]{:S(2)}) collective-permute-start(bf16[32,768]{1,0:T(8,128)(2,1)S(1)} %get-tuple-element.50.p0), channel_id=1, source_target_pairs={{0,1},{1,2},{2,3},{3,0},{4,5},{5,6},{6,7},{7,4},{8,9},{9,10},{10,1... | collective-permute-start | bytes 147464 | tf_op jit(solution)/shard_map/ppermute | solution.py:644
  58.6 6.3 %collective-permute-start.4 = (bf16[32,768]{1,0:T(8,128)(2,1)S(1)}, bf16[32,768]{1,0:T(8,128)(2,1)S(1)}, u32[]{:S(2)}, u32[]{:S(2)}) collective-permute-start(bf16[32,768]{1,0:T(8,128)(2,1)S(1)} %get-tuple-element.50.p0), channel_id=1, source_target_pairs={{0,3},{1,0},{2,1},{3,2},{4,7},{5,4},{6,5},{7,6},{8,11},{9,8},{10,9... | collective-permute-start | bytes 147464 | tf_op jit(solution)/shard_map/ppermute | solution.py:644
  60.1 5.6 %collective-permute-start.3 = (bf16[32,768]{1,0:T(8,128)(2,1)S(1)}, bf16[32,768]{1,0:T(8,128)(2,1)S(1)}, u32[]{:S(2)}, u32[]{:S(2)}) collective-permute-start(bf16[32,768]{1,0:T(8,128)(2,1)S(1)} %get-tuple-element.50.p0), channel_id=1, source_target_pairs={{0,2},{1,3},{2,0},{3,1},{4,6},{5,7},{6,4},{7,5},{8,10},{9,11},{10,... | collective-permute-start | bytes 147464 | tf_op jit(solution)/shard_map/ppermute | solution.py:644
  65.7 29.0 %copy-start = (bf16[384,1536]{1,0:T(8,128)(2,1)S(1)}, bf16[384,1536]{1,0:T(8,128)(2,1)}, u32[]{:S(2)}) copy-start(bf16[384,1536]{1,0:T(8,128)(2,1)} %weight_ref.1) | copy-start | bytes 3538948
  67.7 17.8 %all-to-all-start = ((bf16[8,32,768]{2,1,0:T(8,128)(2,1)}), bf16[8,32,768]{2,1,0:T(8,128)(2,1)S(1)}, u32[]{:S(2)}, u32[]{:S(2)}) async-start(bf16[8,32,768]{2,1,0:T(8,128)(2,1)} %get-tuple-element.57), calls=%async_computation.1 | async-start | bytes 786432 | tf_op jit(solution)/shard_map/all_to_all | solution.py:678
  73.6 5.0 %collective-permute-start.7 = (bf16[32,384]{1,0:T(8,128)(2,1)S(1)}, bf16[32,384]{1,0:T(8,128)(2,1)S(1)}, u32[]{:S(2)}, u32[]{:S(2)}) collective-permute-start(bf16[32,384]{1,0:T(8,128)(2,1)S(1)} %get-tuple-element.59.q0), channel_id=1, source_target_pairs={{0,192},{64,0},{128,64},{192,128},{1,193},{65,1},{129,65},{193,129... | collective-permute-start | bytes 73736 | tf_op jit(solution)/shard_map/ppermute | solution.py:644
  74.4 5.3 %collective-permute-start.6 = (bf16[32,384]{1,0:T(8,128)(2,1)S(1)}, bf16[32,384]{1,0:T(8,128)(2,1)S(1)}, u32[]{:S(2)}, u32[]{:S(2)}) collective-permute-start(bf16[32,384]{1,0:T(8,128)(2,1)S(1)} %get-tuple-element.59.q0), channel_id=1, source_target_pairs={{0,128},{64,192},{128,0},{192,64},{1,129},{65,193},{129,1},{193,65... | collective-permute-start | bytes 73736 | tf_op jit(solution)/shard_map/ppermute | solution.py:644
  75.4 4.3 %collective-permute-start.5 = (bf16[32,384]{1,0:T(8,128)(2,1)S(1)}, bf16[32,384]{1,0:T(8,128)(2,1)S(1)}, u32[]{:S(2)}, u32[]{:S(2)}) collective-permute-start(bf16[32,384]{1,0:T(8,128)(2,1)S(1)} %get-tuple-element.59.q0), channel_id=1, source_target_pairs={{0,64},{64,128},{128,192},{192,0},{1,65},{65,129},{129,193},{193,1... | collective-permute-start | bytes 73736 | tf_op jit(solution)/shard_map/ppermute | solution.py:644
  85.4 1.7 %collective-permute-start.8 = (bf16[256,768]{1,0:T(8,128)(2,1)S(1)}, bf16[256,768]{1,0:T(8,128)(2,1)S(1)}, u32[]{:S(2)}, u32[]{:S(2)}) collective-permute-start(bf16[256,768]{1,0:T(8,128)(2,1)S(1)} %bitcast.9), channel_id=1, source_target_pairs={{0,4},{4,0},{1,5},{5,1},{2,6},{6,2},{3,7},{7,3},{8,12},{12,8},{9,1... | collective-permute-start | bytes 1179656 | tf_op jit(solution)/shard_map/ppermute | solution.py:681
  88.3 5.6 %collective-permute-start.9 = (bf16[32,512]{1,0:T(8,128)(2,1)S(1)}, bf16[32,512]{1,0:T(8,128)(2,1)S(1)}, u32[]{:S(2)}, u32[]{:S(2)}) collective-permute-start(bf16[32,512]{1,0:T(8,128)(2,1)S(1)} %get-tuple-element.65), channel_id=1, source_target_pairs={{0,192},{64,0},{128,64},{192,128},{1,193},{65,1},{129,65},{193,129... | collective-permute-start | bytes 98312 | tf_op jit(solution)/shard_map/ppermute | solution.py:644
  89.2 5.4 %collective-permute-start.10 = (bf16[32,512]{1,0:T(8,128)(2,1)S(1)}, bf16[32,512]{1,0:T(8,128)(2,1)S(1)}, u32[]{:S(2)}, u32[]{:S(2)}) collective-permute-start(bf16[32,512]{1,0:T(8,128)(2,1)S(1)} %get-tuple-element.66), channel_id=1, source_target_pairs={{0,128},{64,192},{128,0},{192,64},{1,129},{65,193},{129,1},{193,65... | collective-permute-start | bytes 98312 | tf_op jit(solution)/shard_map/ppermute | solution.py:644
  90.2 4.5 %collective-permute-start.11 = (bf16[32,512]{1,0:T(8,128)(2,1)S(1)}, bf16[32,512]{1,0:T(8,128)(2,1)S(1)}, u32[]{:S(2)}, u32[]{:S(2)}) collective-permute-start(bf16[32,512]{1,0:T(8,128)(2,1)S(1)} %get-tuple-element.67), channel_id=1, source_target_pairs={{0,64},{64,128},{128,192},{192,0},{1,65},{65,129},{129,193},{193,1... | collective-permute-start | bytes 98312 | tf_op jit(solution)/shard_map/ppermute | solution.py:644
  95.2 5.5 %collective-permute-start.14 = (bf16[32,1536]{1,0:T(8,128)(2,1)S(1)}, bf16[32,1536]{1,0:T(8,128)(2,1)S(1)}, u32[]{:S(2)}, u32[]{:S(2)}) collective-permute-start(bf16[32,1536]{1,0:T(8,128)(2,1)S(1)} %coarse_combine.1.p0), channel_id=1, source_target_pairs={{0,3},{1,0},{2,1},{3,2},{4,7},{5,4},{6,5},{7,6},{8,11},{9,8},{10,9... | collective-permute-start | bytes 294920 | tf_op jit(solution)/shard_map/ppermute | solution.py:644
  97.2 6.2 %collective-permute-start.13 = (bf16[32,1536]{1,0:T(8,128)(2,1)S(1)}, bf16[32,1536]{1,0:T(8,128)(2,1)S(1)}, u32[]{:S(2)}, u32[]{:S(2)}) collective-permute-start(bf16[32,1536]{1,0:T(8,128)(2,1)S(1)} %coarse_combine.1.p0), channel_id=1, source_target_pairs={{0,2},{1,3},{2,0},{3,1},{4,6},{5,7},{6,4},{7,5},{8,10},{9,11},{10,... | collective-permute-start | bytes 294920 | tf_op jit(solution)/shard_map/ppermute | solution.py:644
  97.8 6.5 %collective-permute-start.12 = (bf16[32,1536]{1,0:T(8,128)(2,1)S(1)}, bf16[32,1536]{1,0:T(8,128)(2,1)S(1)}, u32[]{:S(2)}, u32[]{:S(2)}) collective-permute-start(bf16[32,1536]{1,0:T(8,128)(2,1)S(1)} %coarse_combine.1.p0), channel_id=1, source_target_pairs={{0,1},{1,2},{2,3},{3,0},{4,5},{5,6},{6,7},{7,4},{8,9},{9,10},{10,1... | collective-permute-start | bytes 294920 | tf_op jit(solution)/shard_map/ppermute | solution.py:644
Sparse Core Ops, SparseCore 0:
  56.8 41.2 reduce-scatter.1

commit v3 on v2

--- a/solution.py
+++ b/solution.py
@@ -13,7 +13,7 @@
 LOG2E = 1.4426950408889634
 ROWS, COLS = 16, 32
 TOKENS = ROWS * COLS
-FRAMES = ("x", "z", "core")
+FRAMES = ("x", "far", "near", "core")
 MIB = 1 << 20
 bf16, f32 = jnp.bfloat16, jnp.float32
 
@@ -675,12 +675,12 @@
     coarse, coarse_q, coarse_kv = coarse_project(
         [partial] + partials, frame_mean, merge, coarse_gain, coarse_qkv
     )
-    coarse_kv = lax.all_to_all(coarse_kv, "z", 0, 0, tiled=True).reshape(256, 768)
-    queries = [coarse_q] + from_others(coarse_q, "x")
+    coarse_kv = lax.all_to_all(coarse_kv, ("x", "near"), 0, 0, tiled=True).reshape(256, 768)
+    queries = [coarse_q] + from_others(coarse_q, "far")
     coarse_kv, queries = lax.optimization_barrier((coarse_kv, queries))
     other_kv = lax.ppermute(coarse_kv, "core", [(0, 1), (1, 0)])
     *parts, split = coarse_attend(queries, coarse_kv, other_kv, jnp.transpose(split, (1, 0)))
-    parts = parts[:1] + [shifted(parts[s], "x", 4 - s) for s in (1, 2, 3)]
+    parts = parts[:1] + [shifted(parts[s], "far", 4 - s) for s in (1, 2, 3)]
     coarse_partial = coarse_combine(parts, coarse_out)
     coarse_partials = [coarse_partial] + from_others(coarse_partial, "mp")
     return split_rows(
@@ -689,7 +689,7 @@
 
 
 def solution(mesh):
-    parts = jax.sharding.Mesh(mesh.devices.reshape(4, 8, 2, 4), FRAMES + ("mp",))
+    parts = jax.sharding.Mesh(mesh.devices.reshape(4, 4, 2, 2, 4), FRAMES + ("mp",))
     in_specs = (
         P(FRAMES, None, None, None),
         P(),

time: 115 us -> 117 us (1.017)
  starting transfers between devices: 32 us -> 37 us
  waiting for transfers between devices: 18.7 us -> 16.2 us
    ppermute x12, starting transfers between devices: 16.7 us -> 23.1 us  [shifted(): return lax.ppermute(value, axis, [(i, (i + shift) % 4) for i in range(4)])]
    all_to_all x1, waiting for transfers between devices: 5.73 us -> 0.01 us  [body(): lax.all_to_all(coarse_kv, ('x', 'near'), 0, 0, tiled=True).reshape(256, 768)]
    ppermute x12, waiting for transfers between devices: 11.2 us -> 14.5 us  [shifted(): return lax.ppermute(value, axis, [(i, (i + shift) % 4) for i in range(4)])]
    all_to_all x1, starting transfers between devices: 5.87 us -> 4.51 us  [body(): lax.all_to_all(coarse_kv, ('x', 'near'), 0, 0, tiled=True).reshape(256, 768)]
  transfers between devices with their start and end apart: 17 -> 17, of which waited for: 12 -> 10; matrix products, arithmetic and copies ran while one was open for 0% -> 0% of each run, Pallas kernels for 22% -> 22%
where the time goes in v3:
time: 117 us
  Pallas kernels  49.6 us (42%)
  starting transfers between devices  37 us (32%)
  waiting for transfers between devices  16.2 us (14%)
  between operations  13.5 us (12%)
    ppermute x12, starting transfers between devices, shifted(): return lax.ppermute(value, axis, [(i, (i + shift) % 4) for i in range(4)])  23.1 us
    pallas_call x1, Pallas kernels, attend_inner(): pl.pallas_call(inner_kernel, in_specs=[vmem] * 3 + [hbm], out_specs=[hbm]...  18.8 us
    pallas_call x1, Pallas kernels, attend_outer(): pl.pallas_call(outer_kernel, in_specs=[pl.BlockSpec(memory_space=pltpu.SM...  15 us
    ppermute x12, waiting for transfers between devices, shifted(): return lax.ppermute(value, axis, [(i, (i + shift) % 4) for i in range(4)])  14.5 us
    ppermute x1, starting transfers between devices, body(): lax.ppermute(initial, FRAMES, [(i + 1, i) for i in range(groups - 1)])  7.47 us
    pallas_call x1, Pallas kernels, fine_project(): pl.pallas_call(fine_project_kernel, in_specs=[pl.BlockSpec(memory_space=p...  6.8 us
    all_to_all x1, starting transfers between devices, body(): lax.all_to_all(coarse_kv, ('x', 'near'), 0, 0, tiled=True).reshape(256, 768)  4.51 us
    pallas_call x1, Pallas kernels, load(): pl.pallas_call(load_kernel, in_specs=[anywhere] * 5, out_specs=[anywhere]...  2.81 us
  transfers between devices with their start and end apart: 17, of which 10 were waited for; matrix products, arithmetic and copies ran while one was open for 0% of the time, Pallas kernels for 22%

profile of v3, /device:TPU:6, one launch (start us, length us, event | category | flops | bytes accessed | tf_op | source)
XLA Modules:
  0.0 116.5 jit_solution(14636772822494012440)
XLA Ops:
  6.5 6.8 %fine_project.1 = (bf16[4,512,192]{2,1,0:T(8,128)(2,1)S(1)}, bf16[4,192,512]{2,1,0:T(8,128)(2,1)S(1)}, bf16[4,512,256]{2,1,0:T(8,128)(2,1)S(1)}, bf16[512,384]{1...) custom-call(s32[1]{0:T(128)} %bitcast.place_ref, ...), custom_call_target="tpu_custom_call" | custom-call | flops 2415919104 | bytes 8000000 | tf_op jit(solution)/shard_map/fine_project/pallas_call | solution.py:125
  13.3 1.9 %collective-permute-start = (bf16[512,384]{1,0:T(8,128)(2,1)}, bf16[512,384]{1,0:T(8,128)(2,1)S(1)}, u32[]{:S(2)}, u32[]{:S(2)}) collective-permute-start(bf16[512,384]{1,0:T(8,128)(2,1)} %get-tuple-element.43), channel_id=1, source_target_pairs={{0,4},{4,8},{8,12},{12,16},{16,20},{20,24},{24,28},{28,32},{32,36}... | collective-permute-start | bytes 1179656 | tf_op jit(solution)/shard_map/ppermute | solution.py:663
  15.3 7.5 %collective-permute-start.1 = (bf16[512,384]{1,0:T(8,128)(2,1)}, bf16[512,384]{1,0:T(8,128)(2,1)}, u32[]{:S(2)}, u32[]{:S(2)}) collective-permute-start(bf16[512,384]{1,0:T(8,128)(2,1)} %get-tuple-element.44), channel_id=1, source_target_pairs={{4,0},{8,4},{12,8},{16,12},{20,16},{24,20},{28,24},{32,28},{36,32}... | collective-permute-start | bytes 1179656 | tf_op jit(solution)/shard_map/ppermute | solution.py:664
  22.9 18.8 %attend_inner.1 = (bf16[4,2,1536,128]{3,2,1,0:T(8,128)(2,1)}, bf16[4,128,384]{2,1,0:T(8,128)(2,1)S(1)}, f32[32,256]{1,0:T(8,128)S(1)}, f32[2,512,384]{2,1,0:T(8,...) custom-call(bf16[4,512,192]{2,1,0:T(8,128)(2,1)S(1)} %get-tuple-element.38.q_ref, ...), custom_call_target="tpu_custom_call" | custom-call | flops 2516582400 | bytes 6000000 | tf_op jit(solution)/shard_map/attend_inner/pallas_call | solution.py:402
  41.7 15.0 %attend_outer.1 = (bf16[4,2,1536,128]{3,2,1,0:T(8,128)(2,1)}, bf16[32,768]{1,0:T(8,128)(2,1)S(1)}) custom-call(f32[2]{0:T(128)S(1)} %pad_maximum_fusion.edge_ref, bf16[4,128,384]{2,1,0:T(8,128)(2,1)S(1)} %get-tuple-element.41.mask_ref, bf16[4,512,192]{2,1,0:T(8,128)(2,1)S(1)} %get-tuple-element.38.q_ref, ...), custom_call_target="tpu_custom_call", output_to_operand_aliasing={{0}: (12, {})} | custom-call | flops 503316480 | bytes 6000000 | tf_op jit(solution)/shard_map/attend_outer/pallas_call | solution.py:425
  56.7 1.9 %collective-permute-start.2 = (bf16[32,768]{1,0:T(8,128)(2,1)S(1)}, bf16[32,768]{1,0:T(8,128)(2,1)S(1)}, u32[]{:S(2)}, u32[]{:S(2)}) collective-permute-start(bf16[32,768]{1,0:T(8,128)(2,1)S(1)} %get-tuple-element.50.p0), channel_id=1, source_target_pairs={{0,1},{1,2},{2,3},{3,0},{4,5},{5,6},{6,7},{7,4},{8,9},{9,10},{10,1... | collective-permute-start | bytes 147464 | tf_op jit(solution)/shard_map/ppermute | solution.py:644
  58.6 1.5 %collective-permute-start.4 = (bf16[32,768]{1,0:T(8,128)(2,1)S(1)}, bf16[32,768]{1,0:T(8,128)(2,1)S(1)}, u32[]{:S(2)}, u32[]{:S(2)}) collective-permute-start(bf16[32,768]{1,0:T(8,128)(2,1)S(1)} %get-tuple-element.50.p0), channel_id=1, source_target_pairs={{0,3},{1,0},{2,1},{3,2},{4,7},{5,4},{6,5},{7,6},{8,11},{9,8},{10,9... | collective-permute-start | bytes 147464 | tf_op jit(solution)/shard_map/ppermute | solution.py:644
  60.1 1.8 %collective-permute-start.3 = (bf16[32,768]{1,0:T(8,128)(2,1)S(1)}, bf16[32,768]{1,0:T(8,128)(2,1)S(1)}, u32[]{:S(2)}, u32[]{:S(2)}) collective-permute-start(bf16[32,768]{1,0:T(8,128)(2,1)S(1)} %get-tuple-element.50.p0), channel_id=1, source_target_pairs={{0,2},{1,3},{2,0},{3,1},{4,6},{5,7},{6,4},{7,5},{8,10},{9,11},{10,... | collective-permute-start | bytes 147464 | tf_op jit(solution)/shard_map/ppermute | solution.py:644
  62.1 2.8 %load.1 = (f32[32,768]{1,0:T(8,128)S(1)}, bf16[768,1536]{1,0:T(8,128)(2,1)S(1)}, bf16[3,1536,384]{2,1,0:T(8,128)(2,1)S(1)}, f32[1536]{0:T(1024)S(1)}) custom-call(bf16[32,768]{1,0:T(8,128)(2,1)S(1)} %collective-permute-done.2._.p1, f32[32,768]{1,0:T(8,128)} %get-tuple-element.51.refs_0_, bf16[768,1536]{1,0:T(8,128)(2,1)} %refs_1_.1, ...), custom_call_target="tpu_custom_call" | custom-call | bytes 6000000 | tf_op jit(solution)/shard_map/load/pallas_call | solution.py:462
  65.7 2.0 %coarse_project.1 = (bf16[32,1536]{1,0:T(8,128)(2,1)S(1)}, bf16[32,384]{1,0:T(8,128)(2,1)S(1)}, bf16[8,32,768]{2,1,0:T(8,128)(2,1)}) custom-call(bf16[32,768]{1,0:T(8,128)(2,1)S(1)} %get-tuple-element.50.p0, bf16[32,768]{1,0:T(8,128)(2,1)S(1)} %collective-permute-done.2._.p1, bf16[32,768]{1,0:T(8,128)(2,1)S(1)} %collective-permute-done.3.p2, ...), custom_call_target="tpu_custom_call" | custom-call | flops 188743680 | bytes 7000000 | tf_op jit(solution)/shard_map/coarse_project/pallas_call | solution.py:494
  67.7 4.5 %all-to-all-start = ((bf16[8,32,768]{2,1,0:T(8,128)(2,1)}), bf16[8,32,768]{2,1,0:T(8,128)(2,1)S(1)}, u32[]{:S(2)}, u32[]{:S(2)}) async-start(bf16[8,32,768]{2,1,0:T(8,128)(2,1)} %get-tuple-element.57), calls=%async_computation.1 | async-start | bytes 786432 | tf_op jit(solution)/shard_map/all_to_all | solution.py:678
  72.2 3.2 %collective-permute-start.7 = (bf16[32,384]{1,0:T(8,128)(2,1)S(1)}, bf16[32,384]{1,0:T(8,128)(2,1)S(1)}, u32[]{:S(2)}, u32[]{:S(2)}) collective-permute-start(bf16[32,384]{1,0:T(8,128)(2,1)S(1)} %get-tuple-element.59.q0), channel_id=1, source_target_pairs={{0,48},{16,0},{32,16},{48,32},{1,49},{17,1},{33,17},{49,33},{2,50}... | collective-permute-start | bytes 73736 | tf_op jit(solution)/shard_map/ppermute | solution.py:644
  75.4 1.7 %collective-permute-start.6 = (bf16[32,384]{1,0:T(8,128)(2,1)S(1)}, bf16[32,384]{1,0:T(8,128)(2,1)S(1)}, u32[]{:S(2)}, u32[]{:S(2)}) collective-permute-start(bf16[32,384]{1,0:T(8,128)(2,1)S(1)} %get-tuple-element.59.q0), channel_id=1, source_target_pairs={{0,32},{16,48},{32,0},{48,16},{1,33},{17,49},{33,1},{49,17},{2,34}... | collective-permute-start | bytes 73736 | tf_op jit(solution)/shard_map/ppermute | solution.py:644
  77.1 2.9 %collective-permute-start.5 = (bf16[32,384]{1,0:T(8,128)(2,1)S(1)}, bf16[32,384]{1,0:T(8,128)(2,1)S(1)}, u32[]{:S(2)}, u32[]{:S(2)}) collective-permute-start(bf16[32,384]{1,0:T(8,128)(2,1)S(1)} %get-tuple-element.59.q0), channel_id=1, source_target_pairs={{0,16},{16,32},{32,48},{48,0},{1,17},{17,33},{33,49},{49,1},{2,18}... | collective-permute-start | bytes 73736 | tf_op jit(solution)/shard_map/ppermute | solution.py:644
  80.0 3.5 %collective-permute-done.6.q2 = bf16[32,384]{1,0:T(8,128)(2,1)S(1)} collective-permute-done((bf16[32,384]{1,0:T(8,128)(2,1)S(1)}, bf16[32,384]{1,0:T(8,128)(2,1)S(1)}, u32[]{:S(2)}, u32[]{:S(2)}) %collective-permute-start.6) | collective-permute-done | bytes 24608 | tf_op jit(solution)/shard_map/ppermute | solution.py:644
  83.6 1.7 %collective-permute-done.8.other_ref = bf16[256,768]{1,0:T(8,128)(2,1)S(1)} collective-permute-done((bf16[256,768]{1,0:T(8,128)(2,1)S(1)}, bf16[256,768]{1,0:T(8,128)(2,1)S(1)}, u32[]{:S(2)}, u32[]{:S(2)}) %collective-permute-start.8) | collective-permute-done | bytes 393248 | tf_op jit(solution)/shard_map/ppermute | solution.py:681
  86.4 1.9 %collective-permute-start.9 = (bf16[32,512]{1,0:T(8,128)(2,1)S(1)}, bf16[32,512]{1,0:T(8,128)(2,1)S(1)}, u32[]{:S(2)}, u32[]{:S(2)}) collective-permute-start(bf16[32,512]{1,0:T(8,128)(2,1)S(1)} %get-tuple-element.65), channel_id=1, source_target_pairs={{0,48},{16,0},{32,16},{48,32},{1,49},{17,1},{33,17},{49,33},{2,50}... | collective-permute-start | bytes 98312 | tf_op jit(solution)/shard_map/ppermute | solution.py:644
  88.3 2.9 %collective-permute-start.10 = (bf16[32,512]{1,0:T(8,128)(2,1)S(1)}, bf16[32,512]{1,0:T(8,128)(2,1)S(1)}, u32[]{:S(2)}, u32[]{:S(2)}) collective-permute-start(bf16[32,512]{1,0:T(8,128)(2,1)S(1)} %get-tuple-element.66), channel_id=1, source_target_pairs={{0,32},{16,48},{32,0},{48,16},{1,33},{17,49},{33,1},{49,17},{2,34}... | collective-permute-start | bytes 98312 | tf_op jit(solution)/shard_map/ppermute | solution.py:644
  91.2 1.9 %collective-permute-start.11 = (bf16[32,512]{1,0:T(8,128)(2,1)S(1)}, bf16[32,512]{1,0:T(8,128)(2,1)S(1)}, u32[]{:S(2)}, u32[]{:S(2)}) collective-permute-start(bf16[32,512]{1,0:T(8,128)(2,1)S(1)} %get-tuple-element.67), channel_id=1, source_target_pairs={{0,16},{16,32},{32,48},{48,0},{1,17},{17,33},{33,49},{49,1},{2,18}... | collective-permute-start | bytes 98312 | tf_op jit(solution)/shard_map/ppermute | solution.py:644
  93.1 3.2 %collective-permute-done.10.p2 = bf16[32,512]{1,0:T(8,128)(2,1)S(1)} collective-permute-done((bf16[32,512]{1,0:T(8,128)(2,1)S(1)}, bf16[32,512]{1,0:T(8,128)(2,1)S(1)}, u32[]{:S(2)}, u32[]{:S(2)}) %collective-permute-start.10) | collective-permute-done | bytes 32800 | tf_op jit(solution)/shard_map/ppermute | solution.py:644
  97.7 2.0 %collective-permute-start.14 = (bf16[32,1536]{1,0:T(8,128)(2,1)S(1)}, bf16[32,1536]{1,0:T(8,128)(2,1)S(1)}, u32[]{:S(2)}, u32[]{:S(2)}) collective-permute-start(bf16[32,1536]{1,0:T(8,128)(2,1)S(1)} %coarse_combine.1.p0), channel_id=1, source_target_pairs={{0,3},{1,0},{2,1},{3,2},{4,7},{5,4},{6,5},{7,6},{8,11},{9,8},{10,9... | collective-permute-start | bytes 294920 | tf_op jit(solution)/shard_map/ppermute | solution.py:644
  101.0 2.2 %collective-permute-done.14.p3 = bf16[32,1536]{1,0:T(8,128)(2,1)S(1)} collective-permute-done((bf16[32,1536]{1,0:T(8,128)(2,1)S(1)}, bf16[32,1536]{1,0:T(8,128)(2,1)S(1)}, u32[]{:S(2)}, u32[]{:S(2)}) %collective-permute-start.14) | collective-permute-done | bytes 98336 | tf_op jit(solution)/shard_map/ppermute | solution.py:644
  103.2 2.7 %collective-permute-done.13.p2 = bf16[32,1536]{1,0:T(8,128)(2,1)S(1)} collective-permute-done((bf16[32,1536]{1,0:T(8,128)(2,1)S(1)}, bf16[32,1536]{1,0:T(8,128)(2,1)S(1)}, u32[]{:S(2)}, u32[]{:S(2)}) %collective-permute-start.13) | collective-permute-done | bytes 98336 | tf_op jit(solution)/shard_map/ppermute | solution.py:644
  106.9 2.7 %split_rows.1 = bf16[4,16,32,192]{3,2,1,0:T(8,128)(2,1)} custom-call(bf16[4,512,192]{2,1,0:T(8,128)(2,1)} %get-tuple-element.37.x_hbm, bf16[2,1536,128]{2,1,0:T(8,128)(2,1)} %bitcast.12, bf16[32,1536]{1,0:T(8,128)(2,1)S(1)} %get-tuple-element.56.coarse_ref, bf16[32,1536]{1,0:T(8,128)(2,1)S(1)} %coarse_combine.1.p0, ...), custom_call_target="tpu_custom_call" | custom-call | flops 18874368 | bytes 4000000 | tf_op jit(solution)/shard_map/split_rows/pallas_call | solution.py:625
  (22 shorter events, 5.9 us)
Async XLA Ops:
  6.5 100.4 %reduce-scatter.2.cloned.1.call-start = ((), (), s32[]{:S(2)}) async-start(), calls=%async_computation.2 | async-start | bytes 3932160 | tf_op jit(solution)/shard_map/reduce_scatter | solution.py:670
  13.3 28.3 %collective-permute-start = (bf16[512,384]{1,0:T(8,128)(2,1)}, bf16[512,384]{1,0:T(8,128)(2,1)S(1)}, u32[]{:S(2)}, u32[]{:S(2)}) collective-permute-start(bf16[512,384]{1,0:T(8,128)(2,1)} %get-tuple-element.43), channel_id=1, source_target_pairs={{0,4},{4,8},{8,12},{12,16},{16,20},{20,24},{24,28},{28,32},{32,36}... | collective-permute-start | bytes 1179656 | tf_op jit(solution)/shard_map/ppermute | solution.py:663
  15.3 26.4 %collective-permute-start.1 = (bf16[512,384]{1,0:T(8,128)(2,1)}, bf16[512,384]{1,0:T(8,128)(2,1)}, u32[]{:S(2)}, u32[]{:S(2)}) collective-permute-start(bf16[512,384]{1,0:T(8,128)(2,1)} %get-tuple-element.44), channel_id=1, source_target_pairs={{4,0},{8,4},{12,8},{16,12},{20,16},{24,20},{28,24},{32,28},{36,32}... | collective-permute-start | bytes 1179656 | tf_op jit(solution)/shard_map/ppermute | solution.py:664
  56.7 5.4 %collective-permute-start.2 = (bf16[32,768]{1,0:T(8,128)(2,1)S(1)}, bf16[32,768]{1,0:T(8,128)(2,1)S(1)}, u32[]{:S(2)}, u32[]{:S(2)}) collective-permute-start(bf16[32,768]{1,0:T(8,128)(2,1)S(1)} %get-tuple-element.50.p0), channel_id=1, source_target_pairs={{0,1},{1,2},{2,3},{3,0},{4,5},{5,6},{6,7},{7,4},{8,9},{9,10},{10,1... | collective-permute-start | bytes 147464 | tf_op jit(solution)/shard_map/ppermute | solution.py:644
  58.6 6.3 %collective-permute-start.4 = (bf16[32,768]{1,0:T(8,128)(2,1)S(1)}, bf16[32,768]{1,0:T(8,128)(2,1)S(1)}, u32[]{:S(2)}, u32[]{:S(2)}) collective-permute-start(bf16[32,768]{1,0:T(8,128)(2,1)S(1)} %get-tuple-element.50.p0), channel_id=1, source_target_pairs={{0,3},{1,0},{2,1},{3,2},{4,7},{5,4},{6,5},{7,6},{8,11},{9,8},{10,9... | collective-permute-start | bytes 147464 | tf_op jit(solution)/shard_map/ppermute | solution.py:644
  60.1 5.6 %collective-permute-start.3 = (bf16[32,768]{1,0:T(8,128)(2,1)S(1)}, bf16[32,768]{1,0:T(8,128)(2,1)S(1)}, u32[]{:S(2)}, u32[]{:S(2)}) collective-permute-start(bf16[32,768]{1,0:T(8,128)(2,1)S(1)} %get-tuple-element.50.p0), channel_id=1, source_target_pairs={{0,2},{1,3},{2,0},{3,1},{4,6},{5,7},{6,4},{7,5},{8,10},{9,11},{10,... | collective-permute-start | bytes 147464 | tf_op jit(solution)/shard_map/ppermute | solution.py:644
  65.7 31.5 %copy-start = (bf16[384,1536]{1,0:T(8,128)(2,1)S(1)}, bf16[384,1536]{1,0:T(8,128)(2,1)}, u32[]{:S(2)}) copy-start(bf16[384,1536]{1,0:T(8,128)(2,1)} %weight_ref.1) | copy-start | bytes 3538948
  67.7 15.9 %all-to-all-start = ((bf16[8,32,768]{2,1,0:T(8,128)(2,1)}), bf16[8,32,768]{2,1,0:T(8,128)(2,1)S(1)}, u32[]{:S(2)}, u32[]{:S(2)}) async-start(bf16[8,32,768]{2,1,0:T(8,128)(2,1)} %get-tuple-element.57), calls=%async_computation.1 | async-start | bytes 786432 | tf_op jit(solution)/shard_map/all_to_all | solution.py:678
  72.2 7.8 %collective-permute-start.7 = (bf16[32,384]{1,0:T(8,128)(2,1)S(1)}, bf16[32,384]{1,0:T(8,128)(2,1)S(1)}, u32[]{:S(2)}, u32[]{:S(2)}) collective-permute-start(bf16[32,384]{1,0:T(8,128)(2,1)S(1)} %get-tuple-element.59.q0), channel_id=1, source_target_pairs={{0,48},{16,0},{32,16},{48,32},{1,49},{17,1},{33,17},{49,33},{2,50}... | collective-permute-start | bytes 73736 | tf_op jit(solution)/shard_map/ppermute | solution.py:644
  75.4 8.1 %collective-permute-start.6 = (bf16[32,384]{1,0:T(8,128)(2,1)S(1)}, bf16[32,384]{1,0:T(8,128)(2,1)S(1)}, u32[]{:S(2)}, u32[]{:S(2)}) collective-permute-start(bf16[32,384]{1,0:T(8,128)(2,1)S(1)} %get-tuple-element.59.q0), channel_id=1, source_target_pairs={{0,32},{16,48},{32,0},{48,16},{1,33},{17,49},{33,1},{49,17},{2,34}... | collective-permute-start | bytes 73736 | tf_op jit(solution)/shard_map/ppermute | solution.py:644
  77.1 6.5 %collective-permute-start.5 = (bf16[32,384]{1,0:T(8,128)(2,1)S(1)}, bf16[32,384]{1,0:T(8,128)(2,1)S(1)}, u32[]{:S(2)}, u32[]{:S(2)}) collective-permute-start(bf16[32,384]{1,0:T(8,128)(2,1)S(1)} %get-tuple-element.59.q0), channel_id=1, source_target_pairs={{0,16},{16,32},{32,48},{48,0},{1,17},{17,33},{33,49},{49,1},{2,18}... | collective-permute-start | bytes 73736 | tf_op jit(solution)/shard_map/ppermute | solution.py:644
  83.6 1.7 %collective-permute-start.8 = (bf16[256,768]{1,0:T(8,128)(2,1)S(1)}, bf16[256,768]{1,0:T(8,128)(2,1)S(1)}, u32[]{:S(2)}, u32[]{:S(2)}) collective-permute-start(bf16[256,768]{1,0:T(8,128)(2,1)S(1)} %bitcast.9), channel_id=1, source_target_pairs={{0,4},{4,0},{1,5},{5,1},{2,6},{6,2},{3,7},{7,3},{8,12},{12,8},{9,1... | collective-permute-start | bytes 1179656 | tf_op jit(solution)/shard_map/ppermute | solution.py:681
  86.4 6.7 %collective-permute-start.9 = (bf16[32,512]{1,0:T(8,128)(2,1)S(1)}, bf16[32,512]{1,0:T(8,128)(2,1)S(1)}, u32[]{:S(2)}, u32[]{:S(2)}) collective-permute-start(bf16[32,512]{1,0:T(8,128)(2,1)S(1)} %get-tuple-element.65), channel_id=1, source_target_pairs={{0,48},{16,0},{32,16},{48,32},{1,49},{17,1},{33,17},{49,33},{2,50}... | collective-permute-start | bytes 98312 | tf_op jit(solution)/shard_map/ppermute | solution.py:644
  88.3 8.0 %collective-permute-start.10 = (bf16[32,512]{1,0:T(8,128)(2,1)S(1)}, bf16[32,512]{1,0:T(8,128)(2,1)S(1)}, u32[]{:S(2)}, u32[]{:S(2)}) collective-permute-start(bf16[32,512]{1,0:T(8,128)(2,1)S(1)} %get-tuple-element.66), channel_id=1, source_target_pairs={{0,32},{16,48},{32,0},{48,16},{1,33},{17,49},{33,1},{49,17},{2,34}... | collective-permute-start | bytes 98312 | tf_op jit(solution)/shard_map/ppermute | solution.py:644
  91.2 6.0 %collective-permute-start.11 = (bf16[32,512]{1,0:T(8,128)(2,1)S(1)}, bf16[32,512]{1,0:T(8,128)(2,1)S(1)}, u32[]{:S(2)}, u32[]{:S(2)}) collective-permute-start(bf16[32,512]{1,0:T(8,128)(2,1)S(1)} %get-tuple-element.67), channel_id=1, source_target_pairs={{0,16},{16,32},{32,48},{48,0},{1,17},{17,33},{33,49},{49,1},{2,18}... | collective-permute-start | bytes 98312 | tf_op jit(solution)/shard_map/ppermute | solution.py:644
  97.7 5.5 %collective-permute-start.14 = (bf16[32,1536]{1,0:T(8,128)(2,1)S(1)}, bf16[32,1536]{1,0:T(8,128)(2,1)S(1)}, u32[]{:S(2)}, u32[]{:S(2)}) collective-permute-start(bf16[32,1536]{1,0:T(8,128)(2,1)S(1)} %coarse_combine.1.p0), channel_id=1, source_target_pairs={{0,3},{1,0},{2,1},{3,2},{4,7},{5,4},{6,5},{7,6},{8,11},{9,8},{10,9... | collective-permute-start | bytes 294920 | tf_op jit(solution)/shard_map/ppermute | solution.py:644
  99.7 6.2 %collective-permute-start.13 = (bf16[32,1536]{1,0:T(8,128)(2,1)S(1)}, bf16[32,1536]{1,0:T(8,128)(2,1)S(1)}, u32[]{:S(2)}, u32[]{:S(2)}) collective-permute-start(bf16[32,1536]{1,0:T(8,128)(2,1)S(1)} %coarse_combine.1.p0), channel_id=1, source_target_pairs={{0,2},{1,3},{2,0},{3,1},{4,6},{5,7},{6,4},{7,5},{8,10},{9,11},{10,... | collective-permute-start | bytes 294920 | tf_op jit(solution)/shard_map/ppermute | solution.py:644
  100.3 6.6 %collective-permute-start.12 = (bf16[32,1536]{1,0:T(8,128)(2,1)S(1)}, bf16[32,1536]{1,0:T(8,128)(2,1)S(1)}, u32[]{:S(2)}, u32[]{:S(2)}) collective-permute-start(bf16[32,1536]{1,0:T(8,128)(2,1)S(1)} %coarse_combine.1.p0), channel_id=1, source_target_pairs={{0,1},{1,2},{2,3},{3,0},{4,5},{5,6},{6,7},{7,4},{8,9},{9,10},{10,1... | collective-permute-start | bytes 294920 | tf_op jit(solution)/shard_map/ppermute | solution.py:644
Sparse Core Ops, SparseCore 0:
  56.8 41.2 reduce-scatter.1

commit v4 on v2

--- a/solution.py
+++ b/solution.py
@@ -90,6 +90,17 @@
             out_copies[-1].start()
         x = x_ref[frame]
         wide = x.astype(f32)
+        added = jnp.sum(wide.reshape(4, 4, COLS, 768), axis=1).reshape(4 * COLS, 768)
+        sum_ref[...] = sum_ref[...] + added if step else added
+        if step == 3:
+            mean_ref[...] = jnp.dot(
+                block_mean_matrix(4),
+                sum_ref[...],
+                preferred_element_type=f32,
+                precision=lax.Precision.HIGHEST,
+            )
+            out_copies.append(pltpu.make_async_copy(mean_ref, mean_hbm, out_sems.at[3]))
+            out_copies[-1].start()
         projected = nt_dot(x, rows_ref[...])
         scale = lax.rsqrt(jnp.mean(wide * wide, axis=-1, keepdims=True) + EPSILON)
         projected = projected * scale
@@ -99,19 +110,9 @@
         ones_ref[frame] = jnp.where(lane < 192, projected[:, :256], 1.0).astype(bf16)
         along = jnp.transpose(jnp.broadcast_to(scale, (TOKENS, 128)))[:1]
         key_ref[frame] = (nt_dot(rows_ref[192:384, :], x) * along).astype(bf16)
-        added = jnp.sum(wide.reshape(4, 4, COLS, 768), axis=1).reshape(4 * COLS, 768)
-        sum_ref[...] = sum_ref[...] + added if step else added
         if step < 2:
             edge_ref[step] = pairs.astype(bf16)
             out_copies[step].start()
-    mean_ref[...] = jnp.dot(
-        block_mean_matrix(4),
-        sum_ref[...],
-        preferred_element_type=f32,
-        precision=lax.Precision.HIGHEST,
-    )
-    out_copies.append(pltpu.make_async_copy(mean_ref, mean_hbm, out_sems.at[3]))
-    out_copies[-1].start()
     for copy in out_copies:
         copy.wait()
 

time: 115 us -> 114 us (level)
  no operation moved by 1% of the time
where the time goes in v4:
time: 114 us; the launch traced here: 113 us
  Pallas kernels  48.9 us (43%)
  starting transfers between devices  32.1 us (28%)
  waiting for transfers between devices  18.5 us (16%)
  between operations  13.5 us (12%)
    pallas_call x1, Pallas kernels, attend_inner(): pl.pallas_call(inner_kernel, in_specs=[vmem] * 3 + [hbm], out_specs=[hbm]...  18.8 us
    ppermute x12, starting transfers between devices, shifted(): return lax.ppermute(value, axis, [(i, (i + shift) % 4) for i in range(4)])  16.9 us
    pallas_call x1, Pallas kernels, attend_outer(): pl.pallas_call(outer_kernel, in_specs=[pl.BlockSpec(memory_space=pltpu.SM...  15 us
    ppermute x12, waiting for transfers between devices, shifted(): return lax.ppermute(value, axis, [(i, (i + shift) % 4) for i in range(4)])  11.1 us
    ppermute x1, starting transfers between devices, body(): lax.ppermute(initial, FRAMES, [(i + 1, i) for i in range(groups - 1)])  7.47 us
    pallas_call x1, Pallas kernels, fine_project(): pl.pallas_call(fine_project_kernel, in_specs=[pl.BlockSpec(memory_space=p...  6.09 us
    all_to_all x1, starting transfers between devices, body(): lax.all_to_all(coarse_kv, 'z', 0, 0, tiled=True).reshape(256, 768)  5.85 us
    all_to_all x1, waiting for transfers between devices, body(): lax.all_to_all(coarse_kv, 'z', 0, 0, tiled=True).reshape(256, 768)  5.73 us
  transfers between devices with their start and end apart: 17, of which 12 were waited for; matrix products, arithmetic and copies ran while one was open for 0% of the time, Pallas kernels for 22%

profile of v4, /device:TPU:6, one launch (start us, length us, event | category | flops | bytes accessed | tf_op | source)
XLA Modules:
  0.0 113.2 jit_solution(6696407693098495031)
XLA Ops:
  6.5 6.1 %fine_project.1 = (bf16[4,512,192]{2,1,0:T(8,128)(2,1)S(1)}, bf16[4,192,512]{2,1,0:T(8,128)(2,1)S(1)}, bf16[4,512,256]{2,1,0:T(8,128)(2,1)S(1)}, bf16[512,384]{1...) custom-call(s32[1]{0:T(128)} %bitcast.place_ref, ...), custom_call_target="tpu_custom_call" | custom-call | flops 2415919104 | bytes 8000000 | tf_op jit(solution)/shard_map/fine_project/pallas_call | solution.py:126
  12.6 1.9 %collective-permute-start = (bf16[512,384]{1,0:T(8,128)(2,1)}, bf16[512,384]{1,0:T(8,128)(2,1)S(1)}, u32[]{:S(2)}, u32[]{:S(2)}) collective-permute-start(bf16[512,384]{1,0:T(8,128)(2,1)} %get-tuple-element.43), channel_id=1, source_target_pairs={{0,4},{4,8},{8,12},{12,16},{16,20},{20,24},{24,28},{28,32},{32,36}... | collective-permute-start | bytes 1179656 | tf_op jit(solution)/shard_map/ppermute | solution.py:664
  14.6 7.5 %collective-permute-start.1 = (bf16[512,384]{1,0:T(8,128)(2,1)}, bf16[512,384]{1,0:T(8,128)(2,1)}, u32[]{:S(2)}, u32[]{:S(2)}) collective-permute-start(bf16[512,384]{1,0:T(8,128)(2,1)} %get-tuple-element.44), channel_id=1, source_target_pairs={{4,0},{8,4},{12,8},{16,12},{20,16},{24,20},{28,24},{32,28},{36,32}... | collective-permute-start | bytes 1179656 | tf_op jit(solution)/shard_map/ppermute | solution.py:665
  22.1 18.8 %attend_inner.1 = (bf16[4,2,1536,128]{3,2,1,0:T(8,128)(2,1)}, bf16[4,128,384]{2,1,0:T(8,128)(2,1)S(1)}, f32[32,256]{1,0:T(8,128)S(1)}, f32[2,512,384]{2,1,0:T(8,...) custom-call(bf16[4,512,192]{2,1,0:T(8,128)(2,1)S(1)} %get-tuple-element.38.q_ref, ...), custom_call_target="tpu_custom_call" | custom-call | flops 2516582400 | bytes 6000000 | tf_op jit(solution)/shard_map/attend_inner/pallas_call | solution.py:403
  41.0 15.0 %attend_outer.1 = (bf16[4,2,1536,128]{3,2,1,0:T(8,128)(2,1)}, bf16[32,768]{1,0:T(8,128)(2,1)S(1)}) custom-call(f32[2]{0:T(128)S(1)} %pad_maximum_fusion.edge_ref, bf16[4,128,384]{2,1,0:T(8,128)(2,1)S(1)} %get-tuple-element.41.mask_ref, bf16[4,512,192]{2,1,0:T(8,128)(2,1)S(1)} %get-tuple-element.38.q_ref, ...), custom_call_target="tpu_custom_call", output_to_operand_aliasing={{0}: (12, {})} | custom-call | flops 503316480 | bytes 6000000 | tf_op jit(solution)/shard_map/attend_outer/pallas_call | solution.py:426
  56.0 1.9 %collective-permute-start.2 = (bf16[32,768]{1,0:T(8,128)(2,1)S(1)}, bf16[32,768]{1,0:T(8,128)(2,1)S(1)}, u32[]{:S(2)}, u32[]{:S(2)}) collective-permute-start(bf16[32,768]{1,0:T(8,128)(2,1)S(1)} %get-tuple-element.50.p0), channel_id=1, source_target_pairs={{0,1},{1,2},{2,3},{3,0},{4,5},{5,6},{6,7},{7,4},{8,9},{9,10},{10,1... | collective-permute-start | bytes 147464 | tf_op jit(solution)/shard_map/ppermute | solution.py:645
  57.9 1.5 %collective-permute-start.4 = (bf16[32,768]{1,0:T(8,128)(2,1)S(1)}, bf16[32,768]{1,0:T(8,128)(2,1)S(1)}, u32[]{:S(2)}, u32[]{:S(2)}) collective-permute-start(bf16[32,768]{1,0:T(8,128)(2,1)S(1)} %get-tuple-element.50.p0), channel_id=1, source_target_pairs={{0,3},{1,0},{2,1},{3,2},{4,7},{5,4},{6,5},{7,6},{8,11},{9,8},{10,9... | collective-permute-start | bytes 147464 | tf_op jit(solution)/shard_map/ppermute | solution.py:645
  59.4 1.8 %collective-permute-start.3 = (bf16[32,768]{1,0:T(8,128)(2,1)S(1)}, bf16[32,768]{1,0:T(8,128)(2,1)S(1)}, u32[]{:S(2)}, u32[]{:S(2)}) collective-permute-start(bf16[32,768]{1,0:T(8,128)(2,1)S(1)} %get-tuple-element.50.p0), channel_id=1, source_target_pairs={{0,2},{1,3},{2,0},{3,1},{4,6},{5,7},{6,4},{7,5},{8,10},{9,11},{10,... | collective-permute-start | bytes 147464 | tf_op jit(solution)/shard_map/ppermute | solution.py:645
  61.4 2.8 %load.1 = (f32[32,768]{1,0:T(8,128)S(1)}, bf16[768,1536]{1,0:T(8,128)(2,1)S(1)}, bf16[3,1536,384]{2,1,0:T(8,128)(2,1)S(1)}, f32[1536]{0:T(1024)S(1)}) custom-call(bf16[32,768]{1,0:T(8,128)(2,1)S(1)} %collective-permute-done.2._.p1, f32[32,768]{1,0:T(8,128)} %get-tuple-element.51.refs_0_, bf16[768,1536]{1,0:T(8,128)(2,1)} %refs_1_.1, ...), custom_call_target="tpu_custom_call" | custom-call | bytes 6000000 | tf_op jit(solution)/shard_map/load/pallas_call | solution.py:463
  65.0 2.0 %coarse_project.1 = (bf16[32,1536]{1,0:T(8,128)(2,1)S(1)}, bf16[32,384]{1,0:T(8,128)(2,1)S(1)}, bf16[8,32,768]{2,1,0:T(8,128)(2,1)}) custom-call(bf16[32,768]{1,0:T(8,128)(2,1)S(1)} %get-tuple-element.50.p0, bf16[32,768]{1,0:T(8,128)(2,1)S(1)} %collective-permute-done.2._.p1, bf16[32,768]{1,0:T(8,128)(2,1)S(1)} %collective-permute-done.3.p2, ...), custom_call_target="tpu_custom_call" | custom-call | flops 188743680 | bytes 7000000 | tf_op jit(solution)/shard_map/coarse_project/pallas_call | solution.py:495
  67.0 5.9 %all-to-all-start = ((bf16[8,32,768]{2,1,0:T(8,128)(2,1)}), bf16[8,32,768]{2,1,0:T(8,128)(2,1)S(1)}, u32[]{:S(2)}, u32[]{:S(2)}) async-start(bf16[8,32,768]{2,1,0:T(8,128)(2,1)} %get-tuple-element.57), calls=%async_computation.1 | async-start | bytes 786432 | tf_op jit(solution)/shard_map/all_to_all | solution.py:679
  73.7 1.1 collective-permute-start.6
  74.8 2.1 %collective-permute-start.5 = (bf16[32,384]{1,0:T(8,128)(2,1)S(1)}, bf16[32,384]{1,0:T(8,128)(2,1)S(1)}, u32[]{:S(2)}, u32[]{:S(2)}) collective-permute-start(bf16[32,384]{1,0:T(8,128)(2,1)S(1)} %get-tuple-element.59.q0), channel_id=1, source_target_pairs={{0,64},{64,128},{128,192},{192,0},{1,65},{65,129},{129,193},{193,1... | collective-permute-start | bytes 73736 | tf_op jit(solution)/shard_map/ppermute | solution.py:645
  77.9 1.1 collective-permute-done.6.q2
  79.0 5.7 %all-to-all-done = bf16[8,32,768]{2,1,0:T(8,128)(2,1)S(1)} async-done(((bf16[8,32,768]{2,1,0:T(8,128)(2,1)}), bf16[8,32,768]{2,1,0:T(8,128)(2,1)S(1)}, u32[]{:S(2)}, u32[]{:S(2)}) %all-to-all-start) | async-done | bytes 393248 | tf_op jit(solution)/shard_map/all_to_all | solution.py:679
  84.7 1.7 %collective-permute-done.8.other_ref = bf16[256,768]{1,0:T(8,128)(2,1)S(1)} collective-permute-done((bf16[256,768]{1,0:T(8,128)(2,1)S(1)}, bf16[256,768]{1,0:T(8,128)(2,1)S(1)}, u32[]{:S(2)}, u32[]{:S(2)}) %collective-permute-start.8) | collective-permute-done | bytes 393248 | tf_op jit(solution)/shard_map/ppermute | solution.py:682
  86.4 1.1 coarse_attend.1
  88.5 1.1 collective-permute-start.10
  89.6 2.1 %collective-permute-start.11 = (bf16[32,512]{1,0:T(8,128)(2,1)S(1)}, bf16[32,512]{1,0:T(8,128)(2,1)S(1)}, u32[]{:S(2)}, u32[]{:S(2)}) collective-permute-start(bf16[32,512]{1,0:T(8,128)(2,1)S(1)} %get-tuple-element.67), channel_id=1, source_target_pairs={{0,64},{64,128},{128,192},{192,0},{1,65},{65,129},{129,193},{193,1... | collective-permute-start | bytes 98312 | tf_op jit(solution)/shard_map/ppermute | solution.py:645
  91.7 1.4 %collective-permute-done.9.p1 = bf16[32,512]{1,0:T(8,128)(2,1)S(1)} collective-permute-done((bf16[32,512]{1,0:T(8,128)(2,1)S(1)}, bf16[32,512]{1,0:T(8,128)(2,1)S(1)}, u32[]{:S(2)}, u32[]{:S(2)}) %collective-permute-start.9) | collective-permute-done | bytes 32800 | tf_op jit(solution)/shard_map/ppermute | solution.py:645
  94.4 2.0 %collective-permute-start.14 = (bf16[32,1536]{1,0:T(8,128)(2,1)S(1)}, bf16[32,1536]{1,0:T(8,128)(2,1)S(1)}, u32[]{:S(2)}, u32[]{:S(2)}) collective-permute-start(bf16[32,1536]{1,0:T(8,128)(2,1)S(1)} %coarse_combine.1.p0), channel_id=1, source_target_pairs={{0,3},{1,0},{2,1},{3,2},{4,7},{5,4},{6,5},{7,6},{8,11},{9,8},{10,9... | collective-permute-start | bytes 294920 | tf_op jit(solution)/shard_map/ppermute | solution.py:645
  97.9 2.0 %collective-permute-done.14.p3 = bf16[32,1536]{1,0:T(8,128)(2,1)S(1)} collective-permute-done((bf16[32,1536]{1,0:T(8,128)(2,1)S(1)}, bf16[32,1536]{1,0:T(8,128)(2,1)S(1)}, u32[]{:S(2)}, u32[]{:S(2)}) %collective-permute-start.14) | collective-permute-done | bytes 98336 | tf_op jit(solution)/shard_map/ppermute | solution.py:645
  99.9 2.7 %collective-permute-done.13.p2 = bf16[32,1536]{1,0:T(8,128)(2,1)S(1)} collective-permute-done((bf16[32,1536]{1,0:T(8,128)(2,1)S(1)}, bf16[32,1536]{1,0:T(8,128)(2,1)S(1)}, u32[]{:S(2)}, u32[]{:S(2)}) %collective-permute-start.13) | collective-permute-done | bytes 98336 | tf_op jit(solution)/shard_map/ppermute | solution.py:645
  103.6 2.7 %split_rows.1 = bf16[4,16,32,192]{3,2,1,0:T(8,128)(2,1)} custom-call(bf16[4,512,192]{2,1,0:T(8,128)(2,1)} %get-tuple-element.37.x_hbm, bf16[2,1536,128]{2,1,0:T(8,128)(2,1)} %bitcast.12, bf16[32,1536]{1,0:T(8,128)(2,1)S(1)} %get-tuple-element.56.coarse_ref, bf16[32,1536]{1,0:T(8,128)(2,1)S(1)} %coarse_combine.1.p0, ...), custom_call_target="tpu_custom_call" | custom-call | flops 18874368 | bytes 4000000 | tf_op jit(solution)/shard_map/split_rows/pallas_call | solution.py:626
  (22 shorter events, 7.5 us)
Async XLA Ops:
  6.5 97.1 %reduce-scatter.2.cloned.1.call-start = ((), (), s32[]{:S(2)}) async-start(), calls=%async_computation.2 | async-start | bytes 3932160 | tf_op jit(solution)/shard_map/reduce_scatter | solution.py:671
  12.6 28.3 %collective-permute-start = (bf16[512,384]{1,0:T(8,128)(2,1)}, bf16[512,384]{1,0:T(8,128)(2,1)S(1)}, u32[]{:S(2)}, u32[]{:S(2)}) collective-permute-start(bf16[512,384]{1,0:T(8,128)(2,1)} %get-tuple-element.43), channel_id=1, source_target_pairs={{0,4},{4,8},{8,12},{12,16},{16,20},{20,24},{24,28},{28,32},{32,36}... | collective-permute-start | bytes 1179656 | tf_op jit(solution)/shard_map/ppermute | solution.py:664
  14.6 26.4 %collective-permute-start.1 = (bf16[512,384]{1,0:T(8,128)(2,1)}, bf16[512,384]{1,0:T(8,128)(2,1)}, u32[]{:S(2)}, u32[]{:S(2)}) collective-permute-start(bf16[512,384]{1,0:T(8,128)(2,1)} %get-tuple-element.44), channel_id=1, source_target_pairs={{4,0},{8,4},{12,8},{16,12},{20,16},{24,20},{28,24},{32,28},{36,32}... | collective-permute-start | bytes 1179656 | tf_op jit(solution)/shard_map/ppermute | solution.py:665
  56.0 5.4 %collective-permute-start.2 = (bf16[32,768]{1,0:T(8,128)(2,1)S(1)}, bf16[32,768]{1,0:T(8,128)(2,1)S(1)}, u32[]{:S(2)}, u32[]{:S(2)}) collective-permute-start(bf16[32,768]{1,0:T(8,128)(2,1)S(1)} %get-tuple-element.50.p0), channel_id=1, source_target_pairs={{0,1},{1,2},{2,3},{3,0},{4,5},{5,6},{6,7},{7,4},{8,9},{9,10},{10,1... | collective-permute-start | bytes 147464 | tf_op jit(solution)/shard_map/ppermute | solution.py:645
  57.9 6.3 %collective-permute-start.4 = (bf16[32,768]{1,0:T(8,128)(2,1)S(1)}, bf16[32,768]{1,0:T(8,128)(2,1)S(1)}, u32[]{:S(2)}, u32[]{:S(2)}) collective-permute-start(bf16[32,768]{1,0:T(8,128)(2,1)S(1)} %get-tuple-element.50.p0), channel_id=1, source_target_pairs={{0,3},{1,0},{2,1},{3,2},{4,7},{5,4},{6,5},{7,6},{8,11},{9,8},{10,9... | collective-permute-start | bytes 147464 | tf_op jit(solution)/shard_map/ppermute | solution.py:645
  59.4 5.6 %collective-permute-start.3 = (bf16[32,768]{1,0:T(8,128)(2,1)S(1)}, bf16[32,768]{1,0:T(8,128)(2,1)S(1)}, u32[]{:S(2)}, u32[]{:S(2)}) collective-permute-start(bf16[32,768]{1,0:T(8,128)(2,1)S(1)} %get-tuple-element.50.p0), channel_id=1, source_target_pairs={{0,2},{1,3},{2,0},{3,1},{4,6},{5,7},{6,4},{7,5},{8,10},{9,11},{10,... | collective-permute-start | bytes 147464 | tf_op jit(solution)/shard_map/ppermute | solution.py:645
  65.0 29.0 %copy-start = (bf16[384,1536]{1,0:T(8,128)(2,1)S(1)}, bf16[384,1536]{1,0:T(8,128)(2,1)}, u32[]{:S(2)}) copy-start(bf16[384,1536]{1,0:T(8,128)(2,1)} %weight_ref.1) | copy-start | bytes 3538948
  67.0 17.7 %all-to-all-start = ((bf16[8,32,768]{2,1,0:T(8,128)(2,1)}), bf16[8,32,768]{2,1,0:T(8,128)(2,1)S(1)}, u32[]{:S(2)}, u32[]{:S(2)}) async-start(bf16[8,32,768]{2,1,0:T(8,128)(2,1)} %get-tuple-element.57), calls=%async_computation.1 | async-start | bytes 786432 | tf_op jit(solution)/shard_map/all_to_all | solution.py:679
  72.8 5.0 %collective-permute-start.7 = (bf16[32,384]{1,0:T(8,128)(2,1)S(1)}, bf16[32,384]{1,0:T(8,128)(2,1)S(1)}, u32[]{:S(2)}, u32[]{:S(2)}) collective-permute-start(bf16[32,384]{1,0:T(8,128)(2,1)S(1)} %get-tuple-element.59.q0), channel_id=1, source_target_pairs={{0,192},{64,0},{128,64},{192,128},{1,193},{65,1},{129,65},{193,129... | collective-permute-start | bytes 73736 | tf_op jit(solution)/shard_map/ppermute | solution.py:645
  73.7 5.3 %collective-permute-start.6 = (bf16[32,384]{1,0:T(8,128)(2,1)S(1)}, bf16[32,384]{1,0:T(8,128)(2,1)S(1)}, u32[]{:S(2)}, u32[]{:S(2)}) collective-permute-start(bf16[32,384]{1,0:T(8,128)(2,1)S(1)} %get-tuple-element.59.q0), channel_id=1, source_target_pairs={{0,128},{64,192},{128,0},{192,64},{1,129},{65,193},{129,1},{193,65... | collective-permute-start | bytes 73736 | tf_op jit(solution)/shard_map/ppermute | solution.py:645
  74.8 4.2 %collective-permute-start.5 = (bf16[32,384]{1,0:T(8,128)(2,1)S(1)}, bf16[32,384]{1,0:T(8,128)(2,1)S(1)}, u32[]{:S(2)}, u32[]{:S(2)}) collective-permute-start(bf16[32,384]{1,0:T(8,128)(2,1)S(1)} %get-tuple-element.59.q0), channel_id=1, source_target_pairs={{0,64},{64,128},{128,192},{192,0},{1,65},{65,129},{129,193},{193,1... | collective-permute-start | bytes 73736 | tf_op jit(solution)/shard_map/ppermute | solution.py:645
  84.7 1.7 %collective-permute-start.8 = (bf16[256,768]{1,0:T(8,128)(2,1)S(1)}, bf16[256,768]{1,0:T(8,128)(2,1)S(1)}, u32[]{:S(2)}, u32[]{:S(2)}) collective-permute-start(bf16[256,768]{1,0:T(8,128)(2,1)S(1)} %bitcast.9), channel_id=1, source_target_pairs={{0,4},{4,0},{1,5},{5,1},{2,6},{6,2},{3,7},{7,3},{8,12},{12,8},{9,1... | collective-permute-start | bytes 1179656 | tf_op jit(solution)/shard_map/ppermute | solution.py:682
  87.6 5.6 %collective-permute-start.9 = (bf16[32,512]{1,0:T(8,128)(2,1)S(1)}, bf16[32,512]{1,0:T(8,128)(2,1)S(1)}, u32[]{:S(2)}, u32[]{:S(2)}) collective-permute-start(bf16[32,512]{1,0:T(8,128)(2,1)S(1)} %get-tuple-element.65), channel_id=1, source_target_pairs={{0,192},{64,0},{128,64},{192,128},{1,193},{65,1},{129,65},{193,129... | collective-permute-start | bytes 98312 | tf_op jit(solution)/shard_map/ppermute | solution.py:645
  88.5 5.4 %collective-permute-start.10 = (bf16[32,512]{1,0:T(8,128)(2,1)S(1)}, bf16[32,512]{1,0:T(8,128)(2,1)S(1)}, u32[]{:S(2)}, u32[]{:S(2)}) collective-permute-start(bf16[32,512]{1,0:T(8,128)(2,1)S(1)} %get-tuple-element.66), channel_id=1, source_target_pairs={{0,128},{64,192},{128,0},{192,64},{1,129},{65,193},{129,1},{193,65... | collective-permute-start | bytes 98312 | tf_op jit(solution)/shard_map/ppermute | solution.py:645
  89.6 4.4 %collective-permute-start.11 = (bf16[32,512]{1,0:T(8,128)(2,1)S(1)}, bf16[32,512]{1,0:T(8,128)(2,1)S(1)}, u32[]{:S(2)}, u32[]{:S(2)}) collective-permute-start(bf16[32,512]{1,0:T(8,128)(2,1)S(1)} %get-tuple-element.67), channel_id=1, source_target_pairs={{0,64},{64,128},{128,192},{192,0},{1,65},{65,129},{129,193},{193,1... | collective-permute-start | bytes 98312 | tf_op jit(solution)/shard_map/ppermute | solution.py:645
  94.4 5.5 %collective-permute-start.14 = (bf16[32,1536]{1,0:T(8,128)(2,1)S(1)}, bf16[32,1536]{1,0:T(8,128)(2,1)S(1)}, u32[]{:S(2)}, u32[]{:S(2)}) collective-permute-start(bf16[32,1536]{1,0:T(8,128)(2,1)S(1)} %coarse_combine.1.p0), channel_id=1, source_target_pairs={{0,3},{1,0},{2,1},{3,2},{4,7},{5,4},{6,5},{7,6},{8,11},{9,8},{10,9... | collective-permute-start | bytes 294920 | tf_op jit(solution)/shard_map/ppermute | solution.py:645
  96.4 6.2 %collective-permute-start.13 = (bf16[32,1536]{1,0:T(8,128)(2,1)S(1)}, bf16[32,1536]{1,0:T(8,128)(2,1)S(1)}, u32[]{:S(2)}, u32[]{:S(2)}) collective-permute-start(bf16[32,1536]{1,0:T(8,128)(2,1)S(1)} %coarse_combine.1.p0), channel_id=1, source_target_pairs={{0,2},{1,3},{2,0},{3,1},{4,6},{5,7},{6,4},{7,5},{8,10},{9,11},{10,... | collective-permute-start | bytes 294920 | tf_op jit(solution)/shard_map/ppermute | solution.py:645
  97.1 6.5 %collective-permute-start.12 = (bf16[32,1536]{1,0:T(8,128)(2,1)S(1)}, bf16[32,1536]{1,0:T(8,128)(2,1)S(1)}, u32[]{:S(2)}, u32[]{:S(2)}) collective-permute-start(bf16[32,1536]{1,0:T(8,128)(2,1)S(1)} %coarse_combine.1.p0), channel_id=1, source_target_pairs={{0,1},{1,2},{2,3},{3,0},{4,5},{5,6},{6,7},{7,4},{8,9},{9,10},{10,1... | collective-permute-start | bytes 294920 | tf_op jit(solution)/shard_map/ppermute | solution.py:645
Sparse Core Ops, SparseCore 0:
  56.1 41.2 reduce-scatter.1

commit v5 on v4

--- a/solution.py
+++ b/solution.py
@@ -448,10 +448,17 @@
 
 def load_kernel(_, *refs):
     sources, targets, sems = refs[:4], refs[4:8], refs[8]
-    copies = [
-        pltpu.make_async_copy(source, target, sems.at[i])
-        for i, (source, target) in enumerate(zip(sources, targets))
-    ]
+    copies = []
+    for source, target in zip(sources, targets):
+        pieces = [(source, target)]
+        if len(source.shape) == 3:
+            halves = [(i, pl.ds(768 * half, 768)) for i in range(3) for half in range(2)]
+            pieces = [(source.at[i, rows], target.at[i, rows]) for i, rows in halves]
+        elif source.shape[0] == 768:
+            quarters = [pl.ds(192 * i, 192) for i in range(4)]
+            pieces = [(source.at[rows], target.at[rows]) for rows in quarters]
+        for here, there in pieces:
+            copies.append(pltpu.make_async_copy(here, there, sems.at[len(copies)]))
     for copy in copies:
         copy.start()
     for copy in copies:
@@ -465,7 +472,7 @@
         in_specs=[anywhere] * 5,
         out_specs=[anywhere] * 4,
         out_shape=[pltpu.VMEM(array.shape, array.dtype) for array in arrays],
-        scratch_shapes=[pltpu.SemaphoreType.DMA((4,))],
+        scratch_shapes=[pltpu.SemaphoreType.DMA((12,))],
         compiler_params=params(4),
         cost_estimate=cost(0, 6e6),
         name="load",
@@ -583,14 +590,18 @@
     x_hbm, rows_hbm, coarse_ref, p0, p1, p2, p3, weight_ref, out_hbm,
     x_ref, rows_ref, out_ref, in_sems, out_sems,
 ):
-    x_copy = pltpu.make_async_copy(x_hbm, x_ref, in_sems.at[2])
-    x_copy.start()
+    x_copies = [
+        pltpu.make_async_copy(x_hbm.at[frame], x_ref.at[frame], in_sems.at[2 + frame])
+        for frame in range(4)
+    ]
     in_copies = [
         pltpu.make_async_copy(rows_hbm.at[pair], rows_ref.at[pair], in_sems.at[pair])
         for pair in (0, 1)
     ]
-    for copy in in_copies:
-        copy.start()
+    for pair, frames in enumerate(((1, 2), (0, 3))):
+        in_copies[pair].start()
+        for frame in frames:
+            x_copies[frame].start()
     mixed = (p0[...].astype(f32) + p1[...].astype(f32)) + (
         p2[...].astype(f32) + p3[...].astype(f32)
     )
@@ -601,11 +612,11 @@
     spread = jnp.where(col == (row >> 5) * 8 + ((row & 31) >> 2), 1.0, 0.0)
     grid = jnp.dot(spread, split, preferred_element_type=f32, precision=lax.Precision.HIGHEST)
     out_copies = []
-    x_copy.wait()
     for pair, frames in enumerate(((1, 2), (0, 3))):
         in_copies[pair].wait()
         third = rows_ref[pair, 2 * TOKENS :, :].astype(f32)
         for at, frame in enumerate(frames):
+            x_copies[frame].wait()
             x = x_ref[frame].astype(f32)
             one = rows_ref[pair, TOKENS * at : TOKENS * (at + 1), :].astype(f32)
             two = pltpu.roll(third, 64, axis=1) if at else third
@@ -632,7 +643,7 @@
             pltpu.VMEM((4, TOKENS, 192), bf16),
             pltpu.VMEM((2, 3 * TOKENS, 128), bf16),
             pltpu.VMEM((4, ROWS, COLS, 192), bf16),
-            pltpu.SemaphoreType.DMA((3,)),
+            pltpu.SemaphoreType.DMA((6,)),
             pltpu.SemaphoreType.DMA((4,)),
         ],
         compiler_params=params(24),

time: 114 us -> 114 us (level)
  no operation moved by 1% of the time
where the time goes in v5:
time: 114 us; the launch traced here: 113 us
  Pallas kernels  48.8 us (43%)
  starting transfers between devices  32.1 us (28%)
  waiting for transfers between devices  18.5 us (16%)
  between operations  13.5 us (12%)
    pallas_call x1, Pallas kernels, attend_inner(): pl.pallas_call(inner_kernel, in_specs=[vmem] * 3 + [hbm], out_specs=[hbm]...  18.8 us
    ppermute x12, starting transfers between devices, shifted(): return lax.ppermute(value, axis, [(i, (i + shift) % 4) for i in range(4)])  16.9 us
    pallas_call x1, Pallas kernels, attend_outer(): pl.pallas_call(outer_kernel, in_specs=[pl.BlockSpec(memory_space=pltpu.SM...  15 us
    ppermute x12, waiting for transfers between devices, shifted(): return lax.ppermute(value, axis, [(i, (i + shift) % 4) for i in range(4)])  11 us
    ppermute x1, starting transfers between devices, body(): lax.ppermute(initial, FRAMES, [(i + 1, i) for i in range(groups - 1)])  7.47 us
    pallas_call x1, Pallas kernels, fine_project(): pl.pallas_call(fine_project_kernel, in_specs=[pl.BlockSpec(memory_space=p...  6.09 us
    all_to_all x1, starting transfers between devices, body(): lax.all_to_all(coarse_kv, 'z', 0, 0, tiled=True).reshape(256, 768)  5.85 us
    all_to_all x1, waiting for transfers between devices, body(): lax.all_to_all(coarse_kv, 'z', 0, 0, tiled=True).reshape(256, 768)  5.73 us
  transfers between devices with their start and end apart: 17, of which 12 were waited for; matrix products, arithmetic and copies ran while one was open for 0% of the time, Pallas kernels for 22%

profile of v5, /device:TPU:6, one launch (start us, length us, event | category | flops | bytes accessed | tf_op | source)
XLA Modules:
  0.0 113.0 jit_solution(883999262764208118)
XLA Ops:
  6.5 6.1 %fine_project.1 = (bf16[4,512,192]{2,1,0:T(8,128)(2,1)S(1)}, bf16[4,192,512]{2,1,0:T(8,128)(2,1)S(1)}, bf16[4,512,256]{2,1,0:T(8,128)(2,1)S(1)}, bf16[512,384]{1...) custom-call(s32[1]{0:T(128)} %bitcast.place_ref, ...), custom_call_target="tpu_custom_call" | custom-call | flops 2415919104 | bytes 8000000 | tf_op jit(solution)/shard_map/fine_project/pallas_call | solution.py:126
  12.6 1.9 %collective-permute-start = (bf16[512,384]{1,0:T(8,128)(2,1)}, bf16[512,384]{1,0:T(8,128)(2,1)S(1)}, u32[]{:S(2)}, u32[]{:S(2)}) collective-permute-start(bf16[512,384]{1,0:T(8,128)(2,1)} %get-tuple-element.43), channel_id=1, source_target_pairs={{0,4},{4,8},{8,12},{12,16},{16,20},{20,24},{24,28},{28,32},{32,36}... | collective-permute-start | bytes 1179656 | tf_op jit(solution)/shard_map/ppermute | solution.py:675
  14.6 7.5 %collective-permute-start.1 = (bf16[512,384]{1,0:T(8,128)(2,1)}, bf16[512,384]{1,0:T(8,128)(2,1)}, u32[]{:S(2)}, u32[]{:S(2)}) collective-permute-start(bf16[512,384]{1,0:T(8,128)(2,1)} %get-tuple-element.44), channel_id=1, source_target_pairs={{4,0},{8,4},{12,8},{16,12},{20,16},{24,20},{28,24},{32,28},{36,32}... | collective-permute-start | bytes 1179656 | tf_op jit(solution)/shard_map/ppermute | solution.py:676
  22.1 18.8 %attend_inner.1 = (bf16[4,2,1536,128]{3,2,1,0:T(8,128)(2,1)}, bf16[4,128,384]{2,1,0:T(8,128)(2,1)S(1)}, f32[32,256]{1,0:T(8,128)S(1)}, f32[2,512,384]{2,1,0:T(8,...) custom-call(bf16[4,512,192]{2,1,0:T(8,128)(2,1)S(1)} %get-tuple-element.38.q_ref, ...), custom_call_target="tpu_custom_call" | custom-call | flops 2516582400 | bytes 6000000 | tf_op jit(solution)/shard_map/attend_inner/pallas_call | solution.py:403
  41.0 15.0 %attend_outer.1 = (bf16[4,2,1536,128]{3,2,1,0:T(8,128)(2,1)}, bf16[32,768]{1,0:T(8,128)(2,1)S(1)}) custom-call(f32[2]{0:T(128)S(1)} %pad_maximum_fusion.edge_ref, bf16[4,128,384]{2,1,0:T(8,128)(2,1)S(1)} %get-tuple-element.41.mask_ref, bf16[4,512,192]{2,1,0:T(8,128)(2,1)S(1)} %get-tuple-element.38.q_ref, ...), custom_call_target="tpu_custom_call", output_to_operand_aliasing={{0}: (12, {})} | custom-call | flops 503316480 | bytes 6000000 | tf_op jit(solution)/shard_map/attend_outer/pallas_call | solution.py:426
  56.0 1.9 %collective-permute-start.2 = (bf16[32,768]{1,0:T(8,128)(2,1)S(1)}, bf16[32,768]{1,0:T(8,128)(2,1)S(1)}, u32[]{:S(2)}, u32[]{:S(2)}) collective-permute-start(bf16[32,768]{1,0:T(8,128)(2,1)S(1)} %get-tuple-element.50.p0), channel_id=1, source_target_pairs={{0,1},{1,2},{2,3},{3,0},{4,5},{5,6},{6,7},{7,4},{8,9},{9,10},{10,1... | collective-permute-start | bytes 147464 | tf_op jit(solution)/shard_map/ppermute | solution.py:656
  57.9 1.5 %collective-permute-start.4 = (bf16[32,768]{1,0:T(8,128)(2,1)S(1)}, bf16[32,768]{1,0:T(8,128)(2,1)S(1)}, u32[]{:S(2)}, u32[]{:S(2)}) collective-permute-start(bf16[32,768]{1,0:T(8,128)(2,1)S(1)} %get-tuple-element.50.p0), channel_id=1, source_target_pairs={{0,3},{1,0},{2,1},{3,2},{4,7},{5,4},{6,5},{7,6},{8,11},{9,8},{10,9... | collective-permute-start | bytes 147464 | tf_op jit(solution)/shard_map/ppermute | solution.py:656
  59.4 1.8 %collective-permute-start.3 = (bf16[32,768]{1,0:T(8,128)(2,1)S(1)}, bf16[32,768]{1,0:T(8,128)(2,1)S(1)}, u32[]{:S(2)}, u32[]{:S(2)}) collective-permute-start(bf16[32,768]{1,0:T(8,128)(2,1)S(1)} %get-tuple-element.50.p0), channel_id=1, source_target_pairs={{0,2},{1,3},{2,0},{3,1},{4,6},{5,7},{6,4},{7,5},{8,10},{9,11},{10,... | collective-permute-start | bytes 147464 | tf_op jit(solution)/shard_map/ppermute | solution.py:656
  61.4 2.8 %load.1 = (f32[32,768]{1,0:T(8,128)S(1)}, bf16[768,1536]{1,0:T(8,128)(2,1)S(1)}, bf16[3,1536,384]{2,1,0:T(8,128)(2,1)S(1)}, f32[1536]{0:T(1024)S(1)}) custom-call(bf16[32,768]{1,0:T(8,128)(2,1)S(1)} %collective-permute-done.2._.p1, f32[32,768]{1,0:T(8,128)} %get-tuple-element.51.refs_0_, bf16[768,1536]{1,0:T(8,128)(2,1)} %refs_1_.1, ...), custom_call_target="tpu_custom_call" | custom-call | bytes 6000000 | tf_op jit(solution)/shard_map/load/pallas_call | solution.py:470
  65.0 2.0 %coarse_project.1 = (bf16[32,1536]{1,0:T(8,128)(2,1)S(1)}, bf16[32,384]{1,0:T(8,128)(2,1)S(1)}, bf16[8,32,768]{2,1,0:T(8,128)(2,1)}) custom-call(bf16[32,768]{1,0:T(8,128)(2,1)S(1)} %get-tuple-element.50.p0, bf16[32,768]{1,0:T(8,128)(2,1)S(1)} %collective-permute-done.2._.p1, bf16[32,768]{1,0:T(8,128)(2,1)S(1)} %collective-permute-done.3.p2, ...), custom_call_target="tpu_custom_call" | custom-call | flops 188743680 | bytes 7000000 | tf_op jit(solution)/shard_map/coarse_project/pallas_call | solution.py:502
  67.0 5.9 %all-to-all-start = ((bf16[8,32,768]{2,1,0:T(8,128)(2,1)}), bf16[8,32,768]{2,1,0:T(8,128)(2,1)S(1)}, u32[]{:S(2)}, u32[]{:S(2)}) async-start(bf16[8,32,768]{2,1,0:T(8,128)(2,1)} %get-tuple-element.57), calls=%async_computation.1 | async-start | bytes 786432 | tf_op jit(solution)/shard_map/all_to_all | solution.py:690
  73.7 1.1 collective-permute-start.6
  74.8 2.1 %collective-permute-start.5 = (bf16[32,384]{1,0:T(8,128)(2,1)S(1)}, bf16[32,384]{1,0:T(8,128)(2,1)S(1)}, u32[]{:S(2)}, u32[]{:S(2)}) collective-permute-start(bf16[32,384]{1,0:T(8,128)(2,1)S(1)} %get-tuple-element.59.q0), channel_id=1, source_target_pairs={{0,64},{64,128},{128,192},{192,0},{1,65},{65,129},{129,193},{193,1... | collective-permute-start | bytes 73736 | tf_op jit(solution)/shard_map/ppermute | solution.py:656
  77.9 1.1 collective-permute-done.6.q2
  79.0 5.7 %all-to-all-done = bf16[8,32,768]{2,1,0:T(8,128)(2,1)S(1)} async-done(((bf16[8,32,768]{2,1,0:T(8,128)(2,1)}), bf16[8,32,768]{2,1,0:T(8,128)(2,1)S(1)}, u32[]{:S(2)}, u32[]{:S(2)}) %all-to-all-start) | async-done | bytes 393248 | tf_op jit(solution)/shard_map/all_to_all | solution.py:690
  84.7 1.7 %collective-permute-done.8.other_ref = bf16[256,768]{1,0:T(8,128)(2,1)S(1)} collective-permute-done((bf16[256,768]{1,0:T(8,128)(2,1)S(1)}, bf16[256,768]{1,0:T(8,128)(2,1)S(1)}, u32[]{:S(2)}, u32[]{:S(2)}) %collective-permute-start.8) | collective-permute-done | bytes 393248 | tf_op jit(solution)/shard_map/ppermute | solution.py:693
  86.4 1.1 coarse_attend.1
  88.5 1.1 collective-permute-start.10
  89.6 2.1 %collective-permute-start.11 = (bf16[32,512]{1,0:T(8,128)(2,1)S(1)}, bf16[32,512]{1,0:T(8,128)(2,1)S(1)}, u32[]{:S(2)}, u32[]{:S(2)}) collective-permute-start(bf16[32,512]{1,0:T(8,128)(2,1)S(1)} %get-tuple-element.67), channel_id=1, source_target_pairs={{0,64},{64,128},{128,192},{192,0},{1,65},{65,129},{129,193},{193,1... | collective-permute-start | bytes 98312 | tf_op jit(solution)/shard_map/ppermute | solution.py:656
  91.7 1.4 %collective-permute-done.9.p1 = bf16[32,512]{1,0:T(8,128)(2,1)S(1)} collective-permute-done((bf16[32,512]{1,0:T(8,128)(2,1)S(1)}, bf16[32,512]{1,0:T(8,128)(2,1)S(1)}, u32[]{:S(2)}, u32[]{:S(2)}) %collective-permute-start.9) | collective-permute-done | bytes 32800 | tf_op jit(solution)/shard_map/ppermute | solution.py:656
  94.4 2.0 %collective-permute-start.14 = (bf16[32,1536]{1,0:T(8,128)(2,1)S(1)}, bf16[32,1536]{1,0:T(8,128)(2,1)S(1)}, u32[]{:S(2)}, u32[]{:S(2)}) collective-permute-start(bf16[32,1536]{1,0:T(8,128)(2,1)S(1)} %coarse_combine.1.p0), channel_id=1, source_target_pairs={{0,3},{1,0},{2,1},{3,2},{4,7},{5,4},{6,5},{7,6},{8,11},{9,8},{10,9... | collective-permute-start | bytes 294920 | tf_op jit(solution)/shard_map/ppermute | solution.py:656
  97.9 2.0 %collective-permute-done.14.p3 = bf16[32,1536]{1,0:T(8,128)(2,1)S(1)} collective-permute-done((bf16[32,1536]{1,0:T(8,128)(2,1)S(1)}, bf16[32,1536]{1,0:T(8,128)(2,1)S(1)}, u32[]{:S(2)}, u32[]{:S(2)}) %collective-permute-start.14) | collective-permute-done | bytes 98336 | tf_op jit(solution)/shard_map/ppermute | solution.py:656
  99.9 2.7 %collective-permute-done.13.p2 = bf16[32,1536]{1,0:T(8,128)(2,1)S(1)} collective-permute-done((bf16[32,1536]{1,0:T(8,128)(2,1)S(1)}, bf16[32,1536]{1,0:T(8,128)(2,1)S(1)}, u32[]{:S(2)}, u32[]{:S(2)}) %collective-permute-start.13) | collective-permute-done | bytes 98336 | tf_op jit(solution)/shard_map/ppermute | solution.py:656
  103.6 2.6 %split_rows.1 = bf16[4,16,32,192]{3,2,1,0:T(8,128)(2,1)} custom-call(bf16[4,512,192]{2,1,0:T(8,128)(2,1)} %get-tuple-element.37.x_hbm, bf16[2,1536,128]{2,1,0:T(8,128)(2,1)} %bitcast.12, bf16[32,1536]{1,0:T(8,128)(2,1)S(1)} %get-tuple-element.56.coarse_ref, bf16[32,1536]{1,0:T(8,128)(2,1)S(1)} %coarse_combine.1.p0, ...), custom_call_target="tpu_custom_call" | custom-call | flops 18874368 | bytes 4000000 | tf_op jit(solution)/shard_map/split_rows/pallas_call | solution.py:637
  (22 shorter events, 7.5 us)
Async XLA Ops:
  6.5 97.1 %reduce-scatter.2.cloned.1.call-start = ((), (), s32[]{:S(2)}) async-start(), calls=%async_computation.2 | async-start | bytes 3932160 | tf_op jit(solution)/shard_map/reduce_scatter | solution.py:682
  12.6 28.3 %collective-permute-start = (bf16[512,384]{1,0:T(8,128)(2,1)}, bf16[512,384]{1,0:T(8,128)(2,1)S(1)}, u32[]{:S(2)}, u32[]{:S(2)}) collective-permute-start(bf16[512,384]{1,0:T(8,128)(2,1)} %get-tuple-element.43), channel_id=1, source_target_pairs={{0,4},{4,8},{8,12},{12,16},{16,20},{20,24},{24,28},{28,32},{32,36}... | collective-permute-start | bytes 1179656 | tf_op jit(solution)/shard_map/ppermute | solution.py:675
  14.6 26.4 %collective-permute-start.1 = (bf16[512,384]{1,0:T(8,128)(2,1)}, bf16[512,384]{1,0:T(8,128)(2,1)}, u32[]{:S(2)}, u32[]{:S(2)}) collective-permute-start(bf16[512,384]{1,0:T(8,128)(2,1)} %get-tuple-element.44), channel_id=1, source_target_pairs={{4,0},{8,4},{12,8},{16,12},{20,16},{24,20},{28,24},{32,28},{36,32}... | collective-permute-start | bytes 1179656 | tf_op jit(solution)/shard_map/ppermute | solution.py:676
  56.0 5.4 %collective-permute-start.2 = (bf16[32,768]{1,0:T(8,128)(2,1)S(1)}, bf16[32,768]{1,0:T(8,128)(2,1)S(1)}, u32[]{:S(2)}, u32[]{:S(2)}) collective-permute-start(bf16[32,768]{1,0:T(8,128)(2,1)S(1)} %get-tuple-element.50.p0), channel_id=1, source_target_pairs={{0,1},{1,2},{2,3},{3,0},{4,5},{5,6},{6,7},{7,4},{8,9},{9,10},{10,1... | collective-permute-start | bytes 147464 | tf_op jit(solution)/shard_map/ppermute | solution.py:656
  57.9 6.4 %collective-permute-start.4 = (bf16[32,768]{1,0:T(8,128)(2,1)S(1)}, bf16[32,768]{1,0:T(8,128)(2,1)S(1)}, u32[]{:S(2)}, u32[]{:S(2)}) collective-permute-start(bf16[32,768]{1,0:T(8,128)(2,1)S(1)} %get-tuple-element.50.p0), channel_id=1, source_target_pairs={{0,3},{1,0},{2,1},{3,2},{4,7},{5,4},{6,5},{7,6},{8,11},{9,8},{10,9... | collective-permute-start | bytes 147464 | tf_op jit(solution)/shard_map/ppermute | solution.py:656
  59.4 5.6 %collective-permute-start.3 = (bf16[32,768]{1,0:T(8,128)(2,1)S(1)}, bf16[32,768]{1,0:T(8,128)(2,1)S(1)}, u32[]{:S(2)}, u32[]{:S(2)}) collective-permute-start(bf16[32,768]{1,0:T(8,128)(2,1)S(1)} %get-tuple-element.50.p0), channel_id=1, source_target_pairs={{0,2},{1,3},{2,0},{3,1},{4,6},{5,7},{6,4},{7,5},{8,10},{9,11},{10,... | collective-permute-start | bytes 147464 | tf_op jit(solution)/shard_map/ppermute | solution.py:656
  65.0 29.0 %copy-start = (bf16[384,1536]{1,0:T(8,128)(2,1)S(1)}, bf16[384,1536]{1,0:T(8,128)(2,1)}, u32[]{:S(2)}) copy-start(bf16[384,1536]{1,0:T(8,128)(2,1)} %weight_ref.1) | copy-start | bytes 3538948
  67.0 17.7 %all-to-all-start = ((bf16[8,32,768]{2,1,0:T(8,128)(2,1)}), bf16[8,32,768]{2,1,0:T(8,128)(2,1)S(1)}, u32[]{:S(2)}, u32[]{:S(2)}) async-start(bf16[8,32,768]{2,1,0:T(8,128)(2,1)} %get-tuple-element.57), calls=%async_computation.1 | async-start | bytes 786432 | tf_op jit(solution)/shard_map/all_to_all | solution.py:690
  72.8 5.0 %collective-permute-start.7 = (bf16[32,384]{1,0:T(8,128)(2,1)S(1)}, bf16[32,384]{1,0:T(8,128)(2,1)S(1)}, u32[]{:S(2)}, u32[]{:S(2)}) collective-permute-start(bf16[32,384]{1,0:T(8,128)(2,1)S(1)} %get-tuple-element.59.q0), channel_id=1, source_target_pairs={{0,192},{64,0},{128,64},{192,128},{1,193},{65,1},{129,65},{193,129... | collective-permute-start | bytes 73736 | tf_op jit(solution)/shard_map/ppermute | solution.py:656
  73.7 5.3 %collective-permute-start.6 = (bf16[32,384]{1,0:T(8,128)(2,1)S(1)}, bf16[32,384]{1,0:T(8,128)(2,1)S(1)}, u32[]{:S(2)}, u32[]{:S(2)}) collective-permute-start(bf16[32,384]{1,0:T(8,128)(2,1)S(1)} %get-tuple-element.59.q0), channel_id=1, source_target_pairs={{0,128},{64,192},{128,0},{192,64},{1,129},{65,193},{129,1},{193,65... | collective-permute-start | bytes 73736 | tf_op jit(solution)/shard_map/ppermute | solution.py:656
  74.8 4.2 %collective-permute-start.5 = (bf16[32,384]{1,0:T(8,128)(2,1)S(1)}, bf16[32,384]{1,0:T(8,128)(2,1)S(1)}, u32[]{:S(2)}, u32[]{:S(2)}) collective-permute-start(bf16[32,384]{1,0:T(8,128)(2,1)S(1)} %get-tuple-element.59.q0), channel_id=1, source_target_pairs={{0,64},{64,128},{128,192},{192,0},{1,65},{65,129},{129,193},{193,1... | collective-permute-start | bytes 73736 | tf_op jit(solution)/shard_map/ppermute | solution.py:656
  84.7 1.7 %collective-permute-start.8 = (bf16[256,768]{1,0:T(8,128)(2,1)S(1)}, bf16[256,768]{1,0:T(8,128)(2,1)S(1)}, u32[]{:S(2)}, u32[]{:S(2)}) collective-permute-start(bf16[256,768]{1,0:T(8,128)(2,1)S(1)} %bitcast.9), channel_id=1, source_target_pairs={{0,4},{4,0},{1,5},{5,1},{2,6},{6,2},{3,7},{7,3},{8,12},{12,8},{9,1... | collective-permute-start | bytes 1179656 | tf_op jit(solution)/shard_map/ppermute | solution.py:693
  87.6 5.6 %collective-permute-start.9 = (bf16[32,512]{1,0:T(8,128)(2,1)S(1)}, bf16[32,512]{1,0:T(8,128)(2,1)S(1)}, u32[]{:S(2)}, u32[]{:S(2)}) collective-permute-start(bf16[32,512]{1,0:T(8,128)(2,1)S(1)} %get-tuple-element.65), channel_id=1, source_target_pairs={{0,192},{64,0},{128,64},{192,128},{1,193},{65,1},{129,65},{193,129... | collective-permute-start | bytes 98312 | tf_op jit(solution)/shard_map/ppermute | solution.py:656
  88.5 5.4 %collective-permute-start.10 = (bf16[32,512]{1,0:T(8,128)(2,1)S(1)}, bf16[32,512]{1,0:T(8,128)(2,1)S(1)}, u32[]{:S(2)}, u32[]{:S(2)}) collective-permute-start(bf16[32,512]{1,0:T(8,128)(2,1)S(1)} %get-tuple-element.66), channel_id=1, source_target_pairs={{0,128},{64,192},{128,0},{192,64},{1,129},{65,193},{129,1},{193,65... | collective-permute-start | bytes 98312 | tf_op jit(solution)/shard_map/ppermute | solution.py:656
  89.6 4.4 %collective-permute-start.11 = (bf16[32,512]{1,0:T(8,128)(2,1)S(1)}, bf16[32,512]{1,0:T(8,128)(2,1)S(1)}, u32[]{:S(2)}, u32[]{:S(2)}) collective-permute-start(bf16[32,512]{1,0:T(8,128)(2,1)S(1)} %get-tuple-element.67), channel_id=1, source_target_pairs={{0,64},{64,128},{128,192},{192,0},{1,65},{65,129},{129,193},{193,1... | collective-permute-start | bytes 98312 | tf_op jit(solution)/shard_map/ppermute | solution.py:656
  94.4 5.5 %collective-permute-start.14 = (bf16[32,1536]{1,0:T(8,128)(2,1)S(1)}, bf16[32,1536]{1,0:T(8,128)(2,1)S(1)}, u32[]{:S(2)}, u32[]{:S(2)}) collective-permute-start(bf16[32,1536]{1,0:T(8,128)(2,1)S(1)} %coarse_combine.1.p0), channel_id=1, source_target_pairs={{0,3},{1,0},{2,1},{3,2},{4,7},{5,4},{6,5},{7,6},{8,11},{9,8},{10,9... | collective-permute-start | bytes 294920 | tf_op jit(solution)/shard_map/ppermute | solution.py:656
  96.4 6.2 %collective-permute-start.13 = (bf16[32,1536]{1,0:T(8,128)(2,1)S(1)}, bf16[32,1536]{1,0:T(8,128)(2,1)S(1)}, u32[]{:S(2)}, u32[]{:S(2)}) collective-permute-start(bf16[32,1536]{1,0:T(8,128)(2,1)S(1)} %coarse_combine.1.p0), channel_id=1, source_target_pairs={{0,2},{1,3},{2,0},{3,1},{4,6},{5,7},{6,4},{7,5},{8,10},{9,11},{10,... | collective-permute-start | bytes 294920 | tf_op jit(solution)/shard_map/ppermute | solution.py:656
  97.1 6.5 %collective-permute-start.12 = (bf16[32,1536]{1,0:T(8,128)(2,1)S(1)}, bf16[32,1536]{1,0:T(8,128)(2,1)S(1)}, u32[]{:S(2)}, u32[]{:S(2)}) collective-permute-start(bf16[32,1536]{1,0:T(8,128)(2,1)S(1)} %coarse_combine.1.p0), channel_id=1, source_target_pairs={{0,1},{1,2},{2,3},{3,0},{4,5},{5,6},{6,7},{7,4},{8,9},{9,10},{10,1... | collective-permute-start | bytes 294920 | tf_op jit(solution)/shard_map/ppermute | solution.py:656
Sparse Core Ops, SparseCore 0:
  56.1 41.2 reduce-scatter.1

commit v6 on v4

--- a/solution.py
+++ b/solution.py
@@ -646,7 +646,8 @@
 
 
 def from_others(value, axis):
-    return [shifted(value, axis, shift) for shift in (1, 2, 3)]
+    second = shifted(value, axis, 2)
+    return [shifted(value, axis, 1), second, shifted(value, axis, 3)]
 
 
 def body(x, fine_gain, fine_qkv, fine_out, merge, coarse_gain, coarse_qkv, coarse_out, split):
@@ -681,7 +682,7 @@
     coarse_kv, queries = lax.optimization_barrier((coarse_kv, queries))
     other_kv = lax.ppermute(coarse_kv, "core", [(0, 1), (1, 0)])
     *parts, split = coarse_attend(queries, coarse_kv, other_kv, jnp.transpose(split, (1, 0)))
-    parts = parts[:1] + [shifted(parts[s], "x", 4 - s) for s in (1, 2, 3)]
+    parts = parts[:1] + [shifted(parts[s], "x", 4 - s) for s in (2, 1, 3)]
     coarse_partial = coarse_combine(parts, coarse_out)
     coarse_partials = [coarse_partial] + from_others(coarse_partial, "mp")
     return split_rows(

time: 114 us -> 115 us (level)
  transfers between devices with their start and end apart: 17 -> 17, of which waited for: 12 -> 11; matrix products, arithmetic and copies ran while one was open for 0% -> 0% of each run, Pallas kernels for 22% -> 22%
where the time goes in v6:
time: 115 us; the launch traced here: 114 us
  Pallas kernels  48.9 us (43%)
  starting transfers between devices  32.8 us (29%)
  waiting for transfers between devices  18.4 us (16%)
  between operations  13.5 us (12%)
    pallas_call x1, Pallas kernels, attend_inner(): pl.pallas_call(inner_kernel, in_specs=[vmem] * 3 + [hbm], out_specs=[hbm]...  18.8 us
    ppermute x12, starting transfers between devices, shifted(): return lax.ppermute(value, axis, [(i, (i + shift) % 4) for i in range(4)])  17.5 us
    pallas_call x1, Pallas kernels, attend_outer(): pl.pallas_call(outer_kernel, in_specs=[pl.BlockSpec(memory_space=pltpu.SM...  15 us
    ppermute x12, waiting for transfers between devices, shifted(): return lax.ppermute(value, axis, [(i, (i + shift) % 4) for i in range(4)])  10.9 us
    ppermute x1, starting transfers between devices, body(): lax.ppermute(initial, FRAMES, [(i + 1, i) for i in range(groups - 1)])  7.47 us
    pallas_call x1, Pallas kernels, fine_project(): pl.pallas_call(fine_project_kernel, in_specs=[pl.BlockSpec(memory_space=p...  6.09 us
    all_to_all x1, starting transfers between devices, body(): lax.all_to_all(coarse_kv, 'z', 0, 0, tiled=True).reshape(256, 768)  5.85 us
    all_to_all x1, waiting for transfers between devices, body(): lax.all_to_all(coarse_kv, 'z', 0, 0, tiled=True).reshape(256, 768)  5.73 us
  transfers between devices with their start and end apart: 17, of which 11 were waited for; matrix products, arithmetic and copies ran while one was open for 0% of the time, Pallas kernels for 22%

profile of v6, /device:TPU:6, one launch (start us, length us, event | category | flops | bytes accessed | tf_op | source)
XLA Modules:
  0.0 113.6 jit_solution(10641755913302511465)
XLA Ops:
  6.5 6.1 %fine_project.1 = (bf16[4,512,192]{2,1,0:T(8,128)(2,1)S(1)}, bf16[4,192,512]{2,1,0:T(8,128)(2,1)S(1)}, bf16[4,512,256]{2,1,0:T(8,128)(2,1)S(1)}, bf16[512,384]{1...) custom-call(s32[1]{0:T(128)} %bitcast.place_ref, ...), custom_call_target="tpu_custom_call" | custom-call | flops 2415919104 | bytes 8000000 | tf_op jit(solution)/shard_map/fine_project/pallas_call | solution.py:126
  12.6 1.9 %collective-permute-start = (bf16[512,384]{1,0:T(8,128)(2,1)}, bf16[512,384]{1,0:T(8,128)(2,1)S(1)}, u32[]{:S(2)}, u32[]{:S(2)}) collective-permute-start(bf16[512,384]{1,0:T(8,128)(2,1)} %get-tuple-element.43), channel_id=1, source_target_pairs={{0,4},{4,8},{8,12},{12,16},{16,20},{20,24},{24,28},{28,32},{32,36}... | collective-permute-start | bytes 1179656 | tf_op jit(solution)/shard_map/ppermute | solution.py:665
  14.6 7.5 %collective-permute-start.1 = (bf16[512,384]{1,0:T(8,128)(2,1)}, bf16[512,384]{1,0:T(8,128)(2,1)}, u32[]{:S(2)}, u32[]{:S(2)}) collective-permute-start(bf16[512,384]{1,0:T(8,128)(2,1)} %get-tuple-element.44), channel_id=1, source_target_pairs={{4,0},{8,4},{12,8},{16,12},{20,16},{24,20},{28,24},{32,28},{36,32}... | collective-permute-start | bytes 1179656 | tf_op jit(solution)/shard_map/ppermute | solution.py:666
  22.1 18.8 %attend_inner.1 = (bf16[4,2,1536,128]{3,2,1,0:T(8,128)(2,1)}, bf16[4,128,384]{2,1,0:T(8,128)(2,1)S(1)}, f32[32,256]{1,0:T(8,128)S(1)}, f32[2,512,384]{2,1,0:T(8,...) custom-call(bf16[4,512,192]{2,1,0:T(8,128)(2,1)S(1)} %get-tuple-element.38.q_ref, ...), custom_call_target="tpu_custom_call" | custom-call | flops 2516582400 | bytes 6000000 | tf_op jit(solution)/shard_map/attend_inner/pallas_call | solution.py:403
  41.0 15.0 %attend_outer.1 = (bf16[4,2,1536,128]{3,2,1,0:T(8,128)(2,1)}, bf16[32,768]{1,0:T(8,128)(2,1)S(1)}) custom-call(f32[2]{0:T(128)S(1)} %pad_maximum_fusion.edge_ref, bf16[4,128,384]{2,1,0:T(8,128)(2,1)S(1)} %get-tuple-element.41.mask_ref, bf16[4,512,192]{2,1,0:T(8,128)(2,1)S(1)} %get-tuple-element.38.q_ref, ...), custom_call_target="tpu_custom_call", output_to_operand_aliasing={{0}: (12, {})} | custom-call | flops 503316480 | bytes 6000000 | tf_op jit(solution)/shard_map/attend_outer/pallas_call | solution.py:426
  56.0 1.9 %collective-permute-start.2 = (bf16[32,768]{1,0:T(8,128)(2,1)S(1)}, bf16[32,768]{1,0:T(8,128)(2,1)S(1)}, u32[]{:S(2)}, u32[]{:S(2)}) collective-permute-start(bf16[32,768]{1,0:T(8,128)(2,1)S(1)} %get-tuple-element.50.p0), channel_id=1, source_target_pairs={{0,1},{1,2},{2,3},{3,0},{4,5},{5,6},{6,7},{7,4},{8,9},{9,10},{10,1... | collective-permute-start | bytes 147464 | tf_op jit(solution)/shard_map/ppermute | solution.py:645
  57.9 1.5 %collective-permute-start.4 = (bf16[32,768]{1,0:T(8,128)(2,1)S(1)}, bf16[32,768]{1,0:T(8,128)(2,1)S(1)}, u32[]{:S(2)}, u32[]{:S(2)}) collective-permute-start(bf16[32,768]{1,0:T(8,128)(2,1)S(1)} %get-tuple-element.50.p0), channel_id=1, source_target_pairs={{0,3},{1,0},{2,1},{3,2},{4,7},{5,4},{6,5},{7,6},{8,11},{9,8},{10,9... | collective-permute-start | bytes 147464 | tf_op jit(solution)/shard_map/ppermute | solution.py:645
  59.4 1.8 %collective-permute-start.3 = (bf16[32,768]{1,0:T(8,128)(2,1)S(1)}, bf16[32,768]{1,0:T(8,128)(2,1)S(1)}, u32[]{:S(2)}, u32[]{:S(2)}) collective-permute-start(bf16[32,768]{1,0:T(8,128)(2,1)S(1)} %get-tuple-element.50.p0), channel_id=1, source_target_pairs={{0,2},{1,3},{2,0},{3,1},{4,6},{5,7},{6,4},{7,5},{8,10},{9,11},{10,... | collective-permute-start | bytes 147464 | tf_op jit(solution)/shard_map/ppermute | solution.py:645
  61.4 2.8 %load.1 = (f32[32,768]{1,0:T(8,128)S(1)}, bf16[768,1536]{1,0:T(8,128)(2,1)S(1)}, bf16[3,1536,384]{2,1,0:T(8,128)(2,1)S(1)}, f32[1536]{0:T(1024)S(1)}) custom-call(bf16[32,768]{1,0:T(8,128)(2,1)S(1)} %collective-permute-done.2._.p1, f32[32,768]{1,0:T(8,128)} %get-tuple-element.51.refs_0_, bf16[768,1536]{1,0:T(8,128)(2,1)} %refs_1_.1, ...), custom_call_target="tpu_custom_call" | custom-call | bytes 6000000 | tf_op jit(solution)/shard_map/load/pallas_call | solution.py:463
  65.0 2.0 %coarse_project.1 = (bf16[32,1536]{1,0:T(8,128)(2,1)S(1)}, bf16[32,384]{1,0:T(8,128)(2,1)S(1)}, bf16[8,32,768]{2,1,0:T(8,128)(2,1)}) custom-call(bf16[32,768]{1,0:T(8,128)(2,1)S(1)} %get-tuple-element.50.p0, bf16[32,768]{1,0:T(8,128)(2,1)S(1)} %collective-permute-done.2._.p1, bf16[32,768]{1,0:T(8,128)(2,1)S(1)} %collective-permute-done.3.p2, ...), custom_call_target="tpu_custom_call" | custom-call | flops 188743680 | bytes 7000000 | tf_op jit(solution)/shard_map/coarse_project/pallas_call | solution.py:495
  67.0 5.9 %all-to-all-start = ((bf16[8,32,768]{2,1,0:T(8,128)(2,1)}), bf16[8,32,768]{2,1,0:T(8,128)(2,1)S(1)}, u32[]{:S(2)}, u32[]{:S(2)}) async-start(bf16[8,32,768]{2,1,0:T(8,128)(2,1)} %get-tuple-element.57), calls=%async_computation.1 | async-start | bytes 786432 | tf_op jit(solution)/shard_map/all_to_all | solution.py:680
  73.7 1.1 collective-permute-start.6
  74.8 2.1 %collective-permute-start.5 = (bf16[32,384]{1,0:T(8,128)(2,1)S(1)}, bf16[32,384]{1,0:T(8,128)(2,1)S(1)}, u32[]{:S(2)}, u32[]{:S(2)}) collective-permute-start(bf16[32,384]{1,0:T(8,128)(2,1)S(1)} %get-tuple-element.59.q0), channel_id=1, source_target_pairs={{0,64},{64,128},{128,192},{192,0},{1,65},{65,129},{129,193},{193,1... | collective-permute-start | bytes 73736 | tf_op jit(solution)/shard_map/ppermute | solution.py:645
  77.9 1.1 collective-permute-done.6.q2
  79.0 5.7 %all-to-all-done = bf16[8,32,768]{2,1,0:T(8,128)(2,1)S(1)} async-done(((bf16[8,32,768]{2,1,0:T(8,128)(2,1)}), bf16[8,32,768]{2,1,0:T(8,128)(2,1)S(1)}, u32[]{:S(2)}, u32[]{:S(2)}) %all-to-all-start) | async-done | bytes 393248 | tf_op jit(solution)/shard_map/all_to_all | solution.py:680
  84.7 1.7 %collective-permute-done.8.other_ref = bf16[256,768]{1,0:T(8,128)(2,1)S(1)} collective-permute-done((bf16[256,768]{1,0:T(8,128)(2,1)S(1)}, bf16[256,768]{1,0:T(8,128)(2,1)S(1)}, u32[]{:S(2)}, u32[]{:S(2)}) %collective-permute-start.8) | collective-permute-done | bytes 393248 | tf_op jit(solution)/shard_map/ppermute | solution.py:683
  86.4 1.1 coarse_attend.1
  87.6 1.5 %collective-permute-start.9 = (bf16[32,512]{1,0:T(8,128)(2,1)S(1)}, bf16[32,512]{1,0:T(8,128)(2,1)S(1)}, u32[]{:S(2)}, u32[]{:S(2)}) collective-permute-start(bf16[32,512]{1,0:T(8,128)(2,1)S(1)} %get-tuple-element.65), channel_id=1, source_target_pairs={{0,128},{64,192},{128,0},{192,64},{1,129},{65,193},{129,1},{193,65... | collective-permute-start | bytes 98312 | tf_op jit(solution)/shard_map/ppermute | solution.py:645
  89.1 3.2 %collective-permute-start.11 = (bf16[32,512]{1,0:T(8,128)(2,1)S(1)}, bf16[32,512]{1,0:T(8,128)(2,1)S(1)}, u32[]{:S(2)}, u32[]{:S(2)}) collective-permute-start(bf16[32,512]{1,0:T(8,128)(2,1)S(1)} %get-tuple-element.67), channel_id=1, source_target_pairs={{0,64},{64,128},{128,192},{192,0},{1,65},{65,129},{129,193},{193,1... | collective-permute-start | bytes 98312 | tf_op jit(solution)/shard_map/ppermute | solution.py:645
  93.1 1.1 collective-permute-done.10.p2
  94.7 2.0 %collective-permute-start.14 = (bf16[32,1536]{1,0:T(8,128)(2,1)S(1)}, bf16[32,1536]{1,0:T(8,128)(2,1)S(1)}, u32[]{:S(2)}, u32[]{:S(2)}) collective-permute-start(bf16[32,1536]{1,0:T(8,128)(2,1)S(1)} %coarse_combine.1.p0), channel_id=1, source_target_pairs={{0,3},{1,0},{2,1},{3,2},{4,7},{5,4},{6,5},{7,6},{8,11},{9,8},{10,9... | collective-permute-start | bytes 294920 | tf_op jit(solution)/shard_map/ppermute | solution.py:645
  98.1 2.4 %collective-permute-done.14.p3 = bf16[32,1536]{1,0:T(8,128)(2,1)S(1)} collective-permute-done((bf16[32,1536]{1,0:T(8,128)(2,1)S(1)}, bf16[32,1536]{1,0:T(8,128)(2,1)S(1)}, u32[]{:S(2)}, u32[]{:S(2)}) %collective-permute-start.14) | collective-permute-done | bytes 98336 | tf_op jit(solution)/shard_map/ppermute | solution.py:645
  100.5 2.7 %collective-permute-done.13.p2 = bf16[32,1536]{1,0:T(8,128)(2,1)S(1)} collective-permute-done((bf16[32,1536]{1,0:T(8,128)(2,1)S(1)}, bf16[32,1536]{1,0:T(8,128)(2,1)S(1)}, u32[]{:S(2)}, u32[]{:S(2)}) %collective-permute-start.13) | collective-permute-done | bytes 98336 | tf_op jit(solution)/shard_map/ppermute | solution.py:645
  104.1 2.7 %split_rows.1 = bf16[4,16,32,192]{3,2,1,0:T(8,128)(2,1)} custom-call(bf16[4,512,192]{2,1,0:T(8,128)(2,1)} %get-tuple-element.37.x_hbm, bf16[2,1536,128]{2,1,0:T(8,128)(2,1)} %bitcast.12, bf16[32,1536]{1,0:T(8,128)(2,1)S(1)} %get-tuple-element.56.coarse_ref, bf16[32,1536]{1,0:T(8,128)(2,1)S(1)} %coarse_combine.1.p0, ...), custom_call_target="tpu_custom_call" | custom-call | flops 18874368 | bytes 4000000 | tf_op jit(solution)/shard_map/split_rows/pallas_call | solution.py:626
  (22 shorter events, 6.4 us)
Async XLA Ops:
  6.5 97.5 %reduce-scatter.2.cloned.1.call-start = ((), (), s32[]{:S(2)}) async-start(), calls=%async_computation.2 | async-start | bytes 3932160 | tf_op jit(solution)/shard_map/reduce_scatter | solution.py:672
  12.6 28.3 %collective-permute-start = (bf16[512,384]{1,0:T(8,128)(2,1)}, bf16[512,384]{1,0:T(8,128)(2,1)S(1)}, u32[]{:S(2)}, u32[]{:S(2)}) collective-permute-start(bf16[512,384]{1,0:T(8,128)(2,1)} %get-tuple-element.43), channel_id=1, source_target_pairs={{0,4},{4,8},{8,12},{12,16},{16,20},{20,24},{24,28},{28,32},{32,36}... | collective-permute-start | bytes 1179656 | tf_op jit(solution)/shard_map/ppermute | solution.py:665
  14.6 26.4 %collective-permute-start.1 = (bf16[512,384]{1,0:T(8,128)(2,1)}, bf16[512,384]{1,0:T(8,128)(2,1)}, u32[]{:S(2)}, u32[]{:S(2)}) collective-permute-start(bf16[512,384]{1,0:T(8,128)(2,1)} %get-tuple-element.44), channel_id=1, source_target_pairs={{4,0},{8,4},{12,8},{16,12},{20,16},{24,20},{28,24},{32,28},{36,32}... | collective-permute-start | bytes 1179656 | tf_op jit(solution)/shard_map/ppermute | solution.py:666
  56.0 5.4 %collective-permute-start.2 = (bf16[32,768]{1,0:T(8,128)(2,1)S(1)}, bf16[32,768]{1,0:T(8,128)(2,1)S(1)}, u32[]{:S(2)}, u32[]{:S(2)}) collective-permute-start(bf16[32,768]{1,0:T(8,128)(2,1)S(1)} %get-tuple-element.50.p0), channel_id=1, source_target_pairs={{0,1},{1,2},{2,3},{3,0},{4,5},{5,6},{6,7},{7,4},{8,9},{9,10},{10,1... | collective-permute-start | bytes 147464 | tf_op jit(solution)/shard_map/ppermute | solution.py:645
  57.9 6.3 %collective-permute-start.4 = (bf16[32,768]{1,0:T(8,128)(2,1)S(1)}, bf16[32,768]{1,0:T(8,128)(2,1)S(1)}, u32[]{:S(2)}, u32[]{:S(2)}) collective-permute-start(bf16[32,768]{1,0:T(8,128)(2,1)S(1)} %get-tuple-element.50.p0), channel_id=1, source_target_pairs={{0,3},{1,0},{2,1},{3,2},{4,7},{5,4},{6,5},{7,6},{8,11},{9,8},{10,9... | collective-permute-start | bytes 147464 | tf_op jit(solution)/shard_map/ppermute | solution.py:645
  59.4 5.6 %collective-permute-start.3 = (bf16[32,768]{1,0:T(8,128)(2,1)S(1)}, bf16[32,768]{1,0:T(8,128)(2,1)S(1)}, u32[]{:S(2)}, u32[]{:S(2)}) collective-permute-start(bf16[32,768]{1,0:T(8,128)(2,1)S(1)} %get-tuple-element.50.p0), channel_id=1, source_target_pairs={{0,2},{1,3},{2,0},{3,1},{4,6},{5,7},{6,4},{7,5},{8,10},{9,11},{10,... | collective-permute-start | bytes 147464 | tf_op jit(solution)/shard_map/ppermute | solution.py:645
  65.0 29.2 %copy-start = (bf16[384,1536]{1,0:T(8,128)(2,1)S(1)}, bf16[384,1536]{1,0:T(8,128)(2,1)}, u32[]{:S(2)}) copy-start(bf16[384,1536]{1,0:T(8,128)(2,1)} %weight_ref.1) | copy-start | bytes 3538948
  67.0 17.7 %all-to-all-start = ((bf16[8,32,768]{2,1,0:T(8,128)(2,1)}), bf16[8,32,768]{2,1,0:T(8,128)(2,1)S(1)}, u32[]{:S(2)}, u32[]{:S(2)}) async-start(bf16[8,32,768]{2,1,0:T(8,128)(2,1)} %get-tuple-element.57), calls=%async_computation.1 | async-start | bytes 786432 | tf_op jit(solution)/shard_map/all_to_all | solution.py:680
  72.8 5.0 %collective-permute-start.7 = (bf16[32,384]{1,0:T(8,128)(2,1)S(1)}, bf16[32,384]{1,0:T(8,128)(2,1)S(1)}, u32[]{:S(2)}, u32[]{:S(2)}) collective-permute-start(bf16[32,384]{1,0:T(8,128)(2,1)S(1)} %get-tuple-element.59.q0), channel_id=1, source_target_pairs={{0,192},{64,0},{128,64},{192,128},{1,193},{65,1},{129,65},{193,129... | collective-permute-start | bytes 73736 | tf_op jit(solution)/shard_map/ppermute | solution.py:645
  73.7 5.3 %collective-permute-start.6 = (bf16[32,384]{1,0:T(8,128)(2,1)S(1)}, bf16[32,384]{1,0:T(8,128)(2,1)S(1)}, u32[]{:S(2)}, u32[]{:S(2)}) collective-permute-start(bf16[32,384]{1,0:T(8,128)(2,1)S(1)} %get-tuple-element.59.q0), channel_id=1, source_target_pairs={{0,128},{64,192},{128,0},{192,64},{1,129},{65,193},{129,1},{193,65... | collective-permute-start | bytes 73736 | tf_op jit(solution)/shard_map/ppermute | solution.py:645
  74.8 4.2 %collective-permute-start.5 = (bf16[32,384]{1,0:T(8,128)(2,1)S(1)}, bf16[32,384]{1,0:T(8,128)(2,1)S(1)}, u32[]{:S(2)}, u32[]{:S(2)}) collective-permute-start(bf16[32,384]{1,0:T(8,128)(2,1)S(1)} %get-tuple-element.59.q0), channel_id=1, source_target_pairs={{0,64},{64,128},{128,192},{192,0},{1,65},{65,129},{129,193},{193,1... | collective-permute-start | bytes 73736 | tf_op jit(solution)/shard_map/ppermute | solution.py:645
  84.7 1.7 %collective-permute-start.8 = (bf16[256,768]{1,0:T(8,128)(2,1)S(1)}, bf16[256,768]{1,0:T(8,128)(2,1)S(1)}, u32[]{:S(2)}, u32[]{:S(2)}) collective-permute-start(bf16[256,768]{1,0:T(8,128)(2,1)S(1)} %bitcast.9), channel_id=1, source_target_pairs={{0,4},{4,0},{1,5},{5,1},{2,6},{6,2},{3,7},{7,3},{8,12},{12,8},{9,1... | collective-permute-start | bytes 1179656 | tf_op jit(solution)/shard_map/ppermute | solution.py:683
  87.6 5.5 %collective-permute-start.9 = (bf16[32,512]{1,0:T(8,128)(2,1)S(1)}, bf16[32,512]{1,0:T(8,128)(2,1)S(1)}, u32[]{:S(2)}, u32[]{:S(2)}) collective-permute-start(bf16[32,512]{1,0:T(8,128)(2,1)S(1)} %get-tuple-element.65), channel_id=1, source_target_pairs={{0,128},{64,192},{128,0},{192,64},{1,129},{65,193},{129,1},{193,65... | collective-permute-start | bytes 98312 | tf_op jit(solution)/shard_map/ppermute | solution.py:645
  89.1 5.1 %collective-permute-start.10 = (bf16[32,512]{1,0:T(8,128)(2,1)S(1)}, bf16[32,512]{1,0:T(8,128)(2,1)S(1)}, u32[]{:S(2)}, u32[]{:S(2)}) collective-permute-start(bf16[32,512]{1,0:T(8,128)(2,1)S(1)} %get-tuple-element.66), channel_id=1, source_target_pairs={{0,192},{64,0},{128,64},{192,128},{1,193},{65,1},{129,65},{193,129... | collective-permute-start | bytes 98312 | tf_op jit(solution)/shard_map/ppermute | solution.py:645
  89.1 5.1 %collective-permute-start.11 = (bf16[32,512]{1,0:T(8,128)(2,1)S(1)}, bf16[32,512]{1,0:T(8,128)(2,1)S(1)}, u32[]{:S(2)}, u32[]{:S(2)}) collective-permute-start(bf16[32,512]{1,0:T(8,128)(2,1)S(1)} %get-tuple-element.67), channel_id=1, source_target_pairs={{0,64},{64,128},{128,192},{192,0},{1,65},{65,129},{129,193},{193,1... | collective-permute-start | bytes 98312 | tf_op jit(solution)/shard_map/ppermute | solution.py:645
  94.7 5.8 %collective-permute-start.14 = (bf16[32,1536]{1,0:T(8,128)(2,1)S(1)}, bf16[32,1536]{1,0:T(8,128)(2,1)S(1)}, u32[]{:S(2)}, u32[]{:S(2)}) collective-permute-start(bf16[32,1536]{1,0:T(8,128)(2,1)S(1)} %coarse_combine.1.p0), channel_id=1, source_target_pairs={{0,3},{1,0},{2,1},{3,2},{4,7},{5,4},{6,5},{7,6},{8,11},{9,8},{10,9... | collective-permute-start | bytes 294920 | tf_op jit(solution)/shard_map/ppermute | solution.py:645
  96.7 6.5 %collective-permute-start.13 = (bf16[32,1536]{1,0:T(8,128)(2,1)S(1)}, bf16[32,1536]{1,0:T(8,128)(2,1)S(1)}, u32[]{:S(2)}, u32[]{:S(2)}) collective-permute-start(bf16[32,1536]{1,0:T(8,128)(2,1)S(1)} %coarse_combine.1.p0), channel_id=1, source_target_pairs={{0,2},{1,3},{2,0},{3,1},{4,6},{5,7},{6,4},{7,5},{8,10},{9,11},{10,... | collective-permute-start | bytes 294920 | tf_op jit(solution)/shard_map/ppermute | solution.py:645
  97.3 6.7 %collective-permute-start.12 = (bf16[32,1536]{1,0:T(8,128)(2,1)S(1)}, bf16[32,1536]{1,0:T(8,128)(2,1)S(1)}, u32[]{:S(2)}, u32[]{:S(2)}) collective-permute-start(bf16[32,1536]{1,0:T(8,128)(2,1)S(1)} %coarse_combine.1.p0), channel_id=1, source_target_pairs={{0,1},{1,2},{2,3},{3,0},{4,5},{5,6},{6,7},{7,4},{8,9},{9,10},{10,1... | collective-permute-start | bytes 294920 | tf_op jit(solution)/shard_map/ppermute | solution.py:645
Sparse Core Ops, SparseCore 0:
  56.1 41.2 reduce-scatter.1
